TPU v7x, 768 devices: a whole 4x8x12 slice. The times are simulated.
768 devices in a mesh: dp: 48 (over y, z_lo, core), fsdp: 16 (over z_hi, x).
Axes of the slice: x: 4, y: 8, z: 12 (z_hi: 4, z_lo: 3; z = z_hi * 3 + z_lo), core: 2. Of those that a mesh axis runs over, the one named last changes fastest.
Arguments:
- tokens: bfloat16 [768, 8192], P(None, 'fsdp'), may hold values from -6 to 6
- targets: bfloat16 [768, 8192], P(None, 'fsdp'), may hold values from -6 to 6
- gate_weights: bfloat16 [2, 12288, 8192], P(None, 'dp', 'fsdp'), may hold values from -6 to 6
- up_weights: bfloat16 [2, 12288, 8192], P(None, 'dp', 'fsdp'), may hold values from -6 to 6
- means: float32 [12288, 8192], P('dp', 'fsdp'), may hold values from -6 to 6
- hessian: float32 [12288, 8192], P('dp', 'fsdp'), may hold values from 0.1 to 1
- momentum: float32 [12288, 8192], P('dp', 'fsdp'), may hold values from -4 to 4
- noise: bfloat16 [2, 12288, 8192], P(None, 'dp', 'fsdp'), may hold values from -6 to 6
Outputs:
- new_means: float32 [12288, 8192], P('dp', 'fsdp')
- new_hessian: float32 [12288, 8192], P('dp', 'fsdp')
- new_momentum: float32 [12288, 8192], P('dp', 'fsdp')
All inputs are finite; a program needn't handle non-finite values.
Results may differ from a plain program's by a relative error of at most 0.013.
Values may be sent and summed in bfloat16 or wider, within the bound.
No kernel may reach another device: no remote copies, remote signals or barrier semaphores. Data moves between devices by JAX's collectives and lax.ppermute only.
A program may use at most 32 MiB of HBM per device.

v0:
```python
import math

import jax
import jax.numpy as jnp
from jax import lax
from jax.sharding import PartitionSpec as P

D = 8192


prior_size = 16.0
weight_decay = 0.001
beta_one = 0.9
beta_two = 0.95
step_rate = 0.2
loss_gain = 300.0


def shards(tokens, targets, gate_weights, up_weights, means, hessian, momentum, noise):
    token_count = tokens.shape[0]
    unit_count = means.shape[0]
    hidden_count = unit_count * lax.axis_size("dp")
    scale_in = 1.0 / math.sqrt(D)
    scale_out = 1.0 / math.sqrt(hidden_count)
    error_gain = loss_gain / math.sqrt(token_count)
    rows_share = token_count // lax.axis_size("dp")
    rows_width = token_count // lax.axis_size("fsdp")
    inv_sigma = jnp.sqrt(prior_size * (hessian + weight_decay))
    noise_f = noise.astype(jnp.float32)
    samples = (means[None] + noise_f / inv_sigma[None]).astype(jnp.bfloat16)
    sample_grads = []
    for sample in range(2):
        gate_w = gate_weights[sample]
        up_w = up_weights[sample]

        def both_units(begin_row, row_count, gate_w=gate_w, up_w=up_w):
            gate_term = jnp.dot(tokens, gate_w.T, preferred_element_type=jnp.float32)
            up_term = jnp.dot(tokens, up_w.T, preferred_element_type=jnp.float32)
            return jnp.concatenate([gate_term, up_term], axis=1)

        unit_share = (
            lax.psum_scatter(
                both_units(jnp.int32(0), rows_width * lax.axis_size("fsdp")),
                "fsdp",
                scatter_dimension=0,
                tiled=True,
            )
            * scale_in
        )
        gate_sum = unit_share[:, :unit_count]
        up_sum = unit_share[:, unit_count:]
        sigmoid_gate = jax.nn.sigmoid(gate_sum)
        hidden_share = (gate_sum * sigmoid_gate * up_sum).astype(jnp.bfloat16)
        hidden = lax.all_gather(hidden_share, "fsdp", axis=0, tiled=True)
        weights = samples[sample]

        def project(begin_row, row_count, hidden=hidden, weights=weights):
            return jnp.dot(hidden, weights, preferred_element_type=jnp.float32)

        out_share = (
            lax.psum_scatter(
                project(jnp.int32(0), rows_share * lax.axis_size("dp")),
                "dp",
                scatter_dimension=0,
                tiled=True,
            )
            * scale_out
        )
        first_row = lax.axis_index("dp") * rows_share
        goal_rows = lax.dynamic_slice_in_dim(targets, first_row, rows_share, 0)
        d_share = (error_gain * (out_share - goal_rows.astype(jnp.float32))).astype(jnp.bfloat16)

        def accumulate(running, part_rows, begin_row, hidden=hidden):
            return jnp.dot(hidden.T, part_rows, preferred_element_type=jnp.float32)

        zero_grad = jnp.zeros((hidden.shape[1], tokens.shape[1]), jnp.float32)
        folded = accumulate(
            zero_grad, lax.all_gather(d_share, "dp", axis=0, tiled=True), jnp.int32(0)
        )
        sample_grads.append(folded * scale_out)
    grad_mean = 0.5 * (sample_grads[0] + sample_grads[1])
    curv_mean = 0.5 * (sample_grads[0] * noise_f[0] + sample_grads[1] * noise_f[1]) * inv_sigma
    new_momentum = beta_one * momentum + (1.0 - beta_one) * grad_mean
    spread = hessian - curv_mean
    new_hessian = (
        beta_two * hessian
        + (1.0 - beta_two) * curv_mean
        + 0.5 * (1.0 - beta_two) ** 2 * spread * spread / (hessian + weight_decay)
    )
    new_means = means - step_rate * (new_momentum + weight_decay * means) / (
        new_hessian + weight_decay
    )
    return (new_means, new_hessian, new_momentum)


def solution(mesh):
    in_specs = (
        P(None, "fsdp"),
        P(None, "fsdp"),
        P(None, "dp", "fsdp"),
        P(None, "dp", "fsdp"),
        P("dp", "fsdp"),
        P("dp", "fsdp"),
        P("dp", "fsdp"),
        P(None, "dp", "fsdp"),
    )
    out_specs = (P("dp", "fsdp"), P("dp", "fsdp"), P("dp", "fsdp"))
    return jax.shard_map(shards, mesh=mesh, in_specs=in_specs, out_specs=out_specs, check_vma=False)
```

profile of v0, /device:TPU:197, one launch (start us, length us, event | category | flops | bytes accessed | tf_op | source)
XLA Modules:
  0.0 822.4 jit_solution(4917181251316336737)
XLA Ops:
  7.2 1.1 copy-done
  8.3 1.3 fusion.11
  9.7 0.4 fusion.9
  10.1 0.1 pad_maximum_fusion.1
  10.2 1.6 copy.17
  11.8 0.0 reduce-scatter.13.cloned.1.call-start
  11.9 0.4 fusion.13
  12.3 0.6 copy-done.4
  12.8 0.4 fusion.15
  13.2 0.1 pad_maximum_fusion
  13.4 1.6 copy.15
  15.0 0.0 reduce-scatter.11.cloned.1.call-start
  15.1 1.0 copy-done.5
  16.0 0.2 multiply_sqrt_fusion
  16.2 1.2 add_convert_fusion
  17.4 105.1 %reduce-scatter.15.cloned.1.call-done = f32[48,512]{1,0:T(8,128)} async-done(((f32[768,512]{1,0:T(8,128)}), f32[48,512]{1,0:T(8,128)}) %reduce-scatter.15.cloned.1.call-update) | async-done | bytes 98320 | tf_op jit(solution)/shard_map/reduce_scatter | solution.py:42
  122.5 0.9 broadcast_multiply_fusion
  123.4 36.9 %all_gather.14 = bf16[768,256]{1,0:T(8,128)(2,1)S(1)} all-gather(bf16[48,256]{1,0:T(8,128)(2,1)S(1)} %fusion.21), channel_id=1, replica_groups=mesh['dp'=48,'fsdp'=16] {'fsdp'}, dimensions={0}, use_global_device_ids=true | all-gather | bytes 417792 | tf_op jit(solution)/shard_map/all_gather | solution.py:54
  160.4 1.5 fusion.7
  161.9 0.0 reduce-scatter.9.cloned.1.call-start
  162.0 71.3 %reduce-scatter.13.cloned.1.call-done = f32[48,512]{1,0:T(8,128)} async-done(((f32[768,512]{1,0:T(8,128)}), f32[48,512]{1,0:T(8,128)}) %reduce-scatter.13.cloned.1.call-update) | async-done | bytes 98320 | tf_op jit(solution)/shard_map/reduce_scatter | solution.py:42
  233.3 0.9 broadcast_multiply_fusion.1
  234.2 35.5 %all_gather.12 = bf16[768,256]{1,0:T(8,128)(2,1)S(1)} all-gather(bf16[48,256]{1,0:T(8,128)(2,1)S(1)} %fusion.22), channel_id=1, replica_groups=mesh['dp'=48,'fsdp'=16] {'fsdp'}, dimensions={0}, use_global_device_ids=true | all-gather | bytes 417792 | tf_op jit(solution)/shard_map/all_gather | solution.py:54
  269.7 1.5 fusion.8
  271.3 1.1 convert_element_type.23
  272.4 183.5 %reduce-scatter.11.cloned.1.call-done = f32[16,512]{1,0:T(8,128)} async-done(((f32[768,512]{1,0:T(8,128)}), f32[16,512]{1,0:T(8,128)}) %reduce-scatter.11.cloned.1.call-update) | async-done | bytes 32784 | tf_op jit(solution)/shard_map/reduce_scatter | solution.py:61
  455.9 225.8 %reduce-scatter.9.cloned.1.call-done = f32[16,512]{1,0:T(8,128)} async-done(((f32[768,512]{1,0:T(8,128)}), f32[16,512]{1,0:T(8,128)}) %reduce-scatter.9.cloned.1.call-update) | async-done | bytes 32784 | tf_op jit(solution)/shard_map/reduce_scatter | solution.py:61
  681.8 0.8 fusion.26
  682.6 67.5 %all_gather.15 = bf16[768,512]{1,0:T(8,128)(2,1)S(1)} all-gather(bf16[16,512]{1,0:T(8,128)(2,1)S(1)} %get-tuple-element.6), channel_id=1, replica_groups=mesh['dp'=48,'fsdp'=16] {'dp'}, dimensions={0}, use_global_device_ids=true | all-gather | bytes 802816 | tf_op jit(solution)/shard_map/all_gather | solution.py:78
  750.1 0.4 convolution_multiply_fusion
  750.5 63.4 %all_gather.13 = bf16[768,512]{1,0:T(8,128)(2,1)S(1)} all-gather(bf16[16,512]{1,0:T(8,128)(2,1)S(1)} %get-tuple-element.7), channel_id=1, replica_groups=mesh['dp'=48,'fsdp'=16] {'dp'}, dimensions={0}, use_global_device_ids=true | all-gather | bytes 802816 | tf_op jit(solution)/shard_map/all_gather | solution.py:78
  813.9 2.0 divide_subtract_fusion
  (20 shorter events, 0.2 us)
Async XLA Ops:
  7.2 1.1 copy-start
  7.2 2.5 copy-start.3
  7.2 115.3 %reduce-scatter.15.cloned.1.call-start = ((), (), s32[]{:S(2)}) async-start(), calls=%async_computation.7 | async-start | bytes 1671168 | tf_op jit(solution)/shard_map/reduce_scatter | solution.py:42
  11.8 1.0 copy-start.4
  11.8 221.5 %reduce-scatter.13.cloned.1.call-start = ((), (), s32[]{:S(2)}) async-start(), calls=%async_computation.6 | async-start | bytes 1671168 | tf_op jit(solution)/shard_map/reduce_scatter | solution.py:42
  15.0 1.0 copy-start.5
  15.0 1.2 copy-start.1
  15.0 440.9 %reduce-scatter.11.cloned.1.call-start = ((), (), s32[]{:S(2)}) async-start(), calls=%async_computation.5 | async-start | bytes 1605632 | tf_op jit(solution)/shard_map/reduce_scatter | solution.py:61
  161.9 519.9 %reduce-scatter.9.cloned.1.call-start = ((), (), s32[]{:S(2)}) async-start(), calls=%async_computation.4 | async-start | bytes 1605632 | tf_op jit(solution)/shard_map/reduce_scatter | solution.py:61
  682.6 131.2 %copy-start.2 = (f32[2,256,512]{2,1,0:T(8,128)S(1)}, f32[2,256,512]{2,1,0:T(8,128)}, u32[]{:S(2)}) copy-start(f32[2,256,512]{2,1,0:T(8,128)} %convert_element_type.23) | copy-start | bytes 3145732
  682.6 131.2 %copy-start.6 = (f32[256,512]{1,0:T(8,128)S(1)}, f32[256,512]{1,0:T(8,128)}, u32[]{:S(2)}) copy-start(f32[256,512]{1,0:T(8,128)} %param.12) | copy-start | bytes 1572868
  682.6 131.2 %copy-start.7 = (f32[256,512]{1,0:T(8,128)S(1)}, f32[256,512]{1,0:T(8,128)}, u32[]{:S(2)}) copy-start(f32[256,512]{1,0:T(8,128)} %param.14) | copy-start | bytes 1572868
Sparse Core Ops, SparseCore 0:
  12.7 109.7 reduce-scatter.14
  127.2 106.0 reduce-scatter.12
  236.4 219.4 reduce-scatter.10
  459.2 222.5 reduce-scatter.8
where the time goes:
time: 823 us; the launch traced here: 822 us
  waiting for transfers between devices  586 us (71%)
  blocking collectives  203 us (25%)
  between operations  13.9 us (2%)
    reduce_scatter x2, waiting for transfers between devices, shards(): lax.psum_scatter(project(jnp.int32(0), rows_share * lax.axis_size('dp')),...  409 us
    reduce_scatter x2, waiting for transfers between devices, shards(): lax.psum_scatter(both_units(jnp.int32(0), rows_width * lax.axis_size('fsd...  176 us
    all_gather x2, blocking collectives, shards(): lax.all_gather(d_share, 'dp', axis=0, tiled=True)  131 us
    all_gather x2, blocking collectives, shards(): hidden = lax.all_gather(hidden_share, 'fsdp', axis=0, tiled=True)  72.4 us
  transfers between devices with their start and end apart: 4, of which 4 were waited for; matrix products, arithmetic and copies ran while one was open for 1% of the time, Pallas kernels for 0%

commit v1 on v0

v1 whole, which is shorter than its diff:
```python
import math

import jax
import jax.numpy as jnp
from jax import lax
from jax.sharding import Mesh, PartitionSpec as P

D = 8192


prior_size = 16.0
weight_decay = 0.001
beta_one = 0.9
beta_two = 0.95
step_rate = 0.2
loss_gain = 300.0

bf16 = jnp.bfloat16
f32 = jnp.float32
SWAP = [(0, 1), (1, 0)]


def exchange_sum(parts, axis):
    return jnp.sum(lax.all_to_all(parts, axis, 0, 0, tiled=True).astype(f32), axis=0)


def shards(tokens, targets, gate_weights, up_weights, means, hessian, momentum, noise):
    token_count = tokens.shape[0]
    width = tokens.shape[1]
    unit_count = means.shape[0]
    size_x, size_zh = lax.axis_size("x"), lax.axis_size("zh")
    size_y, size_zl, size_c = lax.axis_size("y"), lax.axis_size("zl"), lax.axis_size("c")
    hidden_count = unit_count * size_y * size_zl * size_c
    scale_in = 1.0 / math.sqrt(D)
    scale_out = 1.0 / math.sqrt(hidden_count)
    error_gain = loss_gain / math.sqrt(token_count)
    both = 2 * unit_count

    inv_sigma = jnp.sqrt(prior_size * (hessian + weight_decay))
    noise_f = noise.astype(f32)
    samples = (means[None] + noise_f / inv_sigma[None]).astype(bf16)

    gate_term = jnp.dot(tokens, gate_weights.reshape(both, width).T, preferred_element_type=f32)
    up_term = jnp.dot(tokens, up_weights.reshape(both, width).T, preferred_element_type=f32)
    terms = jnp.concatenate([gate_term.astype(bf16), up_term.astype(bf16)], axis=1)
    terms = exchange_sum(terms.reshape(size_x, -1, 2 * both), "x").astype(bf16)
    sums = exchange_sum(terms.reshape(size_zh, -1, 2 * both), "zh") * scale_in
    gate_sum, up_sum = sums[:, :both], sums[:, both:]
    hidden_share = (gate_sum * jax.nn.sigmoid(gate_sum) * up_sum).astype(bf16)
    hidden = lax.all_gather(hidden_share, "zh", axis=0, tiled=True)
    hidden = lax.all_gather(hidden, "x", axis=0, tiled=True)

    half = token_count // size_c
    core = lax.axis_index("c")
    hidden_own = lax.dynamic_slice_in_dim(hidden, core * half, half, 0)
    hidden_other = lax.dynamic_slice_in_dim(hidden, (1 - core) * half, half, 0)

    def project(rows):
        return jnp.concatenate(
            [
                jnp.dot(rows[:, s * unit_count : (s + 1) * unit_count], samples[s], preferred_element_type=f32)
                for s in range(2)
            ],
            axis=1,
        )

    arrived = lax.ppermute(project(hidden_other).astype(bf16), "c", SWAP)
    out_half = (project(hidden_own) + arrived.astype(f32)).astype(bf16)
    rows_share = half // (size_y * size_zl)
    out_share = exchange_sum(out_half.reshape(size_y * size_zl, rows_share, 2 * width), ("y", "zl")) * scale_out
    first_row = core * half + (lax.axis_index("y") * size_zl + lax.axis_index("zl")) * rows_share
    goal = lax.dynamic_slice_in_dim(targets, first_row, rows_share, 0).astype(f32)
    goal = jnp.concatenate([goal, goal], axis=1)
    d_share = (error_gain * (out_share - goal)).astype(bf16)
    d_own = lax.all_gather(d_share, ("y", "zl"), axis=0, tiled=True)
    d_other = lax.ppermute(d_own, "c", SWAP)

    sample_grads = []
    for s in range(2):
        units = slice(s * unit_count, (s + 1) * unit_count)
        places = slice(s * width, (s + 1) * width)
        own = jnp.dot(hidden_own[:, units].T, d_own[:, places], preferred_element_type=f32)
        other = jnp.dot(hidden_other[:, units].T, d_other[:, places], preferred_element_type=f32)
        sample_grads.append((own + other) * scale_out)
    grad_mean = 0.5 * (sample_grads[0] + sample_grads[1])
    curv_mean = 0.5 * (sample_grads[0] * noise_f[0] + sample_grads[1] * noise_f[1]) * inv_sigma
    new_momentum = beta_one * momentum + (1.0 - beta_one) * grad_mean
    spread = hessian - curv_mean
    new_hessian = (
        beta_two * hessian
        + (1.0 - beta_two) * curv_mean
        + 0.5 * (1.0 - beta_two) ** 2 * spread * spread / (hessian + weight_decay)
    )
    new_means = means - step_rate * (new_momentum + weight_decay * means) / (
        new_hessian + weight_decay
    )
    return (new_means, new_hessian, new_momentum)


def solution(mesh):
    fine = Mesh(mesh.devices.reshape(8, 3, 2, 4, 4), ("y", "zl", "c", "zh", "x"))
    dp, fsdp = ("y", "zl", "c"), ("zh", "x")
    in_specs = (
        P(None, fsdp),
        P(None, fsdp),
        P(None, dp, fsdp),
        P(None, dp, fsdp),
        P(dp, fsdp),
        P(dp, fsdp),
        P(dp, fsdp),
        P(None, dp, fsdp),
    )
    out_specs = (P(dp, fsdp), P(dp, fsdp), P(dp, fsdp))
    return jax.shard_map(shards, mesh=fine, in_specs=in_specs, out_specs=out_specs, check_vma=False)
```

time: 823 us -> 206 us (0.25)
  the two profiles are of different devices: /device:TPU:197 before, /device:TPU:1 now
where the time goes in v1:
time: 206 us; the launch traced here: 202 us
  blocking collectives  99.3 us (48%)
  starting transfers between devices  55.5 us (27%)
  waiting for transfers between devices  30.6 us (15%)
  other arithmetic  6.3 us (3%)
  matrix products  6.25 us (3%)
  local copies, waits for them, and re-layouts  3.52 us (2%)
    all_gather x1, blocking collectives, shards(): d_own = lax.all_gather(d_share, ('y', 'zl'), axis=0, tiled=True)  52.7 us
    all_to_all x2, starting transfers between devices, exchange_sum(): lax.all_to_all(parts, axis, 0, 0, tiled=True).astype(f32)  30.1 us
    all_to_all x2, waiting for transfers between devices, exchange_sum(): lax.all_to_all(parts, axis, 0, 0, tiled=True).astype(f32)  27.8 us
    all_gather x1, blocking collectives, shards(): hidden = lax.all_gather(hidden_share, 'zh', axis=0, tiled=True)  18.5 us
    all_to_all x1, blocking collectives, exchange_sum(): lax.all_to_all(parts, axis, 0, 0, tiled=True).astype(f32)  17.4 us
    ppermute x1, starting transfers between devices, shards(): arrived = lax.ppermute(project(hidden_other).astype(bf16), 'c', SWAP)  12.8 us
    ppermute x1, starting transfers between devices, shards(): d_other = lax.ppermute(d_own, 'c', SWAP)  12.6 us
    all_gather x1, blocking collectives, shards(): hidden = lax.all_gather(hidden, 'x', axis=0, tiled=True)  10.7 us
  transfers between devices with their start and end apart: 4, of which 4 were waited for; matrix products, arithmetic and copies ran while one was open for 2% of the time, Pallas kernels for 0%

profile of v1, /device:TPU:1, one launch (start us, length us, event | category | flops | bytes accessed | tf_op | source)
XLA Modules:
  0.0 202.3 jit_solution(15908305834065054811)
XLA Ops:
  0.7 1.1 copy-done
  1.8 1.6 convolution_convert_fusion.1
  3.4 0.6 convolution_convert_fusion
  4.2 1.6 copy.12
  5.8 17.4 %all_to_all.15 = bf16[4,192,1024]{2,1,0:T(8,128)(2,1)S(1)} all-to-all(bf16[4,192,1024]{2,1,0:T(8,128)(2,1)} %bitcast.39), channel_id=1, replica_groups=mesh['y'=8,'zl'=3,'c'=2,'zh'=4,'x'=4] {'x'}, dimensions={0} | all-to-all | bytes 3145728 | tf_op jit(solution)/shard_map/all_to_all | solution.py:24
  23.2 1.1 reduce_sum.30
  24.3 21.5 %all-to-all-start.1 = ((bf16[4,48,1024]{2,1,0:T(8,128)(2,1)}), bf16[4,48,1024]{2,1,0:T(8,128)(2,1)S(1)}, u32[]{:S(2)}, u32[]{:S(2)}) async-start(bf16[4,48,1024]{2,1,0:T(8,128)(2,1)} %bitcast.3), calls=%async_computation.1 | async-start | bytes 786432 | tf_op jit(solution)/shard_map/all_to_all | solution.py:24
  45.8 0.2 multiply_sqrt_fusion
  46.0 1.2 add_convert_fusion
  47.2 10.0 %all-to-all-done.1 = bf16[4,48,1024]{2,1,0:T(8,128)(2,1)S(1)} async-done(((bf16[4,48,1024]{2,1,0:T(8,128)(2,1)}), bf16[4,48,1024]{2,1,0:T(8,128)(2,1)S(1)}, u32[]{:S(2)}, u32[]{:S(2)}) %all-to-all-start.1) | async-done | bytes 393248 | tf_op jit(solution)/shard_map/all_to_all | solution.py:24
  57.4 18.5 %all_gather.9 = bf16[192,512]{1,0:T(8,128)(2,1)S(1)} all-gather(bf16[48,512]{1,0:T(8,128)(2,1)S(1)} %fusion.26), channel_id=1, replica_groups=mesh['y'=8,'zl'=3,'c'=2,'zh'=4,'x'=4] {'zh'}, dimensions={0}, use_global_device_ids=true | all-gather | bytes 245760 | tf_op jit(solution)/shard_map/all_gather | solution.py:50
  75.9 10.7 %all_gather.10 = bf16[768,512]{1,0:T(8,128)(2,1)S(1)} all-gather(bf16[192,512]{1,0:T(8,128)(2,1)S(1)} %all_gather.9), channel_id=1, replica_groups=mesh['y'=8,'zl'=3,'c'=2,'zh'=4,'x'=4] {'x'}, dimensions={0}, use_global_device_ids=true | all-gather | bytes 983040 | tf_op jit(solution)/shard_map/all_gather | solution.py:51
  86.6 0.3 convolution_convert_fusion.3
  86.8 0.3 convolution_convert_fusion.2
  87.1 1.0 pad_maximum_fusion.1
  88.1 12.8 %collective-permute-start = (bf16[384,1024]{1,0:T(8,128)(2,1)}, bf16[384,1024]{1,0:T(8,128)(2,1)}, u32[]{:S(2)}, u32[]{:S(2)}) collective-permute-start(bf16[384,1024]{1,0:T(8,128)(2,1)} %pad_maximum_fusion.1), channel_id=1, source_target_pairs={{0,16},{16,0},{1,17},{17,1},{2,18},{18,2},{3,19},{19,3},{4,20},{20... | collective-permute-start | bytes 2359304 | tf_op jit(solution)/shard_map/ppermute | solution.py:67
  101.0 0.3 fusion.16
  101.2 0.2 fusion.17
  101.5 1.7 collective-permute-done
  103.2 2.3 %fusion = bf16[384,1024]{1,0:T(8,128)(2,1)} fusion(f32[384,512]{1,0:T(8,128)S(1)} %fusion.17, f32[384,512]{1,0:T(8,128)S(1)} %fusion.16, bf16[384,1024]{1,0:T(8,128)(2,1)} %collective-permute-done), kind=kLoop, calls=%fused_computation.2 | loop fusion | flops 1572864 | bytes 3145728 | tf_op jit(solution)/shard_map/convert_element_type | solution.py:68
  105.5 8.6 %all-to-all-start.2 = ((bf16[24,16,1024]{2,1,0:T(8,128)(2,1)}), bf16[24,16,1024]{2,1,0:T(8,128)(2,1)S(1)}, u32[]{:S(2)}, u32[]{:S(2)}) async-start(bf16[24,16,1024]{2,1,0:T(8,128)(2,1)} %bitcast.6), calls=%async_computation.2 | async-start | bytes 1572864 | tf_op jit(solution)/shard_map/all_to_all | solution.py:24
  114.1 0.7 constant_dynamic-slice_fusion
  114.8 17.8 %all-to-all-done.2 = bf16[24,16,1024]{2,1,0:T(8,128)(2,1)S(1)} async-done(((bf16[24,16,1024]{2,1,0:T(8,128)(2,1)}), bf16[24,16,1024]{2,1,0:T(8,128)(2,1)S(1)}, u32[]{:S(2)}, u32[]{:S(2)}) %all-to-all-start.2) | async-done | bytes 786464 | tf_op jit(solution)/shard_map/all_to_all | solution.py:24
  132.6 0.1 convert_reduce_fusion
  132.7 52.7 %all_gather.11 = bf16[384,1024]{1,0:T(8,128)(2,1)S(1)} all-gather(bf16[16,1024]{1,0:T(8,128)(2,1)S(1)} %multiply_convert_fusion), channel_id=1, replica_groups=mesh['y'=8,'zl'=3,'c'=2,'zh'=4,'x'=4] {'y','zl'}, dimensions={0}, use_global_device_ids=true | all-gather | bytes 819200 | tf_op jit(solution)/shard_map/all_gather | solution.py:75
  185.5 12.6 %collective-permute-start.1 = (bf16[384,1024]{1,0:T(8,128)(2,1)S(1)}, bf16[384,1024]{1,0:T(8,128)(2,1)S(1)}, u32[]{:S(2)}, u32[]{:S(2)}) collective-permute-start(bf16[384,1024]{1,0:T(8,128)(2,1)S(1)} %all_gather.11), channel_id=1, source_target_pairs={{0,16},{16,0},{1,17},{17,1},{2,18},{18,2},{3,19},{19,3},{4,20},{20... | collective-permute-start | bytes 2359304 | tf_op jit(solution)/shard_map/ppermute | solution.py:76
  198.1 0.1 convert_element_type.38
  198.2 0.3 fusion.11
  198.6 0.3 fusion.14
  198.9 1.1 collective-permute-done.1
  200.0 0.3 fusion.1
  200.3 2.0 divide_subtract_fusion
  (16 shorter events, 0.3 us)
Async XLA Ops:
  0.6 1.1 copy-start
  0.6 2.8 %copy-start.4 = (bf16[2,256,512]{2,1,0:T(8,128)(2,1)S(1)}, bf16[2,256,512]{2,1,0:T(8,128)(2,1)}, u32[]{:S(2)}) copy-start(bf16[2,256,512]{2,1,0:T(8,128)(2,1)} %param.11) | copy-start | bytes 1572868
  23.2 22.6 %copy-start.2 = (f32[256,512]{1,0:T(8,128)S(1)}, f32[256,512]{1,0:T(8,128)}, u32[]{:S(2)}) copy-start(f32[256,512]{1,0:T(8,128)} %param.13) | copy-start | bytes 1572868
  23.2 22.8 %copy-start.1 = (bf16[2,256,512]{2,1,0:T(8,128)(2,1)S(1)}, bf16[2,256,512]{2,1,0:T(8,128)(2,1)}, u32[]{:S(2)}) copy-start(bf16[2,256,512]{2,1,0:T(8,128)(2,1)} %param.15) | copy-start | bytes 1572868
  24.3 32.9 %all-to-all-start.1 = ((bf16[4,48,1024]{2,1,0:T(8,128)(2,1)}), bf16[4,48,1024]{2,1,0:T(8,128)(2,1)S(1)}, u32[]{:S(2)}, u32[]{:S(2)}) async-start(bf16[4,48,1024]{2,1,0:T(8,128)(2,1)} %bitcast.3), calls=%async_computation.1 | async-start | bytes 786432 | tf_op jit(solution)/shard_map/all_to_all | solution.py:24
  88.1 15.1 %collective-permute-start = (bf16[384,1024]{1,0:T(8,128)(2,1)}, bf16[384,1024]{1,0:T(8,128)(2,1)}, u32[]{:S(2)}, u32[]{:S(2)}) collective-permute-start(bf16[384,1024]{1,0:T(8,128)(2,1)} %pad_maximum_fusion.1), channel_id=1, source_target_pairs={{0,16},{16,0},{1,17},{17,1},{2,18},{18,2},{3,19},{19,3},{4,20},{20... | collective-permute-start | bytes 2359304 | tf_op jit(solution)/shard_map/ppermute | solution.py:67
  105.5 27.1 %all-to-all-start.2 = ((bf16[24,16,1024]{2,1,0:T(8,128)(2,1)}), bf16[24,16,1024]{2,1,0:T(8,128)(2,1)S(1)}, u32[]{:S(2)}, u32[]{:S(2)}) async-start(bf16[24,16,1024]{2,1,0:T(8,128)(2,1)} %bitcast.6), calls=%async_computation.2 | async-start | bytes 1572864 | tf_op jit(solution)/shard_map/all_to_all | solution.py:24
  185.5 14.5 %collective-permute-start.1 = (bf16[384,1024]{1,0:T(8,128)(2,1)S(1)}, bf16[384,1024]{1,0:T(8,128)(2,1)S(1)}, u32[]{:S(2)}, u32[]{:S(2)}) collective-permute-start(bf16[384,1024]{1,0:T(8,128)(2,1)S(1)} %all_gather.11), channel_id=1, source_target_pairs={{0,16},{16,0},{1,17},{17,1},{2,18},{18,2},{3,19},{19,3},{4,20},{20... | collective-permute-start | bytes 2359304 | tf_op jit(solution)/shard_map/ppermute | solution.py:76
  198.5 1.8 copy-start.3
  198.5 1.8 copy-start.5

commit v2 on v1

v2 whole, which is shorter than its diff:
```python
import math

import jax
import jax.numpy as jnp
from jax import lax
from jax.experimental import pallas as pl
from jax.experimental.pallas import tpu as pltpu
from jax.sharding import Mesh, PartitionSpec as P

D = 8192


prior_size = 16.0
weight_decay = 0.001
beta_one = 0.9
beta_two = 0.95
step_rate = 0.2
loss_gain = 300.0

bf16 = jnp.bfloat16
f32 = jnp.float32
SWAP = [(0, 1), (1, 0)]
ROWS = 16


def trade(parts, axis):
    return lax.all_to_all(parts, axis, 0, 0, tiled=True)


def terms_kernel(tokens_ref, gate_ref, up_ref, terms_ref):
    rows = tokens_ref[...]
    both = gate_ref.shape[0]
    for place, weights_ref in ((0, gate_ref), (both, up_ref)):
        terms_ref[:, place : place + both] = lax.dot_general(
            rows, weights_ref[...], (((1,), (1,)), ((), ())), preferred_element_type=f32
        ).astype(bf16)


def gate_up_terms(tokens, gate_weights, up_weights, blocks):
    count, width = tokens.shape
    both = gate_weights.shape[0]
    return pl.pallas_call(
        terms_kernel,
        grid=(blocks,),
        in_specs=[
            pl.BlockSpec((count // blocks, width), lambda i: (i, 0)),
            pl.BlockSpec((both, width), lambda i: (0, 0)),
            pl.BlockSpec((both, width), lambda i: (0, 0)),
        ],
        out_specs=pl.BlockSpec((count // blocks, 2 * both), lambda i: (i, 0)),
        out_shape=jax.ShapeDtypeStruct((count, 2 * both), bf16),
        compiler_params=pltpu.CompilerParams(vmem_limit_bytes=16 * 1024 * 1024),
    )(tokens, gate_weights, up_weights)


def shards(tokens, targets, gate_weights, up_weights, means, hessian, momentum, noise):
    token_count = tokens.shape[0]
    width = tokens.shape[1]
    unit_count = means.shape[0]
    size_x, size_zh = lax.axis_size("x"), lax.axis_size("zh")
    size_y, size_zl, size_c = lax.axis_size("y"), lax.axis_size("zl"), lax.axis_size("c")
    hidden_count = unit_count * size_y * size_zl * size_c
    scale_in = 1.0 / math.sqrt(D)
    scale_out = 1.0 / math.sqrt(hidden_count)
    error_gain = loss_gain / math.sqrt(token_count)
    both = 2 * unit_count
    core = lax.axis_index("c")

    inv_sigma = jnp.sqrt(prior_size * (hessian + weight_decay))
    noise_f = noise.astype(f32)
    samples = (means[None] + noise_f / inv_sigma[None]).astype(bf16)
    weights_own = lax.dynamic_index_in_dim(samples, core, 0, False)
    weights_other = lax.ppermute(lax.dynamic_index_in_dim(samples, 1 - core, 0, False), "c", SWAP)

    terms = gate_up_terms(
        tokens, gate_weights.reshape(both, width), up_weights.reshape(both, width), size_x
    )
    terms = trade(terms.reshape(size_x, -1, 2 * both), "x")
    terms = jnp.sum(terms.astype(f32), axis=0).astype(bf16)
    terms = trade(terms.reshape(size_zh, -1, 2 * both), "zh")
    sums = jnp.sum(terms.astype(f32), axis=0) * scale_in
    gate_sum, up_sum = sums[:, :both], sums[:, both:]
    hidden_share = (gate_sum * jax.nn.sigmoid(gate_sum) * up_sum).astype(bf16)
    share = hidden_share.shape[0]
    out_parts = jnp.stack([hidden_share[:, :unit_count], hidden_share[:, unit_count:]])
    out_parts = jnp.broadcast_to(out_parts[:, None], (size_c, size_zh * size_x, share, unit_count))
    hidden = trade(out_parts.reshape(-1, share, unit_count), ("c", "zh", "x"))
    hidden = hidden.reshape(size_c, token_count, unit_count)
    hidden_own = lax.dynamic_index_in_dim(hidden, core, 0, False)
    hidden_other = lax.dynamic_index_in_dim(hidden, 1 - core, 0, False)

    partial = jnp.dot(hidden_own, weights_own, preferred_element_type=f32) + jnp.dot(
        hidden_other, weights_other, preferred_element_type=f32
    )
    chips = size_y * size_zl
    rows_share = token_count // chips
    partial = trade(partial.astype(bf16).reshape(chips, rows_share, width), ("y", "zl"))
    out_share = jnp.sum(partial.astype(f32), axis=0) * scale_out
    chip = lax.axis_index("y") * size_zl + lax.axis_index("zl")
    per_share = share // ROWS
    goal = []
    for piece in range(rows_share // ROWS):
        place = chip * (rows_share // ROWS) + piece
        owner = place // per_share
        first_row = (
            (owner % size_x) * (token_count // size_x)
            + (owner // size_x) * share
            + (place % per_share) * ROWS
        )
        goal.append(lax.dynamic_slice_in_dim(targets, first_row, ROWS, 0))
    goal = jnp.concatenate(goal, axis=0).astype(f32)
    d_share = (error_gain * (out_share - goal)).astype(bf16)
    d_out = trade(jnp.broadcast_to(d_share[None], (chips, rows_share, width)), ("y", "zl"))
    d_out = d_out.reshape(token_count, width)

    def grad(hidden_part):
        return jnp.dot(hidden_part.T, d_out, preferred_element_type=f32) * scale_out

    grad_other = lax.ppermute(grad(hidden_other), "c", SWAP)
    grad_own = grad(hidden_own)
    noise_own = lax.dynamic_index_in_dim(noise, core, 0, False).astype(f32)
    noise_other = lax.dynamic_index_in_dim(noise, 1 - core, 0, False).astype(f32)
    grad_mean = 0.5 * (grad_own + grad_other)
    curv_mean = 0.5 * (grad_own * noise_own + grad_other * noise_other) * inv_sigma
    new_momentum = beta_one * momentum + (1.0 - beta_one) * grad_mean
    spread = hessian - curv_mean
    new_hessian = (
        beta_two * hessian
        + (1.0 - beta_two) * curv_mean
        + 0.5 * (1.0 - beta_two) ** 2 * spread * spread / (hessian + weight_decay)
    )
    new_means = means - step_rate * (new_momentum + weight_decay * means) / (
        new_hessian + weight_decay
    )
    return (new_means, new_hessian, new_momentum)


def solution(mesh):
    fine = Mesh(mesh.devices.reshape(8, 3, 2, 4, 4), ("y", "zl", "c", "zh", "x"))
    dp, fsdp = ("y", "zl", "c"), ("zh", "x")
    in_specs = (
        P(None, fsdp),
        P(None, fsdp),
        P(None, dp, fsdp),
        P(None, dp, fsdp),
        P(dp, fsdp),
        P(dp, fsdp),
        P(dp, fsdp),
        P(None, dp, fsdp),
    )
    out_specs = (P(dp, fsdp), P(dp, fsdp), P(dp, fsdp))
    return jax.shard_map(shards, mesh=fine, in_specs=in_specs, out_specs=out_specs, check_vma=False)
```

time: 206 us -> 173 us (0.84); the launches traced: 202 us -> 173 us
  blocking collectives: 99.3 us -> 76.6 us
  starting transfers between devices: 55.5 us -> 36 us
  waiting for transfers between devices: 30.6 us -> 47.2 us
  other arithmetic: 6.3 us -> 0.91 us
  matrix products: 6.25 us -> 4.06 us
    all_gather x3 -> x0, blocking collectives: 81.9 us -> none  [the longest x1 52.7 us: shards(): d_own = lax.all_gather(d_share, ('y', 'zl'), axis=0, tiled=True)]
    all_to_all x1 -> x3, blocking collectives: 17.4 us -> 76.6 us  [trade(): return lax.all_to_all(parts, axis, 0, 0, tiled=True)]
    all_to_all x2, waiting for transfers between devices: 27.8 us -> 45.7 us  [trade(): return lax.all_to_all(parts, axis, 0, 0, tiled=True)]
    ppermute x2, starting transfers between devices: 25.4 us -> 9.1 us  [the longest x1 6.95 us: shards(): grad_other = lax.ppermute(grad(hidden_other), 'c', SWAP)]
    all_to_all x2, starting transfers between devices: 30.1 us -> 26.9 us  [trade(): return lax.all_to_all(parts, axis, 0, 0, tiled=True)]
    convert_element_type x2 -> x0, other arithmetic: 2.43 us -> none  [the longest x1 2.31 us: shards(): out_half = (project(hidden_own) + arrived.astype(f32)).astype(bf16)]
    dot_general x10 -> x4, matrix products: 6.25 us -> 4.06 us  [the longest x2 2.44 us: grad(): return jnp.dot(hidden_part.T, d_out, preferred_element_type=f32) * scale_out]
    unnamed x12 -> x14, local copies, waits for them, and re-layouts: 1.15 us -> 3.23 us
  transfers between devices with their start and end apart: 4 -> 4, of which waited for: 4 -> 3; matrix products, arithmetic and copies ran while one was open for 2% -> 1% of each run, Pallas kernels for 0% -> 0%
where the time goes in v2:
time: 173 us
  blocking collectives  76.6 us (44%)
  waiting for transfers between devices  47.2 us (27%)
  starting transfers between devices  36 us (21%)
  local copies, waits for them, and re-layouts  5.02 us (3%)
  matrix products  4.06 us (2%)
  Pallas kernels  2.03 us (1%)
    all_to_all x3, blocking collectives, trade(): return lax.all_to_all(parts, axis, 0, 0, tiled=True)  76.6 us
    all_to_all x2, waiting for transfers between devices, trade(): return lax.all_to_all(parts, axis, 0, 0, tiled=True)  45.7 us
    all_to_all x2, starting transfers between devices, trade(): return lax.all_to_all(parts, axis, 0, 0, tiled=True)  26.9 us
    ppermute x1, starting transfers between devices, shards(): grad_other = lax.ppermute(grad(hidden_other), 'c', SWAP)  6.95 us
  transfers between devices with their start and end apart: 4, of which 3 were waited for; matrix products, arithmetic and copies ran while one was open for 1% of the time, Pallas kernels for 0%

profile of v2, /device:TPU:1, one launch (start us, length us, event | category | flops | bytes accessed | tf_op | source)
XLA Modules:
  0.0 172.8 jit_solution(1378193353870335410)
XLA Ops:
  0.6 1.1 copy-done
  1.8 1.0 copy-done.1
  2.8 1.0 copy-done.2
  3.8 2.0 %shard_map.103 = bf16[768,1024]{1,0:T(8,128)(2,1)S(1)} custom-call(bf16[768,512]{1,0:T(8,128)(2,1)S(1)} %copy-done, bf16[512,512]{1,0:T(8,128)(2,1)S(1)} %bitcast.41, bf16[512,512]{1,0:T(8,128)(2,1)S(1)} %bitcast.42), custom_call_target="tpu_custom_call" | custom-call | tf_op jit(solution)/shard_map/pallas_call | solution.py:42
  5.9 17.2 %all_to_all.25 = bf16[4,192,1024]{2,1,0:T(8,128)(2,1)S(1)} all-to-all(bf16[4,192,1024]{2,1,0:T(8,128)(2,1)S(1)} %bitcast.40), channel_id=1, replica_groups=mesh['y'=8,'zl'=3,'c'=2,'zh'=4,'x'=4] {'x'}, dimensions={0} | all-to-all | bytes 3145728 | tf_op jit(solution)/shard_map/all_to_all | solution.py:27
  23.1 0.3 reduce_sum.30
  23.4 32.5 %all_to_all.26 = bf16[4,48,1024]{2,1,0:T(8,128)(2,1)S(1)} all-to-all(bf16[4,48,1024]{2,1,0:T(8,128)(2,1)S(1)} %bitcast.49), channel_id=1, replica_groups=mesh['y'=8,'zl'=3,'c'=2,'zh'=4,'x'=4] {'zh'}, dimensions={0} | all-to-all | bytes 786432 | tf_op jit(solution)/shard_map/all_to_all | solution.py:27
  55.9 0.1 convert_reduce_fusion.1
  56.0 0.0 copy-start.3
  56.1 0.0 copy-start.4
  56.1 0.0 copy-start.5
  56.1 0.9 broadcast_in_dim.4
  57.0 14.3 %all-to-all-start.2 = ((bf16[32,48,256]{2,1,0:T(8,128)(2,1)}), bf16[32,48,256]{2,1,0:T(8,128)(2,1)S(1)}, u32[]{:S(2)}, u32[]{:S(2)}) async-start(bf16[32,48,256]{2,1,0:T(8,128)(2,1)} %bitcast.6), calls=%async_computation.2 | async-start | bytes 1572864 | tf_op jit(solution)/shard_map/all_to_all | solution.py:27
  71.3 0.2 multiply_sqrt_fusion
  71.5 0.2 add_convert_fusion.1
  71.8 2.2 %collective-permute-start = (bf16[256,512]{1,0:T(8,128)(2,1)S(1)}, bf16[256,512]{1,0:T(8,128)(2,1)S(1)}, u32[]{:S(2)}, u32[]{:S(2)}) collective-permute-start(bf16[256,512]{1,0:T(8,128)(2,1)S(1)} %dynamic-slice_bitcast_fusion), channel_id=1, source_target_pairs={{0,16},{16,0},{1,17},{17,1},{2,18},{18,2},{3,19},{19,3},{4,20},{20... | collective-permute-start | bytes 786440 | tf_op jit(solution)/shard_map/ppermute | solution.py:73
  73.9 28.1 %all-to-all-done.2 = bf16[32,48,256]{2,1,0:T(8,128)(2,1)S(1)} async-done(((bf16[32,48,256]{2,1,0:T(8,128)(2,1)}), bf16[32,48,256]{2,1,0:T(8,128)(2,1)S(1)}, u32[]{:S(2)}, u32[]{:S(2)}) %all-to-all-start.2) | async-done | bytes 786464 | tf_op jit(solution)/shard_map/all_to_all | solution.py:27
  102.1 0.4 fusion.8
  102.4 0.0 collective-permute-done
  102.4 1.3 add_convert_fusion
  103.7 12.7 %all-to-all-start.3 = ((bf16[24,32,512]{2,1,0:T(8,128)(2,1)}), bf16[24,32,512]{2,1,0:T(8,128)(2,1)S(1)}, u32[]{:S(2)}, u32[]{:S(2)}) async-start(bf16[24,32,512]{2,1,0:T(8,128)(2,1)} %bitcast.12), calls=%async_computation.3 | async-start | bytes 1572864 | tf_op jit(solution)/shard_map/all_to_all | solution.py:27
  116.5 0.7 constant_dynamic-slice_fusion.1
  117.2 17.6 %all-to-all-done.3 = bf16[24,32,512]{2,1,0:T(8,128)(2,1)S(1)} async-done(((bf16[24,32,512]{2,1,0:T(8,128)(2,1)}), bf16[24,32,512]{2,1,0:T(8,128)(2,1)S(1)}, u32[]{:S(2)}, u32[]{:S(2)}) %all-to-all-start.3) | async-done | bytes 786464 | tf_op jit(solution)/shard_map/all_to_all | solution.py:27
  134.8 0.1 convert_reduce_fusion
  134.9 0.1 broadcast_in_dim.5
  135.0 0.0 copy-start.6
  135.0 26.9 %all_to_all.27 = bf16[24,32,512]{2,1,0:T(8,128)(2,1)S(1)} all-to-all(bf16[24,32,512]{2,1,0:T(8,128)(2,1)S(1)} %broadcast_in_dim.5), channel_id=1, replica_groups=mesh['y'=8,'zl'=3,'c'=2,'zh'=4,'x'=4] {'y','zl'}, dimensions={0} | all-to-all | bytes 1572864 | tf_op jit(solution)/shard_map/all_to_all | solution.py:27
  161.9 0.4 convolution_multiply_fusion
  162.3 6.9 %collective-permute-start.1 = (f32[256,512]{1,0:T(8,128)S(1)}, f32[256,512]{1,0:T(8,128)S(1)}, u32[]{:S(2)}, u32[]{:S(2)}) collective-permute-start(f32[256,512]{1,0:T(8,128)S(1)} %convolution_multiply_fusion), channel_id=1, source_target_pairs={{0,16},{16,0},{1,17},{17,1},{2,18},{18,2},{3,19},{19,3},{4,20},{20... | collective-permute-start | bytes 1572872 | tf_op jit(solution)/shard_map/ppermute | solution.py:119
  169.2 1.5 collective-permute-done.1
  170.8 0.0 copy-done.6
  170.8 2.0 %divide_subtract_fusion = (f32[256,512]{1,0:T(8,128)}, f32[256,512]{1,0:T(8,128)}, f32[256,512]{1,0:T(8,128)}) fusion(f32[256,512]{1,0:T(8,128)S(1)} %copy-done.4, f32[256,512]{1,0:T(8,128)S(1)} %collective-permute-done.1, f32[256,512]{1,0:T(8,128)S(1)} %copy-done.6, f32[256,512]{1,0:T(8,128)S(1)} %copy-done.3, bf16[2,256,512]{2,1,0:T(8,128)(2,1)S(1)} %copy-done.5, ...), kind=kOutput, calls=%fused_computation.14 | convolution fusion | flops 204996608 | bytes 5375488 | tf_op jit(solution)/shard_map/dot_general | solution.py:117
  (12 shorter events, 0.1 us)
Async XLA Ops:
  0.6 1.1 copy-start
  1.8 1.0 copy-start.1
  2.8 1.0 copy-start.2
  56.0 15.4 %copy-start.3 = (f32[256,512]{1,0:T(8,128)S(1)}, f32[256,512]{1,0:T(8,128)}, u32[]{:S(2)}) copy-start(f32[256,512]{1,0:T(8,128)} %param.13) | copy-start | bytes 1572868
  56.1 15.4 %copy-start.4 = (f32[256,512]{1,0:T(8,128)S(1)}, f32[256,512]{1,0:T(8,128)}, u32[]{:S(2)}) copy-start(f32[256,512]{1,0:T(8,128)} %param.12) | copy-start | bytes 1572868
  56.1 15.4 %copy-start.5 = (bf16[2,256,512]{2,1,0:T(8,128)(2,1)S(1)}, bf16[2,256,512]{2,1,0:T(8,128)(2,1)}, u32[]{:S(2)}) copy-start(bf16[2,256,512]{2,1,0:T(8,128)(2,1)} %param.15) | copy-start | bytes 1572868
  57.0 45.0 %all-to-all-start.2 = ((bf16[32,48,256]{2,1,0:T(8,128)(2,1)}), bf16[32,48,256]{2,1,0:T(8,128)(2,1)S(1)}, u32[]{:S(2)}, u32[]{:S(2)}) async-start(bf16[32,48,256]{2,1,0:T(8,128)(2,1)} %bitcast.6), calls=%async_computation.2 | async-start | bytes 1572864 | tf_op jit(solution)/shard_map/all_to_all | solution.py:27
  71.8 30.7 %collective-permute-start = (bf16[256,512]{1,0:T(8,128)(2,1)S(1)}, bf16[256,512]{1,0:T(8,128)(2,1)S(1)}, u32[]{:S(2)}, u32[]{:S(2)}) collective-permute-start(bf16[256,512]{1,0:T(8,128)(2,1)S(1)} %dynamic-slice_bitcast_fusion), channel_id=1, source_target_pairs={{0,16},{16,0},{1,17},{17,1},{2,18},{18,2},{3,19},{19,3},{4,20},{20... | collective-permute-start | bytes 786440 | tf_op jit(solution)/shard_map/ppermute | solution.py:73
  103.7 31.1 %all-to-all-start.3 = ((bf16[24,32,512]{2,1,0:T(8,128)(2,1)}), bf16[24,32,512]{2,1,0:T(8,128)(2,1)S(1)}, u32[]{:S(2)}, u32[]{:S(2)}) async-start(bf16[24,32,512]{2,1,0:T(8,128)(2,1)} %bitcast.12), calls=%async_computation.3 | async-start | bytes 1572864 | tf_op jit(solution)/shard_map/all_to_all | solution.py:27
  135.0 35.7 %copy-start.6 = (f32[256,512]{1,0:T(8,128)S(1)}, f32[256,512]{1,0:T(8,128)}, u32[]{:S(2)}) copy-start(f32[256,512]{1,0:T(8,128)} %param.14) | copy-start | bytes 1572868
  162.3 8.5 %collective-permute-start.1 = (f32[256,512]{1,0:T(8,128)S(1)}, f32[256,512]{1,0:T(8,128)S(1)}, u32[]{:S(2)}, u32[]{:S(2)}) collective-permute-start(f32[256,512]{1,0:T(8,128)S(1)} %convolution_multiply_fusion), channel_id=1, source_target_pairs={{0,16},{16,0},{1,17},{17,1},{2,18},{18,2},{3,19},{19,3},{4,20},{20... | collective-permute-start | bytes 1572872 | tf_op jit(solution)/shard_map/ppermute | solution.py:119

commit v3 on v2

--- a/solution.py
+++ b/solution.py
@@ -20,7 +20,6 @@
 bf16 = jnp.bfloat16
 f32 = jnp.float32
 SWAP = [(0, 1), (1, 0)]
-ROWS = 16
 
 
 def trade(parts, axis):
@@ -49,7 +48,7 @@
         ],
         out_specs=pl.BlockSpec((count // blocks, 2 * both), lambda i: (i, 0)),
         out_shape=jax.ShapeDtypeStruct((count, 2 * both), bf16),
-        compiler_params=pltpu.CompilerParams(vmem_limit_bytes=16 * 1024 * 1024),
+        compiler_params=pltpu.CompilerParams(vmem_limit_bytes=56 * 1024 * 1024),
     )(tokens, gate_weights, up_weights)
 
 
@@ -82,9 +81,11 @@
     gate_sum, up_sum = sums[:, :both], sums[:, both:]
     hidden_share = (gate_sum * jax.nn.sigmoid(gate_sum) * up_sum).astype(bf16)
     share = hidden_share.shape[0]
-    out_parts = jnp.stack([hidden_share[:, :unit_count], hidden_share[:, unit_count:]])
-    out_parts = jnp.broadcast_to(out_parts[:, None], (size_c, size_zh * size_x, share, unit_count))
-    hidden = trade(out_parts.reshape(-1, share, unit_count), ("c", "zh", "x"))
+    hidden_rows = trade(jnp.broadcast_to(hidden_share[None], (size_zh, share, both)), "zh")
+    hidden_rows = hidden_rows.reshape(size_zh * share, both)
+    out_parts = jnp.stack([hidden_rows[:, :unit_count], hidden_rows[:, unit_count:]])
+    out_parts = jnp.broadcast_to(out_parts[:, None], (size_c, size_x) + out_parts.shape[1:])
+    hidden = trade(out_parts.reshape((size_c * size_x,) + out_parts.shape[2:]), ("c", "x"))
     hidden = hidden.reshape(size_c, token_count, unit_count)
     hidden_own = lax.dynamic_index_in_dim(hidden, core, 0, False)
     hidden_other = lax.dynamic_index_in_dim(hidden, 1 - core, 0, False)
@@ -96,19 +97,8 @@
     rows_share = token_count // chips
     partial = trade(partial.astype(bf16).reshape(chips, rows_share, width), ("y", "zl"))
     out_share = jnp.sum(partial.astype(f32), axis=0) * scale_out
-    chip = lax.axis_index("y") * size_zl + lax.axis_index("zl")
-    per_share = share // ROWS
-    goal = []
-    for piece in range(rows_share // ROWS):
-        place = chip * (rows_share // ROWS) + piece
-        owner = place // per_share
-        first_row = (
-            (owner % size_x) * (token_count // size_x)
-            + (owner // size_x) * share
-            + (place % per_share) * ROWS
-        )
-        goal.append(lax.dynamic_slice_in_dim(targets, first_row, ROWS, 0))
-    goal = jnp.concatenate(goal, axis=0).astype(f32)
+    first_row = (lax.axis_index("y") * size_zl + lax.axis_index("zl")) * rows_share
+    goal = lax.dynamic_slice_in_dim(targets, first_row, rows_share, 0).astype(f32)
     d_share = (error_gain * (out_share - goal)).astype(bf16)
     d_out = trade(jnp.broadcast_to(d_share[None], (chips, rows_share, width)), ("y", "zl"))
     d_out = d_out.reshape(token_count, width)

time: 173 us -> 168 us (0.971)
  waiting for transfers between devices: 47.2 us -> 39.8 us
  local copies, waits for them, and re-layouts: 5.02 us -> 1.78 us
  Pallas kernels: 2.03 us -> 4.78 us
  starting transfers between devices: 36 us -> 37.9 us
    all_to_all x2 -> x3, waiting for transfers between devices: 45.7 us -> 38.3 us  [trade(): return lax.all_to_all(parts, axis, 0, 0, tiled=True)]
    unnamed x14 -> x8, local copies, waits for them, and re-layouts: 3.23 us -> 0.03 us
    pallas_call x1, Pallas kernels: 2.03 us -> 4.78 us  [gate_up_terms(): pl.pallas_call(terms_kernel, grid=(blocks,), in_specs=[pl.BlockSpec((coun...]
    all_to_all x2 -> x3, starting transfers between devices: 26.9 us -> 28.9 us  [trade(): return lax.all_to_all(parts, axis, 0, 0, tiled=True)]
  transfers between devices with their start and end apart: 4 -> 5, of which waited for: 3 -> 4; matrix products, arithmetic and copies ran while one was open for 1% -> 0% of each run, Pallas kernels for 0% -> 0%
where the time goes in v3:
time: 168 us
  blocking collectives  76.8 us (46%)
  waiting for transfers between devices  39.8 us (24%)
  starting transfers between devices  37.9 us (23%)
  Pallas kernels  4.78 us (3%)
  matrix products  4.07 us (2%)
  local copies, waits for them, and re-layouts  1.78 us (1%)
  other arithmetic  1.68 us (1%)
    all_to_all x3, blocking collectives, trade(): return lax.all_to_all(parts, axis, 0, 0, tiled=True)  76.8 us
    all_to_all x3, waiting for transfers between devices, trade(): return lax.all_to_all(parts, axis, 0, 0, tiled=True)  38.3 us
    all_to_all x3, starting transfers between devices, trade(): return lax.all_to_all(parts, axis, 0, 0, tiled=True)  28.9 us
    ppermute x1, starting transfers between devices, shards(): grad_other = lax.ppermute(grad(hidden_other), 'c', SWAP)  7.02 us
    pallas_call x1, Pallas kernels, gate_up_terms(): pl.pallas_call(terms_kernel, grid=(blocks,), in_specs=[pl.BlockSpec((coun...  4.78 us
  transfers between devices with their start and end apart: 5, of which 4 were waited for; matrix products, arithmetic and copies ran while one was open for 0% of the time, Pallas kernels for 0%

profile of v3, /device:TPU:1, one launch (start us, length us, event | category | flops | bytes accessed | tf_op | source)
XLA Modules:
  0.0 167.5 jit_solution(7514874108484029677)
XLA Ops:
  0.6 4.8 %shard_map.103 = bf16[768,1024]{1,0:T(8,128)(2,1)} custom-call(bf16[768,512]{1,0:T(8,128)(2,1)} %tokens_ref.1, bf16[512,512]{1,0:T(8,128)(2,1)} %bitcast.50, bf16[512,512]{1,0:T(8,128)(2,1)} %bitcast.51), custom_call_target="tpu_custom_call" | custom-call | tf_op jit(solution)/shard_map/pallas_call | solution.py:41
  5.4 17.4 %all_to_all.30 = bf16[4,192,1024]{2,1,0:T(8,128)(2,1)S(1)} all-to-all(bf16[4,192,1024]{2,1,0:T(8,128)(2,1)} %bitcast.41), channel_id=1, replica_groups=mesh['y'=8,'zl'=3,'c'=2,'zh'=4,'x'=4] {'x'}, dimensions={0} | all-to-all | bytes 3145728 | tf_op jit(solution)/shard_map/all_to_all | solution.py:26
  22.8 0.3 reduce_sum.30
  23.1 32.5 %all_to_all.31 = bf16[4,48,1024]{2,1,0:T(8,128)(2,1)S(1)} all-to-all(bf16[4,48,1024]{2,1,0:T(8,128)(2,1)S(1)} %bitcast.48), channel_id=1, replica_groups=mesh['y'=8,'zl'=3,'c'=2,'zh'=4,'x'=4] {'zh'}, dimensions={0} | all-to-all | bytes 786432 | tf_op jit(solution)/shard_map/all_to_all | solution.py:26
  55.6 0.1 convert_reduce_fusion.1
  55.8 0.7 broadcast_in_dim.6
  56.5 6.5 %all-to-all-start.2 = ((bf16[4,48,512]{2,1,0:T(8,128)(2,1)}), bf16[4,48,512]{2,1,0:T(8,128)(2,1)S(1)}, u32[]{:S(2)}, u32[]{:S(2)}) async-start(bf16[4,48,512]{2,1,0:T(8,128)(2,1)} %broadcast_in_dim.6), calls=%async_computation.2 | async-start | bytes 393216 | tf_op jit(solution)/shard_map/all_to_all | solution.py:26
  62.9 10.0 %all-to-all-done.2 = bf16[4,48,512]{2,1,0:T(8,128)(2,1)S(1)} async-done(((bf16[4,48,512]{2,1,0:T(8,128)(2,1)}), bf16[4,48,512]{2,1,0:T(8,128)(2,1)S(1)}, u32[]{:S(2)}, u32[]{:S(2)}) %all-to-all-start.2) | async-done | bytes 196640 | tf_op jit(solution)/shard_map/all_to_all | solution.py:26
  72.9 0.0 copy-start
  73.0 0.0 copy-start.1
  73.0 0.0 copy-start.2
  73.0 0.9 broadcast_in_dim.7
  73.9 13.1 %all-to-all-start.3 = ((bf16[8,192,256]{2,1,0:T(8,128)(2,1)}), bf16[8,192,256]{2,1,0:T(8,128)(2,1)S(1)}, u32[]{:S(2)}, u32[]{:S(2)}) async-start(bf16[8,192,256]{2,1,0:T(8,128)(2,1)} %bitcast.7), calls=%async_computation.3 | async-start | bytes 1572864 | tf_op jit(solution)/shard_map/all_to_all | solution.py:26
  87.1 0.0 copy-done
  87.1 0.2 multiply_sqrt_fusion
  87.2 0.2 add_convert_fusion.1
  87.5 2.0 %collective-permute-start = (bf16[256,512]{1,0:T(8,128)(2,1)S(1)}, bf16[256,512]{1,0:T(8,128)(2,1)S(1)}, u32[]{:S(2)}, u32[]{:S(2)}) collective-permute-start(bf16[256,512]{1,0:T(8,128)(2,1)S(1)} %dynamic-slice_bitcast_fusion), channel_id=1, source_target_pairs={{0,16},{16,0},{1,17},{17,1},{2,18},{18,2},{3,19},{19,3},{4,20},{20... | collective-permute-start | bytes 786440 | tf_op jit(solution)/shard_map/ppermute | solution.py:72
  89.5 9.8 %all-to-all-done.3 = bf16[8,192,256]{2,1,0:T(8,128)(2,1)S(1)} async-done(((bf16[8,192,256]{2,1,0:T(8,128)(2,1)}), bf16[8,192,256]{2,1,0:T(8,128)(2,1)S(1)}, u32[]{:S(2)}, u32[]{:S(2)}) %all-to-all-start.3) | async-done | bytes 786464 | tf_op jit(solution)/shard_map/all_to_all | solution.py:26
  99.2 0.4 fusion.8
  99.6 0.0 collective-permute-done
  99.6 1.3 add_convert_fusion
  100.9 9.3 %all-to-all-start.4 = ((bf16[24,32,512]{2,1,0:T(8,128)(2,1)}), bf16[24,32,512]{2,1,0:T(8,128)(2,1)S(1)}, u32[]{:S(2)}, u32[]{:S(2)}) async-start(bf16[24,32,512]{2,1,0:T(8,128)(2,1)} %bitcast.13), calls=%async_computation.4 | async-start | bytes 1572864 | tf_op jit(solution)/shard_map/all_to_all | solution.py:26
  110.2 18.5 %all-to-all-done.4 = bf16[24,32,512]{2,1,0:T(8,128)(2,1)S(1)} async-done(((bf16[24,32,512]{2,1,0:T(8,128)(2,1)}), bf16[24,32,512]{2,1,0:T(8,128)(2,1)S(1)}, u32[]{:S(2)}, u32[]{:S(2)}) %all-to-all-start.4) | async-done | bytes 786464 | tf_op jit(solution)/shard_map/all_to_all | solution.py:26
  128.7 0.1 convert_reduce_fusion
  128.8 0.8 multiply_convert_fusion
  129.6 0.1 broadcast_in_dim.8
  129.7 0.0 copy-start.3
  129.7 26.8 %all_to_all.32 = bf16[24,32,512]{2,1,0:T(8,128)(2,1)S(1)} all-to-all(bf16[24,32,512]{2,1,0:T(8,128)(2,1)S(1)} %broadcast_in_dim.8), channel_id=1, replica_groups=mesh['y'=8,'zl'=3,'c'=2,'zh'=4,'x'=4] {'y','zl'}, dimensions={0} | all-to-all | bytes 1572864 | tf_op jit(solution)/shard_map/all_to_all | solution.py:26
  156.5 0.4 convolution_multiply_fusion
  156.9 7.0 %collective-permute-start.1 = (f32[256,512]{1,0:T(8,128)S(1)}, f32[256,512]{1,0:T(8,128)S(1)}, u32[]{:S(2)}, u32[]{:S(2)}) collective-permute-start(f32[256,512]{1,0:T(8,128)S(1)} %convolution_multiply_fusion), channel_id=1, source_target_pairs={{0,16},{16,0},{1,17},{17,1},{2,18},{18,2},{3,19},{19,3},{4,20},{20... | collective-permute-start | bytes 1572872 | tf_op jit(solution)/shard_map/ppermute | solution.py:109
  164.0 1.5 collective-permute-done.1
  165.5 2.0 %divide_subtract_fusion = (f32[256,512]{1,0:T(8,128)}, f32[256,512]{1,0:T(8,128)}, f32[256,512]{1,0:T(8,128)}) fusion(f32[256,512]{1,0:T(8,128)S(1)} %copy-done.1, f32[256,512]{1,0:T(8,128)S(1)} %collective-permute-done.1, f32[256,512]{1,0:T(8,128)S(1)} %copy-done.3, f32[256,512]{1,0:T(8,128)S(1)} %copy-done, bf16[2,256,512]{2,1,0:T(8,128)(2,1)S(1)} %copy-done.2, ...), kind=kOutput, calls=%fused_computation.14 | convolution fusion | flops 204996608 | bytes 5375488 | tf_op jit(solution)/shard_map/dot_general | solution.py:107
  (8 shorter events, 0.1 us)
Async XLA Ops:
  56.5 16.4 %all-to-all-start.2 = ((bf16[4,48,512]{2,1,0:T(8,128)(2,1)}), bf16[4,48,512]{2,1,0:T(8,128)(2,1)S(1)}, u32[]{:S(2)}, u32[]{:S(2)}) async-start(bf16[4,48,512]{2,1,0:T(8,128)(2,1)} %broadcast_in_dim.6), calls=%async_computation.2 | async-start | bytes 393216 | tf_op jit(solution)/shard_map/all_to_all | solution.py:26
  72.9 14.1 %copy-start = (f32[256,512]{1,0:T(8,128)S(1)}, f32[256,512]{1,0:T(8,128)}, u32[]{:S(2)}) copy-start(f32[256,512]{1,0:T(8,128)} %param.13) | copy-start | bytes 1572868
  73.0 14.3 %copy-start.1 = (f32[256,512]{1,0:T(8,128)S(1)}, f32[256,512]{1,0:T(8,128)}, u32[]{:S(2)}) copy-start(f32[256,512]{1,0:T(8,128)} %param.12) | copy-start | bytes 1572868
  73.0 14.3 %copy-start.2 = (bf16[2,256,512]{2,1,0:T(8,128)(2,1)S(1)}, bf16[2,256,512]{2,1,0:T(8,128)(2,1)}, u32[]{:S(2)}) copy-start(bf16[2,256,512]{2,1,0:T(8,128)(2,1)} %param.15) | copy-start | bytes 1572868
  73.9 25.3 %all-to-all-start.3 = ((bf16[8,192,256]{2,1,0:T(8,128)(2,1)}), bf16[8,192,256]{2,1,0:T(8,128)(2,1)S(1)}, u32[]{:S(2)}, u32[]{:S(2)}) async-start(bf16[8,192,256]{2,1,0:T(8,128)(2,1)} %bitcast.7), calls=%async_computation.3 | async-start | bytes 1572864 | tf_op jit(solution)/shard_map/all_to_all | solution.py:26
  87.5 12.1 %collective-permute-start = (bf16[256,512]{1,0:T(8,128)(2,1)S(1)}, bf16[256,512]{1,0:T(8,128)(2,1)S(1)}, u32[]{:S(2)}, u32[]{:S(2)}) collective-permute-start(bf16[256,512]{1,0:T(8,128)(2,1)S(1)} %dynamic-slice_bitcast_fusion), channel_id=1, source_target_pairs={{0,16},{16,0},{1,17},{17,1},{2,18},{18,2},{3,19},{19,3},{4,20},{20... | collective-permute-start | bytes 786440 | tf_op jit(solution)/shard_map/ppermute | solution.py:72
  100.9 27.8 %all-to-all-start.4 = ((bf16[24,32,512]{2,1,0:T(8,128)(2,1)}), bf16[24,32,512]{2,1,0:T(8,128)(2,1)S(1)}, u32[]{:S(2)}, u32[]{:S(2)}) async-start(bf16[24,32,512]{2,1,0:T(8,128)(2,1)} %bitcast.13), calls=%async_computation.4 | async-start | bytes 1572864 | tf_op jit(solution)/shard_map/all_to_all | solution.py:26
  129.7 35.8 %copy-start.3 = (f32[256,512]{1,0:T(8,128)S(1)}, f32[256,512]{1,0:T(8,128)}, u32[]{:S(2)}) copy-start(f32[256,512]{1,0:T(8,128)} %param.14) | copy-start | bytes 1572868
  156.9 8.5 %collective-permute-start.1 = (f32[256,512]{1,0:T(8,128)S(1)}, f32[256,512]{1,0:T(8,128)S(1)}, u32[]{:S(2)}, u32[]{:S(2)}) collective-permute-start(f32[256,512]{1,0:T(8,128)S(1)} %convolution_multiply_fusion), channel_id=1, source_target_pairs={{0,16},{16,0},{1,17},{17,1},{2,18},{18,2},{3,19},{19,3},{4,20},{20... | collective-permute-start | bytes 1572872 | tf_op jit(solution)/shard_map/ppermute | solution.py:109

commit v4 on v3

--- a/solution.py
+++ b/solution.py
@@ -19,11 +19,16 @@
 
 bf16 = jnp.bfloat16
 f32 = jnp.float32
+SHAPE = (8, 3, 2, 4, 4)
 SWAP = [(0, 1), (1, 0)]
 
 
 def trade(parts, axis):
     return lax.all_to_all(parts, axis, 0, 0, tiled=True)
+
+
+def turn(size, steps):
+    return [(i, (i + steps) % size) for i in range(size)]
 
 
 def terms_kernel(tokens_ref, gate_ref, up_ref, terms_ref):
@@ -65,49 +70,66 @@
     both = 2 * unit_count
     core = lax.axis_index("c")
 
-    inv_sigma = jnp.sqrt(prior_size * (hessian + weight_decay))
-    noise_f = noise.astype(f32)
-    samples = (means[None] + noise_f / inv_sigma[None]).astype(bf16)
-    weights_own = lax.dynamic_index_in_dim(samples, core, 0, False)
-    weights_other = lax.ppermute(lax.dynamic_index_in_dim(samples, 1 - core, 0, False), "c", SWAP)
-
     terms = gate_up_terms(
         tokens, gate_weights.reshape(both, width), up_weights.reshape(both, width), size_x
     )
     terms = trade(terms.reshape(size_x, -1, 2 * both), "x")
     terms = jnp.sum(terms.astype(f32), axis=0).astype(bf16)
+
+    inv_sigma = jnp.sqrt(prior_size * (hessian + weight_decay))
+    samples = (means[None] + noise.astype(f32) / inv_sigma[None]).astype(bf16)
+    weights_own = lax.dynamic_index_in_dim(samples, core, 0, False)
+    weights_other = lax.ppermute(lax.dynamic_index_in_dim(samples, 1 - core, 0, False), "c", SWAP)
+    weights = jnp.concatenate([weights_own, weights_other], axis=0)
+    terms, weights = lax.optimization_barrier((terms, weights))
+    wide = jnp.concatenate([weights] + [lax.ppermute(weights, "x", turn(size_x, k)) for k in range(1, size_x)], axis=1)
+
     terms = trade(terms.reshape(size_zh, -1, 2 * both), "zh")
     sums = jnp.sum(terms.astype(f32), axis=0) * scale_in
     gate_sum, up_sum = sums[:, :both], sums[:, both:]
     hidden_share = (gate_sum * jax.nn.sigmoid(gate_sum) * up_sum).astype(bf16)
     share = hidden_share.shape[0]
-    hidden_rows = trade(jnp.broadcast_to(hidden_share[None], (size_zh, share, both)), "zh")
-    hidden_rows = hidden_rows.reshape(size_zh * share, both)
-    out_parts = jnp.stack([hidden_rows[:, :unit_count], hidden_rows[:, unit_count:]])
-    out_parts = jnp.broadcast_to(out_parts[:, None], (size_c, size_x) + out_parts.shape[1:])
-    hidden = trade(out_parts.reshape((size_c * size_x,) + out_parts.shape[2:]), ("c", "x"))
-    hidden = hidden.reshape(size_c, token_count, unit_count)
+    parts = jnp.stack([hidden_share[:, :unit_count], hidden_share[:, unit_count:]])
+    parts = jnp.broadcast_to(parts[:, None], (size_c, size_zh, share, unit_count))
+    hidden = trade(parts.reshape(-1, share, unit_count), ("c", "zh"))
+    rows_x = size_zh * share
+    hidden = hidden.reshape(size_c, rows_x, unit_count)
     hidden_own = lax.dynamic_index_in_dim(hidden, core, 0, False)
     hidden_other = lax.dynamic_index_in_dim(hidden, 1 - core, 0, False)
 
-    partial = jnp.dot(hidden_own, weights_own, preferred_element_type=f32) + jnp.dot(
-        hidden_other, weights_other, preferred_element_type=f32
+    partial = jnp.dot(hidden_own, wide[:unit_count], preferred_element_type=f32) + jnp.dot(
+        hidden_other, wide[unit_count:], preferred_element_type=f32
     )
     chips = size_y * size_zl
-    rows_share = token_count // chips
-    partial = trade(partial.astype(bf16).reshape(chips, rows_share, width), ("y", "zl"))
-    out_share = jnp.sum(partial.astype(f32), axis=0) * scale_out
-    first_row = (lax.axis_index("y") * size_zl + lax.axis_index("zl")) * rows_share
-    goal = lax.dynamic_slice_in_dim(targets, first_row, rows_share, 0).astype(f32)
-    d_share = (error_gain * (out_share - goal)).astype(bf16)
-    d_out = trade(jnp.broadcast_to(d_share[None], (chips, rows_share, width)), ("y", "zl"))
-    d_out = d_out.reshape(token_count, width)
+    rows_share = rows_x // chips
+    partial = partial.astype(bf16).reshape(chips, rows_share, size_x * width)
+    hidden, partial = lax.optimization_barrier((hidden, partial))
+    here = lax.axis_index("x")
+    rows = jnp.zeros((size_c, size_x, rows_x, unit_count), bf16)
+    for k in range(size_x):
+        block = hidden if k == 0 else lax.ppermute(hidden, "x", turn(size_x, k))
+        rows = lax.dynamic_update_slice(rows, block[:, None], (0, (here - k) % size_x, 0, 0))
+    rows = rows.reshape(size_c, token_count, unit_count)
+    rows_own = lax.dynamic_index_in_dim(rows, core, 0, False)
+    rows_other = lax.dynamic_index_in_dim(rows, 1 - core, 0, False)
+
+    partial, rows_own, rows_other = lax.optimization_barrier(
+        (trade(partial, ("y", "zl")), rows_own, rows_other)
+    )
+    out_share = (jnp.sum(partial.astype(f32), axis=0) * scale_out).astype(bf16)
+    out_share = out_share.reshape(rows_share, size_x, width)
+    sends = jnp.stack(
+        [lax.dynamic_index_in_dim(out_share, (here - place) % size_x, 1, False) for place in range(size_x)]
+    )
+    sends = jnp.broadcast_to(sends[:, None], (size_x, chips, rows_share, width))
+    out = trade(sends.reshape(-1, rows_share, width), ("x", "y", "zl")).reshape(token_count, width)
+    d_out = (error_gain * (out.astype(f32) - targets.astype(f32))).astype(bf16)
 
     def grad(hidden_part):
         return jnp.dot(hidden_part.T, d_out, preferred_element_type=f32) * scale_out
 
-    grad_other = lax.ppermute(grad(hidden_other), "c", SWAP)
-    grad_own = grad(hidden_own)
+    grad_other = lax.ppermute(grad(rows_other), "c", SWAP)
+    grad_own = grad(rows_own)
     noise_own = lax.dynamic_index_in_dim(noise, core, 0, False).astype(f32)
     noise_other = lax.dynamic_index_in_dim(noise, 1 - core, 0, False).astype(f32)
     grad_mean = 0.5 * (grad_own + grad_other)
@@ -126,7 +148,7 @@
 
 
 def solution(mesh):
-    fine = Mesh(mesh.devices.reshape(8, 3, 2, 4, 4), ("y", "zl", "c", "zh", "x"))
+    fine = Mesh(mesh.devices.reshape(SHAPE), ("y", "zl", "c", "zh", "x"))
     dp, fsdp = ("y", "zl", "c"), ("zh", "x")
     in_specs = (
         P(None, fsdp),

time: 168 us -> 156 us (0.929)
  starting transfers between devices: 37.9 us -> 82.6 us
  blocking collectives: 76.8 us -> 32.5 us
  waiting for transfers between devices: 39.8 us -> 23.4 us
  local copies, waits for them, and re-layouts: 1.78 us -> 4.39 us
    all_to_all x3 -> x1, blocking collectives: 76.8 us -> 32.5 us  [trade(): return lax.all_to_all(parts, axis, 0, 0, tiled=True)]
    all_to_all x3 -> x4, waiting for transfers between devices: 38.3 us -> 11.4 us  [trade(): return lax.all_to_all(parts, axis, 0, 0, tiled=True)]
    all_to_all x3 -> x4, starting transfers between devices: 28.9 us -> 50.6 us  [trade(): return lax.all_to_all(parts, axis, 0, 0, tiled=True)]
    ppermute x1 -> x7, starting transfers between devices: 7.02 us -> 20.8 us  [the longest x3 8.42 us: shards(): block = hidden if k == 0 else lax.ppermute(hidden, 'x', turn(size_x, k))]
    ppermute x1 -> x7, waiting for transfers between devices: 1.51 us -> 10.9 us  [the longest x3 7.15 us: shards(): block = hidden if k == 0 else lax.ppermute(hidden, 'x', turn(size_x, k))]
    ppermute x1, starting transfers between devices: 2.01 us -> 11.2 us  [shards(): lax.ppermute(lax.dynamic_index_in_dim(samples, 1 - core, 0, False), 'c',...]
    unnamed x8 -> x17, local copies, waits for them, and re-layouts: 0.03 us -> 2.3 us
  transfers between devices with their start and end apart: 5 -> 12, of which waited for: 4 -> 9; matrix products, arithmetic and copies ran while one was open for 0% -> 3% of each run, Pallas kernels for 0% -> 0%
where the time goes in v4:
time: 156 us; the launch traced here: 155 us
  starting transfers between devices  82.6 us (53%)
  blocking collectives  32.5 us (21%)
  waiting for transfers between devices  23.4 us (15%)
  Pallas kernels  4.76 us (3%)
  local copies, waits for them, and re-layouts  4.39 us (3%)
  matrix products  4.23 us (3%)
  other arithmetic  1.76 us (1%)
    all_to_all x4, starting transfers between devices, trade(): return lax.all_to_all(parts, axis, 0, 0, tiled=True)  50.6 us
    all_to_all x1, blocking collectives, trade(): return lax.all_to_all(parts, axis, 0, 0, tiled=True)  32.5 us
    all_to_all x4, waiting for transfers between devices, trade(): return lax.all_to_all(parts, axis, 0, 0, tiled=True)  11.4 us
    ppermute x1, starting transfers between devices, shards(): lax.ppermute(lax.dynamic_index_in_dim(samples, 1 - core, 0, False), 'c',...  11.2 us
    ppermute x3, starting transfers between devices, shards(): block = hidden if k == 0 else lax.ppermute(hidden, 'x', turn(size_x, k))  8.42 us
    ppermute x3, starting transfers between devices, shards(): lax.ppermute(weights, 'x', turn(size_x, k))  8.41 us
    ppermute x3, waiting for transfers between devices, shards(): block = hidden if k == 0 else lax.ppermute(hidden, 'x', turn(size_x, k))  7.15 us
    pallas_call x1, Pallas kernels, gate_up_terms(): pl.pallas_call(terms_kernel, grid=(blocks,), in_specs=[pl.BlockSpec((coun...  4.76 us
  transfers between devices with their start and end apart: 12, of which 9 were waited for; matrix products, arithmetic and copies ran while one was open for 3% of the time, Pallas kernels for 0%

profile of v4, /device:TPU:1, one launch (start us, length us, event | category | flops | bytes accessed | tf_op | source)
XLA Modules:
  0.0 154.7 jit_solution(10686333885081381491)
XLA Ops:
  0.6 4.8 %shard_map.103 = bf16[768,1024]{1,0:T(8,128)(2,1)} custom-call(bf16[768,512]{1,0:T(8,128)(2,1)} %tokens_ref.1, bf16[512,512]{1,0:T(8,128)(2,1)} %bitcast.77, bf16[512,512]{1,0:T(8,128)(2,1)} %bitcast.78), custom_call_target="tpu_custom_call" | custom-call | tf_op jit(solution)/shard_map/pallas_call | solution.py:46
  5.4 5.0 %all-to-all-start = ((bf16[4,192,1024]{2,1,0:T(8,128)(2,1)}), bf16[4,192,1024]{2,1,0:T(8,128)(2,1)S(1)}, u32[]{:S(2)}, u32[]{:S(2)}) async-start(bf16[4,192,1024]{2,1,0:T(8,128)(2,1)} %bitcast.68), calls=%async_computation | async-start | bytes 3145728 | tf_op jit(solution)/shard_map/all_to_all | solution.py:27
  10.8 11.2 %collective-permute-start = (bf16[256,512]{1,0:T(8,128)(2,1)S(1)}, bf16[256,512]{1,0:T(8,128)(2,1)S(1)}, u32[]{:S(2)}, u32[]{:S(2)}) collective-permute-start(bf16[256,512]{1,0:T(8,128)(2,1)S(1)} %get-tuple-element.23), channel_id=1, source_target_pairs={{0,16},{16,0},{1,17},{17,1},{2,18},{18,2},{3,19},{19,3},{4,20},{20... | collective-permute-start | bytes 786440 | tf_op jit(solution)/shard_map/ppermute | solution.py:82
  22.0 1.1 collective-permute-done
  23.2 1.1 reduce_sum.30
  24.3 21.2 %all-to-all-start.1 = ((bf16[4,48,1024]{2,1,0:T(8,128)(2,1)}), bf16[4,48,1024]{2,1,0:T(8,128)(2,1)S(1)}, u32[]{:S(2)}, u32[]{:S(2)}) async-start(bf16[4,48,1024]{2,1,0:T(8,128)(2,1)} %bitcast.5), calls=%async_computation.1 | async-start | bytes 786432 | tf_op jit(solution)/shard_map/all_to_all | solution.py:27
  45.5 2.2 %collective-permute-start.1 = (bf16[512,512]{1,0:T(8,128)(2,1)S(1)}, bf16[512,512]{1,0:T(8,128)(2,1)}, u32[]{:S(2)}, u32[]{:S(2)}) collective-permute-start(bf16[512,512]{1,0:T(8,128)(2,1)S(1)} %pad_maximum_fusion), channel_id=1, source_target_pairs={{0,1},{1,2},{2,3},{3,0},{4,5},{5,6},{6,7},{7,4},{8,9},{9,10},{10,1... | collective-permute-start | bytes 1572872 | tf_op jit(solution)/shard_map/ppermute | solution.py:85
  47.7 3.7 %collective-permute-start.2 = (bf16[512,512]{1,0:T(8,128)(2,1)S(1)}, bf16[512,512]{1,0:T(8,128)(2,1)}, u32[]{:S(2)}, u32[]{:S(2)}) collective-permute-start(bf16[512,512]{1,0:T(8,128)(2,1)S(1)} %pad_maximum_fusion), channel_id=1, source_target_pairs={{0,2},{1,3},{2,0},{3,1},{4,6},{5,7},{6,4},{7,5},{8,10},{9,11},{10,... | collective-permute-start | bytes 1572872 | tf_op jit(solution)/shard_map/ppermute | solution.py:85
  51.4 2.5 %collective-permute-start.3 = (bf16[512,512]{1,0:T(8,128)(2,1)S(1)}, bf16[512,512]{1,0:T(8,128)(2,1)}, u32[]{:S(2)}, u32[]{:S(2)}) collective-permute-start(bf16[512,512]{1,0:T(8,128)(2,1)S(1)} %pad_maximum_fusion), channel_id=1, source_target_pairs={{0,3},{1,0},{2,1},{3,2},{4,7},{5,4},{6,5},{7,6},{8,11},{9,8},{10,9... | collective-permute-start | bytes 1572872 | tf_op jit(solution)/shard_map/ppermute | solution.py:85
  54.0 2.9 %all-to-all-done.1 = bf16[4,48,1024]{2,1,0:T(8,128)(2,1)S(1)} async-done(((bf16[4,48,1024]{2,1,0:T(8,128)(2,1)}), bf16[4,48,1024]{2,1,0:T(8,128)(2,1)S(1)}, u32[]{:S(2)}, u32[]{:S(2)}) %all-to-all-start.1) | async-done | bytes 393248 | tf_op jit(solution)/shard_map/all_to_all | solution.py:27
  57.0 0.7 broadcast_in_dim.14
  57.7 12.9 %all-to-all-start.2 = ((bf16[8,48,256]{2,1,0:T(8,128)(2,1)}), bf16[8,48,256]{2,1,0:T(8,128)(2,1)S(1)}, u32[]{:S(2)}, u32[]{:S(2)}) async-start(bf16[8,48,256]{2,1,0:T(8,128)(2,1)} %bitcast.8), calls=%async_computation.2 | async-start | bytes 393216 | tf_op jit(solution)/shard_map/all_to_all | solution.py:27
  70.7 1.1 constant_dynamic-update-slice_fusion.2
  71.8 1.1 constant_dynamic-update-slice_fusion.1
  72.9 2.3 %collective-permute-done.3 = bf16[512,512]{1,0:T(8,128)(2,1)} collective-permute-done((bf16[512,512]{1,0:T(8,128)(2,1)S(1)}, bf16[512,512]{1,0:T(8,128)(2,1)}, u32[]{:S(2)}, u32[]{:S(2)}) %collective-permute-start.3) | collective-permute-done | bytes 524320 | tf_op jit(solution)/shard_map/ppermute | solution.py:85
  75.2 1.1 constant_dynamic-update-slice_fusion
  76.3 4.9 %all-to-all-done.2 = bf16[8,48,256]{2,1,0:T(8,128)(2,1)S(1)} async-done(((bf16[8,48,256]{2,1,0:T(8,128)(2,1)}), bf16[8,48,256]{2,1,0:T(8,128)(2,1)S(1)}, u32[]{:S(2)}, u32[]{:S(2)}) %all-to-all-start.2) | async-done | bytes 196640 | tf_op jit(solution)/shard_map/all_to_all | solution.py:27
  81.2 0.4 fusion.4
  81.5 1.3 fusion.1
  82.8 11.5 %all-to-all-start.3 = ((bf16[24,8,2048]{2,1,0:T(8,128)(2,1)}), bf16[24,8,2048]{2,1,0:T(8,128)(2,1)S(1)}, u32[]{:S(2)}, u32[]{:S(2)}) async-start(bf16[24,8,2048]{2,1,0:T(8,128)(2,1)} %fusion.1), calls=%async_computation.3 | async-start | bytes 1572864 | tf_op jit(solution)/shard_map/all_to_all | solution.py:27
  94.4 2.2 %collective-permute-start.4 = (bf16[2,192,256]{2,1,0:T(8,128)(2,1)S(1)}, bf16[2,192,256]{2,1,0:T(8,128)(2,1)S(1)}, u32[]{:S(2)}, u32[]{:S(2)}) collective-permute-start(bf16[2,192,256]{2,1,0:T(8,128)(2,1)S(1)} %bitcast.73), channel_id=1, source_target_pairs={{0,1},{1,2},{2,3},{3,0},{4,5},{5,6},{6,7},{7,4},{8,9},{9,10},{10,1... | collective-permute-start | bytes 589832 | tf_op jit(solution)/shard_map/ppermute | solution.py:110
  96.6 3.7 %collective-permute-start.5 = (bf16[2,192,256]{2,1,0:T(8,128)(2,1)S(1)}, bf16[2,192,256]{2,1,0:T(8,128)(2,1)S(1)}, u32[]{:S(2)}, u32[]{:S(2)}) collective-permute-start(bf16[2,192,256]{2,1,0:T(8,128)(2,1)S(1)} %bitcast.74), channel_id=1, source_target_pairs={{0,2},{1,3},{2,0},{3,1},{4,6},{5,7},{6,4},{7,5},{8,10},{9,11},{10,... | collective-permute-start | bytes 589832 | tf_op jit(solution)/shard_map/ppermute | solution.py:110
  100.3 2.5 %collective-permute-start.6 = (bf16[2,192,256]{2,1,0:T(8,128)(2,1)S(1)}, bf16[2,192,256]{2,1,0:T(8,128)(2,1)S(1)}, u32[]{:S(2)}, u32[]{:S(2)}) collective-permute-start(bf16[2,192,256]{2,1,0:T(8,128)(2,1)S(1)} %bitcast.75), channel_id=1, source_target_pairs={{0,3},{1,0},{2,1},{3,2},{4,7},{5,4},{6,5},{7,6},{8,11},{9,8},{10,9... | collective-permute-start | bytes 589832 | tf_op jit(solution)/shard_map/ppermute | solution.py:110
  102.9 1.4 collective-permute-done.4
  104.3 3.0 %collective-permute-done.5 = bf16[2,192,256]{2,1,0:T(8,128)(2,1)S(1)} collective-permute-done((bf16[2,192,256]{2,1,0:T(8,128)(2,1)S(1)}, bf16[2,192,256]{2,1,0:T(8,128)(2,1)S(1)}, u32[]{:S(2)}, u32[]{:S(2)}) %collective-permute-start.5) | collective-permute-done | bytes 196640 | tf_op jit(solution)/shard_map/ppermute | solution.py:110
  107.4 2.7 %collective-permute-done.6 = bf16[2,192,256]{2,1,0:T(8,128)(2,1)S(1)} collective-permute-done((bf16[2,192,256]{2,1,0:T(8,128)(2,1)S(1)}, bf16[2,192,256]{2,1,0:T(8,128)(2,1)S(1)}, u32[]{:S(2)}, u32[]{:S(2)}) %collective-permute-start.6) | collective-permute-done | bytes 196640 | tf_op jit(solution)/shard_map/ppermute | solution.py:110
  110.2 3.6 %all-to-all-done.3 = bf16[24,8,2048]{2,1,0:T(8,128)(2,1)S(1)} async-done(((bf16[24,8,2048]{2,1,0:T(8,128)(2,1)}), bf16[24,8,2048]{2,1,0:T(8,128)(2,1)S(1)}, u32[]{:S(2)}, u32[]{:S(2)}) %all-to-all-start.3) | async-done | bytes 786464 | tf_op jit(solution)/shard_map/all_to_all | solution.py:27
  114.1 32.5 %all_to_all.25 = bf16[96,8,512]{2,1,0:T(8,128)(2,1)S(1)} all-to-all(bf16[96,8,512]{2,1,0:T(8,128)(2,1)S(1)} %bitcast.69), channel_id=1, replica_groups=mesh['y'=8,'zl'=3,'c'=2,'zh'=4,'x'=4] {'x','y','zl'}, dimensions={0} | all-to-all | bytes 1572864 | tf_op jit(solution)/shard_map/all_to_all | solution.py:27
  146.6 0.5 convolution_multiply_fusion
  147.1 4.0 %collective-permute-start.7 = (f32[256,512]{1,0:T(8,128)S(1)}, f32[256,512]{1,0:T(8,128)S(1)}, u32[]{:S(2)}, u32[]{:S(2)}) collective-permute-start(f32[256,512]{1,0:T(8,128)S(1)} %convolution_multiply_fusion), channel_id=1, source_target_pairs={{0,16},{16,0},{1,17},{17,1},{2,18},{18,2},{3,19},{19,3},{4,20},{20... | collective-permute-start | bytes 1572872 | tf_op jit(solution)/shard_map/ppermute | solution.py:131
  151.1 1.5 collective-permute-done.7
  152.6 2.1 %divide_subtract_fusion = (f32[256,512]{1,0:T(8,128)}, f32[256,512]{1,0:T(8,128)}, f32[256,512]{1,0:T(8,128)}) fusion(f32[256,512]{1,0:T(8,128)S(1)} %copy-done.2, f32[256,512]{1,0:T(8,128)S(1)} %collective-permute-done.7, f32[256,512]{1,0:T(8,128)S(1)} %copy-done.6, f32[256,512]{1,0:T(8,128)S(1)} %copy-done, bf16[2,256,512]{2,1,0:T(8,128)(2,1)S(1)} %copy-done.4, ...), kind=kOutput, calls=%fused_computation.23 | convolution fusion | flops 206962688 | bytes 6160392 | tf_op jit(solution)/shard_map/dot_general | solution.py:129
  (38 shorter events, 1.0 us)
Async XLA Ops:
  5.4 5.0 %copy-start = (f32[256,512]{1,0:T(8,128)S(1)}, f32[256,512]{1,0:T(8,128)}, u32[]{:S(2)}) copy-start(f32[256,512]{1,0:T(8,128)} %param.13) | copy-start | bytes 1572868
  5.4 5.2 %copy-start.1 = (f32[256,512]{1,0:T(8,128)S(1)}, f32[256,512]{1,0:T(8,128)}, u32[]{:S(2)}) copy-start(f32[256,512]{1,0:T(8,128)} %param.12) | copy-start | bytes 1572868
  5.4 5.2 %copy-start.3 = (bf16[2,256,512]{2,1,0:T(8,128)(2,1)S(1)}, bf16[2,256,512]{2,1,0:T(8,128)(2,1)}, u32[]{:S(2)}) copy-start(bf16[2,256,512]{2,1,0:T(8,128)(2,1)} %param.15) | copy-start | bytes 1572868
  5.4 17.8 %all-to-all-start = ((bf16[4,192,1024]{2,1,0:T(8,128)(2,1)}), bf16[4,192,1024]{2,1,0:T(8,128)(2,1)S(1)}, u32[]{:S(2)}, u32[]{:S(2)}) async-start(bf16[4,192,1024]{2,1,0:T(8,128)(2,1)} %bitcast.68), calls=%async_computation | async-start | bytes 3145728 | tf_op jit(solution)/shard_map/all_to_all | solution.py:27
  10.8 12.3 %collective-permute-start = (bf16[256,512]{1,0:T(8,128)(2,1)S(1)}, bf16[256,512]{1,0:T(8,128)(2,1)S(1)}, u32[]{:S(2)}, u32[]{:S(2)}) collective-permute-start(bf16[256,512]{1,0:T(8,128)(2,1)S(1)} %get-tuple-element.23), channel_id=1, source_target_pairs={{0,16},{16,0},{1,17},{17,1},{2,18},{18,2},{3,19},{19,3},{4,20},{20... | collective-permute-start | bytes 786440 | tf_op jit(solution)/shard_map/ppermute | solution.py:82
  24.3 32.5 %all-to-all-start.1 = ((bf16[4,48,1024]{2,1,0:T(8,128)(2,1)}), bf16[4,48,1024]{2,1,0:T(8,128)(2,1)S(1)}, u32[]{:S(2)}, u32[]{:S(2)}) async-start(bf16[4,48,1024]{2,1,0:T(8,128)(2,1)} %bitcast.5), calls=%async_computation.1 | async-start | bytes 786432 | tf_op jit(solution)/shard_map/all_to_all | solution.py:27
  45.5 25.2 %collective-permute-start.1 = (bf16[512,512]{1,0:T(8,128)(2,1)S(1)}, bf16[512,512]{1,0:T(8,128)(2,1)}, u32[]{:S(2)}, u32[]{:S(2)}) collective-permute-start(bf16[512,512]{1,0:T(8,128)(2,1)S(1)} %pad_maximum_fusion), channel_id=1, source_target_pairs={{0,1},{1,2},{2,3},{3,0},{4,5},{5,6},{6,7},{7,4},{8,9},{9,10},{10,1... | collective-permute-start | bytes 1572872 | tf_op jit(solution)/shard_map/ppermute | solution.py:85
  47.7 24.1 %collective-permute-start.2 = (bf16[512,512]{1,0:T(8,128)(2,1)S(1)}, bf16[512,512]{1,0:T(8,128)(2,1)}, u32[]{:S(2)}, u32[]{:S(2)}) collective-permute-start(bf16[512,512]{1,0:T(8,128)(2,1)S(1)} %pad_maximum_fusion), channel_id=1, source_target_pairs={{0,2},{1,3},{2,0},{3,1},{4,6},{5,7},{6,4},{7,5},{8,10},{9,11},{10,... | collective-permute-start | bytes 1572872 | tf_op jit(solution)/shard_map/ppermute | solution.py:85
  51.4 23.8 %collective-permute-start.3 = (bf16[512,512]{1,0:T(8,128)(2,1)S(1)}, bf16[512,512]{1,0:T(8,128)(2,1)}, u32[]{:S(2)}, u32[]{:S(2)}) collective-permute-start(bf16[512,512]{1,0:T(8,128)(2,1)S(1)} %pad_maximum_fusion), channel_id=1, source_target_pairs={{0,3},{1,0},{2,1},{3,2},{4,7},{5,4},{6,5},{7,6},{8,11},{9,8},{10,9... | collective-permute-start | bytes 1572872 | tf_op jit(solution)/shard_map/ppermute | solution.py:85
  57.7 23.5 %all-to-all-start.2 = ((bf16[8,48,256]{2,1,0:T(8,128)(2,1)}), bf16[8,48,256]{2,1,0:T(8,128)(2,1)S(1)}, u32[]{:S(2)}, u32[]{:S(2)}) async-start(bf16[8,48,256]{2,1,0:T(8,128)(2,1)} %bitcast.8), calls=%async_computation.2 | async-start | bytes 393216 | tf_op jit(solution)/shard_map/all_to_all | solution.py:27
  82.8 31.0 %all-to-all-start.3 = ((bf16[24,8,2048]{2,1,0:T(8,128)(2,1)}), bf16[24,8,2048]{2,1,0:T(8,128)(2,1)S(1)}, u32[]{:S(2)}, u32[]{:S(2)}) async-start(bf16[24,8,2048]{2,1,0:T(8,128)(2,1)} %fusion.1), calls=%async_computation.3 | async-start | bytes 1572864 | tf_op jit(solution)/shard_map/all_to_all | solution.py:27
  94.4 9.9 %collective-permute-start.4 = (bf16[2,192,256]{2,1,0:T(8,128)(2,1)S(1)}, bf16[2,192,256]{2,1,0:T(8,128)(2,1)S(1)}, u32[]{:S(2)}, u32[]{:S(2)}) collective-permute-start(bf16[2,192,256]{2,1,0:T(8,128)(2,1)S(1)} %bitcast.73), channel_id=1, source_target_pairs={{0,1},{1,2},{2,3},{3,0},{4,5},{5,6},{6,7},{7,4},{8,9},{9,10},{10,1... | collective-permute-start | bytes 589832 | tf_op jit(solution)/shard_map/ppermute | solution.py:110
  96.6 10.8 %collective-permute-start.5 = (bf16[2,192,256]{2,1,0:T(8,128)(2,1)S(1)}, bf16[2,192,256]{2,1,0:T(8,128)(2,1)S(1)}, u32[]{:S(2)}, u32[]{:S(2)}) collective-permute-start(bf16[2,192,256]{2,1,0:T(8,128)(2,1)S(1)} %bitcast.74), channel_id=1, source_target_pairs={{0,2},{1,3},{2,0},{3,1},{4,6},{5,7},{6,4},{7,5},{8,10},{9,11},{10,... | collective-permute-start | bytes 589832 | tf_op jit(solution)/shard_map/ppermute | solution.py:110
  100.3 9.8 %collective-permute-start.6 = (bf16[2,192,256]{2,1,0:T(8,128)(2,1)S(1)}, bf16[2,192,256]{2,1,0:T(8,128)(2,1)S(1)}, u32[]{:S(2)}, u32[]{:S(2)}) collective-permute-start(bf16[2,192,256]{2,1,0:T(8,128)(2,1)S(1)} %bitcast.75), channel_id=1, source_target_pairs={{0,3},{1,0},{2,1},{3,2},{4,7},{5,4},{6,5},{7,6},{8,11},{9,8},{10,9... | collective-permute-start | bytes 589832 | tf_op jit(solution)/shard_map/ppermute | solution.py:110
  113.8 32.8 %copy-start.5 = (bf16[768,512]{1,0:T(8,128)(2,1)S(1)}, bf16[768,512]{1,0:T(8,128)(2,1)}, u32[]{:S(2)}) copy-start(bf16[768,512]{1,0:T(8,128)(2,1)} %param.9) | copy-start | bytes 2359300
  146.6 6.0 %copy-start.2 = (f32[256,512]{1,0:T(8,128)S(1)}, f32[256,512]{1,0:T(8,128)}, u32[]{:S(2)}) copy-start(f32[256,512]{1,0:T(8,128)} %param.12) | copy-start | bytes 1572868
  146.6 6.0 %copy-start.4 = (bf16[2,256,512]{2,1,0:T(8,128)(2,1)S(1)}, bf16[2,256,512]{2,1,0:T(8,128)(2,1)}, u32[]{:S(2)}) copy-start(bf16[2,256,512]{2,1,0:T(8,128)(2,1)} %param.15) | copy-start | bytes 1572868
  146.6 6.0 %copy-start.6 = (f32[256,512]{1,0:T(8,128)S(1)}, f32[256,512]{1,0:T(8,128)}, u32[]{:S(2)}) copy-start(f32[256,512]{1,0:T(8,128)} %param.14) | copy-start | bytes 1572868
  147.1 5.5 %collective-permute-start.7 = (f32[256,512]{1,0:T(8,128)S(1)}, f32[256,512]{1,0:T(8,128)S(1)}, u32[]{:S(2)}, u32[]{:S(2)}) collective-permute-start(f32[256,512]{1,0:T(8,128)S(1)} %convolution_multiply_fusion), channel_id=1, source_target_pairs={{0,16},{16,0},{1,17},{17,1},{2,18},{18,2},{3,19},{19,3},{4,20},{20... | collective-permute-start | bytes 1572872 | tf_op jit(solution)/shard_map/ppermute | solution.py:131

commit v5 on v4

--- a/solution.py
+++ b/solution.py
@@ -31,7 +31,7 @@
     return [(i, (i + steps) % size) for i in range(size)]
 
 
-def terms_kernel(tokens_ref, gate_ref, up_ref, terms_ref):
+def terms_kernel(place_ref, tokens_ref, gate_ref, up_ref, earlier_ref, terms_ref):
     rows = tokens_ref[...]
     both = gate_ref.shape[0]
     for place, weights_ref in ((0, gate_ref), (both, up_ref)):
@@ -40,21 +40,69 @@
         ).astype(bf16)
 
 
-def gate_up_terms(tokens, gate_weights, up_weights, blocks):
-    count, width = tokens.shape
-    both = gate_weights.shape[0]
+def gate_up_terms(tokens, gate_weights, up_weights, rows, place, earlier):
+    both, width = gate_weights.shape
+    whole = pl.BlockSpec((both, width), lambda i, place: (0, 0))
     return pl.pallas_call(
         terms_kernel,
-        grid=(blocks,),
-        in_specs=[
-            pl.BlockSpec((count // blocks, width), lambda i: (i, 0)),
-            pl.BlockSpec((both, width), lambda i: (0, 0)),
-            pl.BlockSpec((both, width), lambda i: (0, 0)),
-        ],
-        out_specs=pl.BlockSpec((count // blocks, 2 * both), lambda i: (i, 0)),
-        out_shape=jax.ShapeDtypeStruct((count, 2 * both), bf16),
+        grid_spec=pltpu.PrefetchScalarGridSpec(
+            num_scalar_prefetch=1,
+            grid=(1,),
+            in_specs=[pl.BlockSpec((rows, width), lambda i, place: (place[0], 0)), whole, whole, pl.BlockSpec(memory_space=pl.ANY)],
+            out_specs=pl.BlockSpec((rows, 2 * both), lambda i, place: (0, 0)),
+        ),
+        out_shape=jax.ShapeDtypeStruct((rows, 2 * both), bf16),
+        cost_estimate=pl.CostEstimate(
+            flops=4 * rows * both * width, bytes_accessed=2 * rows * (width + 2 * both), transcendentals=0
+        ),
+        compiler_params=pltpu.CompilerParams(vmem_limit_bytes=12 * 1024 * 1024),
+    )(place, tokens, gate_weights, up_weights, earlier)
+
+
+def first_terms_kernel(place_ref, tokens_ref, gate_ref, up_ref, terms_ref, rows, gate, up, sems):
+    count = rows.shape[0]
+    begin = pl.multiple_of(place_ref[0] * count, count)
+    copies = [
+        pltpu.make_async_copy(tokens_ref.at[pl.ds(begin, count)], rows, sems.at[0]),
+        pltpu.make_async_copy(gate_ref, gate, sems.at[1]),
+        pltpu.make_async_copy(up_ref, up, sems.at[2]),
+    ]
+    for copy in copies:
+        copy.start()
+    copies[0].wait()
+    copies[1].wait()
+    both = gate.shape[0]
+    for place, weights, copy in ((0, gate, None), (both, up, copies[2])):
+        if copy is not None:
+            copy.wait()
+        terms_ref[:, place : place + both] = lax.dot_general(
+            rows[...], weights[...], (((1,), (1,)), ((), ())), preferred_element_type=f32
+        ).astype(bf16)
+
+
+def first_gate_up_terms(tokens, gate_weights, up_weights, rows, place):
+    both, width = gate_weights.shape
+    far = pl.BlockSpec(memory_space=pltpu.HBM)
+    return pl.pallas_call(
+        first_terms_kernel,
+        grid_spec=pltpu.PrefetchScalarGridSpec(
+            num_scalar_prefetch=1,
+            grid=(1,),
+            in_specs=[far, far, far],
+            out_specs=pl.BlockSpec((rows, 2 * both), lambda i, place: (0, 0)),
+            scratch_shapes=[
+                pltpu.VMEM((rows, width), bf16),
+                pltpu.VMEM((both, width), bf16),
+                pltpu.VMEM((both, width), bf16),
+                pltpu.SemaphoreType.DMA((3,)),
+            ],
+        ),
+        out_shape=jax.ShapeDtypeStruct((rows, 2 * both), bf16),
+        cost_estimate=pl.CostEstimate(
+            flops=4 * rows * both * width, bytes_accessed=2 * rows * (width + 2 * both), transcendentals=0
+        ),
         compiler_params=pltpu.CompilerParams(vmem_limit_bytes=56 * 1024 * 1024),
-    )(tokens, gate_weights, up_weights)
+    )(place, tokens, gate_weights, up_weights)
 
 
 def shards(tokens, targets, gate_weights, up_weights, means, hessian, momentum, noise):
@@ -70,11 +118,21 @@
     both = 2 * unit_count
     core = lax.axis_index("c")
 
-    terms = gate_up_terms(
-        tokens, gate_weights.reshape(both, width), up_weights.reshape(both, width), size_x
-    )
-    terms = trade(terms.reshape(size_x, -1, 2 * both), "x")
-    terms = jnp.sum(terms.astype(f32), axis=0).astype(bf16)
+    here = lax.axis_index("x")
+    gate_both, up_both = gate_weights.reshape(both, width), up_weights.reshape(both, width)
+
+    order = sorted(range(1, size_x), key=lambda k: -min(k, size_x - k)) + [0]
+    block, terms = None, 0.0
+    for k in order:
+        rows = (tokens, gate_both, up_both, token_count // size_x)
+        place = jnp.full((1,), (here + k) % size_x, jnp.int32)
+        if block is None:
+            block = first_gate_up_terms(*rows, place)
+        else:
+            block = gate_up_terms(*rows, place, block)
+        arrived = lax.ppermute(block, "x", turn(size_x, k)) if k else block
+        terms = terms + arrived.astype(f32)
+    terms = terms.astype(bf16)
 
     inv_sigma = jnp.sqrt(prior_size * (hessian + weight_decay))
     samples = (means[None] + noise.astype(f32) / inv_sigma[None]).astype(bf16)
@@ -104,7 +162,6 @@
     rows_share = rows_x // chips
     partial = partial.astype(bf16).reshape(chips, rows_share, size_x * width)
     hidden, partial = lax.optimization_barrier((hidden, partial))
-    here = lax.axis_index("x")
     rows = jnp.zeros((size_c, size_x, rows_x, unit_count), bf16)
     for k in range(size_x):
         block = hidden if k == 0 else lax.ppermute(hidden, "x", turn(size_x, k))

time: 156 us -> 155 us (level)
  starting transfers between devices: 82.6 us -> 78.3 us
  other arithmetic: 1.76 us -> 5.94 us
  waiting for transfers between devices: 23.4 us -> 20 us
  blocking collectives: 32.5 us -> 35.8 us
    all_to_all x4 -> x3, starting transfers between devices: 50.6 us -> 32 us  [trade(): return lax.all_to_all(parts, axis, 0, 0, tiled=True)]
    ppermute x0 -> x3, starting transfers between devices: none -> 12 us  [shards(): arrived = lax.ppermute(block, 'x', turn(size_x, k)) if k else block]
    all_to_all x1, blocking collectives: 32.5 us -> 35.8 us  [trade(): return lax.all_to_all(parts, axis, 0, 0, tiled=True)]
    all_to_all x4 -> x3, waiting for transfers between devices: 11.4 us -> 8.7 us  [trade(): return lax.all_to_all(parts, axis, 0, 0, tiled=True)]
    ppermute x3, starting transfers between devices: 8.41 us -> 10.5 us  [shards(): lax.ppermute(weights, 'x', turn(size_x, k))]
    convert_element_type x0 -> x1, other arithmetic: none -> 2.12 us  [shards(): terms = terms.astype(bf16)]
    ppermute x3, starting transfers between devices: 8.42 us -> 10.4 us  [shards(): block = hidden if k == 0 else lax.ppermute(hidden, 'x', turn(size_x, k))]
    ppermute x3, waiting for transfers between devices: 7.15 us -> 5.31 us  [shards(): block = hidden if k == 0 else lax.ppermute(hidden, 'x', turn(size_x, k))]
  transfers between devices with their start and end apart: 12 -> 14, of which waited for: 9 -> 9; matrix products, arithmetic and copies ran while one was open for 3% -> 5% of each run, Pallas kernels for 0% -> 1%
where the time goes in v5:
time: 155 us; the launch traced here: 154 us
  starting transfers between devices  78.3 us (51%)
  blocking collectives  35.8 us (23%)
  waiting for transfers between devices  20 us (13%)
  other arithmetic  5.94 us (4%)
  local copies, waits for them, and re-layouts  4.37 us (3%)
  matrix products  4.21 us (3%)
  Pallas kernels  4.19 us (3%)
    all_to_all x1, blocking collectives, trade(): return lax.all_to_all(parts, axis, 0, 0, tiled=True)  35.8 us
    all_to_all x3, starting transfers between devices, trade(): return lax.all_to_all(parts, axis, 0, 0, tiled=True)  32 us
    ppermute x3, starting transfers between devices, shards(): arrived = lax.ppermute(block, 'x', turn(size_x, k)) if k else block  12 us
    ppermute x3, starting transfers between devices, shards(): lax.ppermute(weights, 'x', turn(size_x, k))  10.5 us
    ppermute x3, starting transfers between devices, shards(): block = hidden if k == 0 else lax.ppermute(hidden, 'x', turn(size_x, k))  10.4 us
    ppermute x1, starting transfers between devices, shards(): lax.ppermute(lax.dynamic_index_in_dim(samples, 1 - core, 0, False), 'c',...  9.44 us
    all_to_all x3, waiting for transfers between devices, trade(): return lax.all_to_all(parts, axis, 0, 0, tiled=True)  8.7 us
    ppermute x3, waiting for transfers between devices, shards(): block = hidden if k == 0 else lax.ppermute(hidden, 'x', turn(size_x, k))  5.31 us
  transfers between devices with their start and end apart: 14, of which 9 were waited for; matrix products, arithmetic and copies ran while one was open for 5% of the time, Pallas kernels for 1%

profile of v5, /device:TPU:1, one launch (start us, length us, event | category | flops | bytes accessed | tf_op | source)
XLA Modules:
  0.0 154.0 jit_solution(15878888253695136886)
XLA Ops:
  0.7 2.7 %shard_map.103.earlier_ref = bf16[192,1024]{1,0:T(8,128)(2,1)} custom-call(s32[1]{0:T(128)} %bitcast.place_ref, bf16[768,512]{1,0:T(8,128)(2,1)} %tokens_ref.7, bf16[512,512]{1,0:T(8,128)(2,1)} %bitcast.71, bf16[512,512]{1,0:T(8,128)(2,1)} %bitcast.75), custom_call_target="tpu_custom_call" | custom-call | flops 201326592 | bytes 589824 | tf_op jit(solution)/shard_map/pallas_call | solution.py:86
  3.4 5.5 %collective-permute-start = (bf16[192,1024]{1,0:T(8,128)(2,1)}, bf16[192,1024]{1,0:T(8,128)(2,1)S(1)}, u32[]{:S(2)}, u32[]{:S(2)}) collective-permute-start(bf16[192,1024]{1,0:T(8,128)(2,1)} %shard_map.103.earlier_ref), channel_id=1, source_target_pairs={{0,2},{1,3},{2,0},{3,1},{4,6},{5,7},{6,4},{7,5},{8,10},{9,11},{10,... | collective-permute-start | bytes 1179656 | tf_op jit(solution)/shard_map/ppermute | solution.py:133
  8.9 1.0 copy-done.3
  10.4 2.2 %collective-permute-start.1 = (bf16[192,1024]{1,0:T(8,128)(2,1)S(1)}, bf16[192,1024]{1,0:T(8,128)(2,1)}, u32[]{:S(2)}, u32[]{:S(2)}) collective-permute-start(bf16[192,1024]{1,0:T(8,128)(2,1)S(1)} %shard_map.104.earlier_ref), channel_id=1, source_target_pairs={{0,1},{1,2},{2,3},{3,0},{4,5},{5,6},{6,7},{7,4},{8,9},{9,10},{10,1... | collective-permute-start | bytes 1179656 | tf_op jit(solution)/shard_map/ppermute | solution.py:133
  13.2 4.3 %collective-permute-start.2 = (bf16[192,1024]{1,0:T(8,128)(2,1)S(1)}, bf16[192,1024]{1,0:T(8,128)(2,1)}, u32[]{:S(2)}, u32[]{:S(2)}) collective-permute-start(bf16[192,1024]{1,0:T(8,128)(2,1)S(1)} %shard_map.105.earlier_ref), channel_id=1, source_target_pairs={{0,3},{1,0},{2,1},{3,2},{4,7},{5,4},{6,5},{7,6},{8,11},{9,8},{10,9... | collective-permute-start | bytes 1179656 | tf_op jit(solution)/shard_map/ppermute | solution.py:133
  17.4 1.2 multiply_sqrt_fusion
  18.6 1.4 add_convert_fusion
  20.1 9.4 %collective-permute-start.3 = (bf16[256,512]{1,0:T(8,128)(2,1)S(1)}, bf16[256,512]{1,0:T(8,128)(2,1)}, u32[]{:S(2)}, u32[]{:S(2)}) collective-permute-start(bf16[256,512]{1,0:T(8,128)(2,1)S(1)} %get-tuple-element.23), channel_id=1, source_target_pairs={{0,16},{16,0},{1,17},{17,1},{2,18},{18,2},{3,19},{19,3},{4,20},{20... | collective-permute-start | bytes 786440 | tf_op jit(solution)/shard_map/ppermute | solution.py:140
  30.8 1.0 pad_maximum_fusion
  31.8 2.1 %add_convert_fusion.1 = bf16[192,1024]{1,0:T(8,128)(2,1)} fusion(bf16[192,1024]{1,0:T(8,128)(2,1)S(1)} %shard_map.106, bf16[192,1024]{1,0:T(8,128)(2,1)} %collective-permute-done.2, bf16[192,1024]{1,0:T(8,128)(2,1)} %collective-permute-done.1, bf16[192,1024]{1,0:T(8,128)(2,1)S(1)} %collective-permute-done), kind=kLoop, calls=%fused_computation.15 | loop fusion | flops 1572864 | bytes 1966080 | tf_op jit(solution)/shard_map/convert_element_type | solution.py:135
  33.9 9.8 %all-to-all-start = ((bf16[4,48,1024]{2,1,0:T(8,128)(2,1)}), bf16[4,48,1024]{2,1,0:T(8,128)(2,1)S(1)}, u32[]{:S(2)}, u32[]{:S(2)}) async-start(bf16[4,48,1024]{2,1,0:T(8,128)(2,1)} %bitcast.8), calls=%async_computation | async-start | bytes 786432 | tf_op jit(solution)/shard_map/all_to_all | solution.py:27
  43.7 3.1 %collective-permute-start.4 = (bf16[512,512]{1,0:T(8,128)(2,1)S(1)}, bf16[512,512]{1,0:T(8,128)(2,1)}, u32[]{:S(2)}, u32[]{:S(2)}) collective-permute-start(bf16[512,512]{1,0:T(8,128)(2,1)S(1)} %pad_maximum_fusion), channel_id=1, source_target_pairs={{0,1},{1,2},{2,3},{3,0},{4,5},{5,6},{6,7},{7,4},{8,9},{9,10},{10,1... | collective-permute-start | bytes 1572872 | tf_op jit(solution)/shard_map/ppermute | solution.py:143
  46.8 3.8 %collective-permute-start.5 = (bf16[512,512]{1,0:T(8,128)(2,1)S(1)}, bf16[512,512]{1,0:T(8,128)(2,1)}, u32[]{:S(2)}, u32[]{:S(2)}) collective-permute-start(bf16[512,512]{1,0:T(8,128)(2,1)S(1)} %pad_maximum_fusion), channel_id=1, source_target_pairs={{0,2},{1,3},{2,0},{3,1},{4,6},{5,7},{6,4},{7,5},{8,10},{9,11},{10,... | collective-permute-start | bytes 1572872 | tf_op jit(solution)/shard_map/ppermute | solution.py:143
  50.7 3.6 %collective-permute-start.6 = (bf16[512,512]{1,0:T(8,128)(2,1)S(1)}, bf16[512,512]{1,0:T(8,128)(2,1)S(1)}, u32[]{:S(2)}, u32[]{:S(2)}) collective-permute-start(bf16[512,512]{1,0:T(8,128)(2,1)S(1)} %pad_maximum_fusion), channel_id=1, source_target_pairs={{0,3},{1,0},{2,1},{3,2},{4,7},{5,4},{6,5},{7,6},{8,11},{9,8},{10,9... | collective-permute-start | bytes 1572872 | tf_op jit(solution)/shard_map/ppermute | solution.py:143
  54.3 1.7 %all-to-all-done = bf16[4,48,1024]{2,1,0:T(8,128)(2,1)S(1)} async-done(((bf16[4,48,1024]{2,1,0:T(8,128)(2,1)}), bf16[4,48,1024]{2,1,0:T(8,128)(2,1)S(1)}, u32[]{:S(2)}, u32[]{:S(2)}) %all-to-all-start) | async-done | bytes 393248 | tf_op jit(solution)/shard_map/all_to_all | solution.py:27
  56.8 10.6 %all-to-all-start.1 = ((bf16[8,48,256]{2,1,0:T(8,128)(2,1)}), bf16[8,48,256]{2,1,0:T(8,128)(2,1)S(1)}, u32[]{:S(2)}, u32[]{:S(2)}) async-start(bf16[8,48,256]{2,1,0:T(8,128)(2,1)} %bitcast.11), calls=%async_computation.1 | async-start | bytes 393216 | tf_op jit(solution)/shard_map/all_to_all | solution.py:27
  67.5 1.1 constant_dynamic-update-slice_fusion.2
  68.6 1.7 %collective-permute-done.5 = bf16[512,512]{1,0:T(8,128)(2,1)} collective-permute-done((bf16[512,512]{1,0:T(8,128)(2,1)S(1)}, bf16[512,512]{1,0:T(8,128)(2,1)}, u32[]{:S(2)}, u32[]{:S(2)}) %collective-permute-start.5) | collective-permute-done | bytes 524320 | tf_op jit(solution)/shard_map/ppermute | solution.py:143
  70.2 1.1 constant_dynamic-update-slice_fusion.1
  71.3 2.0 %collective-permute-done.6 = bf16[512,512]{1,0:T(8,128)(2,1)S(1)} collective-permute-done((bf16[512,512]{1,0:T(8,128)(2,1)S(1)}, bf16[512,512]{1,0:T(8,128)(2,1)S(1)}, u32[]{:S(2)}, u32[]{:S(2)}) %collective-permute-start.6) | collective-permute-done | bytes 524320 | tf_op jit(solution)/shard_map/ppermute | solution.py:143
  73.4 4.6 %all-to-all-done.1 = bf16[8,48,256]{2,1,0:T(8,128)(2,1)S(1)} async-done(((bf16[8,48,256]{2,1,0:T(8,128)(2,1)}), bf16[8,48,256]{2,1,0:T(8,128)(2,1)S(1)}, u32[]{:S(2)}, u32[]{:S(2)}) %all-to-all-start.1) | async-done | bytes 196640 | tf_op jit(solution)/shard_map/all_to_all | solution.py:27
  78.4 1.3 fusion.1
  79.6 11.6 %all-to-all-start.2 = ((bf16[24,8,2048]{2,1,0:T(8,128)(2,1)}), bf16[24,8,2048]{2,1,0:T(8,128)(2,1)S(1)}, u32[]{:S(2)}, u32[]{:S(2)}) async-start(bf16[24,8,2048]{2,1,0:T(8,128)(2,1)} %fusion.1), calls=%async_computation.2 | async-start | bytes 1572864 | tf_op jit(solution)/shard_map/all_to_all | solution.py:27
  91.3 3.1 %collective-permute-start.7 = (bf16[2,192,256]{2,1,0:T(8,128)(2,1)S(1)}, bf16[2,192,256]{2,1,0:T(8,128)(2,1)S(1)}, u32[]{:S(2)}, u32[]{:S(2)}) collective-permute-start(bf16[2,192,256]{2,1,0:T(8,128)(2,1)S(1)} %bitcast.83), channel_id=1, source_target_pairs={{0,1},{1,2},{2,3},{3,0},{4,5},{5,6},{6,7},{7,4},{8,9},{9,10},{10,1... | collective-permute-start | bytes 589832 | tf_op jit(solution)/shard_map/ppermute | solution.py:167
  94.4 5.0 %collective-permute-start.8 = (bf16[2,192,256]{2,1,0:T(8,128)(2,1)S(1)}, bf16[2,192,256]{2,1,0:T(8,128)(2,1)S(1)}, u32[]{:S(2)}, u32[]{:S(2)}) collective-permute-start(bf16[2,192,256]{2,1,0:T(8,128)(2,1)S(1)} %bitcast.84), channel_id=1, source_target_pairs={{0,2},{1,3},{2,0},{3,1},{4,6},{5,7},{6,4},{7,5},{8,10},{9,11},{10,... | collective-permute-start | bytes 589832 | tf_op jit(solution)/shard_map/ppermute | solution.py:167
  99.4 2.3 %collective-permute-start.9 = (bf16[2,192,256]{2,1,0:T(8,128)(2,1)S(1)}, bf16[2,192,256]{2,1,0:T(8,128)(2,1)S(1)}, u32[]{:S(2)}, u32[]{:S(2)}) collective-permute-start(bf16[2,192,256]{2,1,0:T(8,128)(2,1)S(1)} %bitcast.85), channel_id=1, source_target_pairs={{0,3},{1,0},{2,1},{3,2},{4,7},{5,4},{6,5},{7,6},{8,11},{9,8},{10,9... | collective-permute-start | bytes 589832 | tf_op jit(solution)/shard_map/ppermute | solution.py:167
  101.9 4.4 %collective-permute-done.8 = bf16[2,192,256]{2,1,0:T(8,128)(2,1)S(1)} collective-permute-done((bf16[2,192,256]{2,1,0:T(8,128)(2,1)S(1)}, bf16[2,192,256]{2,1,0:T(8,128)(2,1)S(1)}, u32[]{:S(2)}, u32[]{:S(2)}) %collective-permute-start.8) | collective-permute-done | bytes 196640 | tf_op jit(solution)/shard_map/ppermute | solution.py:167
  107.3 2.5 %all-to-all-done.2 = bf16[24,8,2048]{2,1,0:T(8,128)(2,1)S(1)} async-done(((bf16[24,8,2048]{2,1,0:T(8,128)(2,1)}), bf16[24,8,2048]{2,1,0:T(8,128)(2,1)S(1)}, u32[]{:S(2)}, u32[]{:S(2)}) %all-to-all-start.2) | async-done | bytes 786464 | tf_op jit(solution)/shard_map/all_to_all | solution.py:27
  110.1 35.8 %all_to_all.20 = bf16[96,8,512]{2,1,0:T(8,128)(2,1)S(1)} all-to-all(bf16[96,8,512]{2,1,0:T(8,128)(2,1)S(1)} %bitcast.79), channel_id=1, replica_groups=mesh['y'=8,'zl'=3,'c'=2,'zh'=4,'x'=4] {'x','y','zl'}, dimensions={0} | all-to-all | bytes 1572864 | tf_op jit(solution)/shard_map/all_to_all | solution.py:27
  146.3 4.0 %collective-permute-start.10 = (f32[256,512]{1,0:T(8,128)S(1)}, f32[256,512]{1,0:T(8,128)S(1)}, u32[]{:S(2)}, u32[]{:S(2)}) collective-permute-start(f32[256,512]{1,0:T(8,128)S(1)} %convolution_multiply_fusion), channel_id=1, source_target_pairs={{0,16},{16,0},{1,17},{17,1},{2,18},{18,2},{3,19},{19,3},{4,20},{20... | collective-permute-start | bytes 1572872 | tf_op jit(solution)/shard_map/ppermute | solution.py:188
  150.4 1.5 collective-permute-done.10
  151.9 2.1 %divide_subtract_fusion = (f32[256,512]{1,0:T(8,128)}, f32[256,512]{1,0:T(8,128)}, f32[256,512]{1,0:T(8,128)}) fusion(f32[256,512]{1,0:T(8,128)S(1)} %copy-done.5, f32[256,512]{1,0:T(8,128)S(1)} %collective-permute-done.10, f32[256,512]{1,0:T(8,128)S(1)} %copy-done.8, f32[256,512]{1,0:T(8,128)S(1)} %copy-done.4, bf16[2,256,512]{2,1,0:T(8,128)(2,1)S(1)} %copy-done.6, ...), kind=kOutput, calls=%fused_computation.24 | convolution fusion | flops 206962688 | bytes 6160392 | tf_op jit(solution)/shard_map/dot_general | solution.py:186
  (49 shorter events, 5.4 us)
Async XLA Ops:
  0.6 8.2 %copy-start = (bf16[768,512]{1,0:T(8,128)(2,1)S(1)}, bf16[768,512]{1,0:T(8,128)(2,1)}, u32[]{:S(2)}) copy-start(bf16[768,512]{1,0:T(8,128)(2,1)} %tokens_ref.7) | copy-start | bytes 2359300
  0.6 8.2 %copy-start.1 = (bf16[2,256,512]{2,1,0:T(8,128)(2,1)S(1)}, bf16[2,256,512]{2,1,0:T(8,128)(2,1)}, u32[]{:S(2)}) copy-start(bf16[2,256,512]{2,1,0:T(8,128)(2,1)} %param.10) | copy-start | bytes 1572868
  0.7 8.2 %copy-start.2 = (bf16[2,256,512]{2,1,0:T(8,128)(2,1)S(1)}, bf16[2,256,512]{2,1,0:T(8,128)(2,1)}, u32[]{:S(2)}) copy-start(bf16[2,256,512]{2,1,0:T(8,128)(2,1)} %param.11) | copy-start | bytes 1572868
  3.4 28.4 %collective-permute-start = (bf16[192,1024]{1,0:T(8,128)(2,1)}, bf16[192,1024]{1,0:T(8,128)(2,1)S(1)}, u32[]{:S(2)}, u32[]{:S(2)}) collective-permute-start(bf16[192,1024]{1,0:T(8,128)(2,1)} %shard_map.103.earlier_ref), channel_id=1, source_target_pairs={{0,2},{1,3},{2,0},{3,1},{4,6},{5,7},{6,4},{7,5},{8,10},{9,11},{10,... | collective-permute-start | bytes 1179656 | tf_op jit(solution)/shard_map/ppermute | solution.py:133
  8.9 1.0 copy-start.3
  10.4 21.4 %collective-permute-start.1 = (bf16[192,1024]{1,0:T(8,128)(2,1)S(1)}, bf16[192,1024]{1,0:T(8,128)(2,1)}, u32[]{:S(2)}, u32[]{:S(2)}) collective-permute-start(bf16[192,1024]{1,0:T(8,128)(2,1)S(1)} %shard_map.104.earlier_ref), channel_id=1, source_target_pairs={{0,1},{1,2},{2,3},{3,0},{4,5},{5,6},{6,7},{7,4},{8,9},{9,10},{10,1... | collective-permute-start | bytes 1179656 | tf_op jit(solution)/shard_map/ppermute | solution.py:133
  13.2 18.6 %collective-permute-start.2 = (bf16[192,1024]{1,0:T(8,128)(2,1)S(1)}, bf16[192,1024]{1,0:T(8,128)(2,1)}, u32[]{:S(2)}, u32[]{:S(2)}) collective-permute-start(bf16[192,1024]{1,0:T(8,128)(2,1)S(1)} %shard_map.105.earlier_ref), channel_id=1, source_target_pairs={{0,3},{1,0},{2,1},{3,2},{4,7},{5,4},{6,5},{7,6},{8,11},{9,8},{10,9... | collective-permute-start | bytes 1179656 | tf_op jit(solution)/shard_map/ppermute | solution.py:133
  20.1 10.7 %collective-permute-start.3 = (bf16[256,512]{1,0:T(8,128)(2,1)S(1)}, bf16[256,512]{1,0:T(8,128)(2,1)}, u32[]{:S(2)}, u32[]{:S(2)}) collective-permute-start(bf16[256,512]{1,0:T(8,128)(2,1)S(1)} %get-tuple-element.23), channel_id=1, source_target_pairs={{0,16},{16,0},{1,17},{17,1},{2,18},{18,2},{3,19},{19,3},{4,20},{20... | collective-permute-start | bytes 786440 | tf_op jit(solution)/shard_map/ppermute | solution.py:140
  33.9 22.0 %all-to-all-start = ((bf16[4,48,1024]{2,1,0:T(8,128)(2,1)}), bf16[4,48,1024]{2,1,0:T(8,128)(2,1)S(1)}, u32[]{:S(2)}, u32[]{:S(2)}) async-start(bf16[4,48,1024]{2,1,0:T(8,128)(2,1)} %bitcast.8), calls=%async_computation | async-start | bytes 786432 | tf_op jit(solution)/shard_map/all_to_all | solution.py:27
  43.7 23.7 %collective-permute-start.4 = (bf16[512,512]{1,0:T(8,128)(2,1)S(1)}, bf16[512,512]{1,0:T(8,128)(2,1)}, u32[]{:S(2)}, u32[]{:S(2)}) collective-permute-start(bf16[512,512]{1,0:T(8,128)(2,1)S(1)} %pad_maximum_fusion), channel_id=1, source_target_pairs={{0,1},{1,2},{2,3},{3,0},{4,5},{5,6},{6,7},{7,4},{8,9},{9,10},{10,1... | collective-permute-start | bytes 1572872 | tf_op jit(solution)/shard_map/ppermute | solution.py:143
  46.8 23.4 %collective-permute-start.5 = (bf16[512,512]{1,0:T(8,128)(2,1)S(1)}, bf16[512,512]{1,0:T(8,128)(2,1)}, u32[]{:S(2)}, u32[]{:S(2)}) collective-permute-start(bf16[512,512]{1,0:T(8,128)(2,1)S(1)} %pad_maximum_fusion), channel_id=1, source_target_pairs={{0,2},{1,3},{2,0},{3,1},{4,6},{5,7},{6,4},{7,5},{8,10},{9,11},{10,... | collective-permute-start | bytes 1572872 | tf_op jit(solution)/shard_map/ppermute | solution.py:143
  50.7 22.7 %collective-permute-start.6 = (bf16[512,512]{1,0:T(8,128)(2,1)S(1)}, bf16[512,512]{1,0:T(8,128)(2,1)S(1)}, u32[]{:S(2)}, u32[]{:S(2)}) collective-permute-start(bf16[512,512]{1,0:T(8,128)(2,1)S(1)} %pad_maximum_fusion), channel_id=1, source_target_pairs={{0,3},{1,0},{2,1},{3,2},{4,7},{5,4},{6,5},{7,6},{8,11},{9,8},{10,9... | collective-permute-start | bytes 1572872 | tf_op jit(solution)/shard_map/ppermute | solution.py:143
  56.8 21.2 %all-to-all-start.1 = ((bf16[8,48,256]{2,1,0:T(8,128)(2,1)}), bf16[8,48,256]{2,1,0:T(8,128)(2,1)S(1)}, u32[]{:S(2)}, u32[]{:S(2)}) async-start(bf16[8,48,256]{2,1,0:T(8,128)(2,1)} %bitcast.11), calls=%async_computation.1 | async-start | bytes 393216 | tf_op jit(solution)/shard_map/all_to_all | solution.py:27
  79.6 30.1 %all-to-all-start.2 = ((bf16[24,8,2048]{2,1,0:T(8,128)(2,1)}), bf16[24,8,2048]{2,1,0:T(8,128)(2,1)S(1)}, u32[]{:S(2)}, u32[]{:S(2)}) async-start(bf16[24,8,2048]{2,1,0:T(8,128)(2,1)} %fusion.1), calls=%async_computation.2 | async-start | bytes 1572864 | tf_op jit(solution)/shard_map/all_to_all | solution.py:27
  91.3 10.5 %collective-permute-start.7 = (bf16[2,192,256]{2,1,0:T(8,128)(2,1)S(1)}, bf16[2,192,256]{2,1,0:T(8,128)(2,1)S(1)}, u32[]{:S(2)}, u32[]{:S(2)}) collective-permute-start(bf16[2,192,256]{2,1,0:T(8,128)(2,1)S(1)} %bitcast.83), channel_id=1, source_target_pairs={{0,1},{1,2},{2,3},{3,0},{4,5},{5,6},{6,7},{7,4},{8,9},{9,10},{10,1... | collective-permute-start | bytes 589832 | tf_op jit(solution)/shard_map/ppermute | solution.py:167
  94.4 11.9 %collective-permute-start.8 = (bf16[2,192,256]{2,1,0:T(8,128)(2,1)S(1)}, bf16[2,192,256]{2,1,0:T(8,128)(2,1)S(1)}, u32[]{:S(2)}, u32[]{:S(2)}) collective-permute-start(bf16[2,192,256]{2,1,0:T(8,128)(2,1)S(1)} %bitcast.84), channel_id=1, source_target_pairs={{0,2},{1,3},{2,0},{3,1},{4,6},{5,7},{6,4},{7,5},{8,10},{9,11},{10,... | collective-permute-start | bytes 589832 | tf_op jit(solution)/shard_map/ppermute | solution.py:167
  99.4 7.8 %collective-permute-start.9 = (bf16[2,192,256]{2,1,0:T(8,128)(2,1)S(1)}, bf16[2,192,256]{2,1,0:T(8,128)(2,1)S(1)}, u32[]{:S(2)}, u32[]{:S(2)}) collective-permute-start(bf16[2,192,256]{2,1,0:T(8,128)(2,1)S(1)} %bitcast.85), channel_id=1, source_target_pairs={{0,3},{1,0},{2,1},{3,2},{4,7},{5,4},{6,5},{7,6},{8,11},{9,8},{10,9... | collective-permute-start | bytes 589832 | tf_op jit(solution)/shard_map/ppermute | solution.py:167
  107.3 38.6 %copy-start.7 = (bf16[768,512]{1,0:T(8,128)(2,1)S(1)}, bf16[768,512]{1,0:T(8,128)(2,1)}, u32[]{:S(2)}) copy-start(bf16[768,512]{1,0:T(8,128)(2,1)} %param.9) | copy-start | bytes 2359300
  110.0 41.9 %copy-start.4 = (f32[256,512]{1,0:T(8,128)S(1)}, f32[256,512]{1,0:T(8,128)}, u32[]{:S(2)}) copy-start(f32[256,512]{1,0:T(8,128)} %param.13) | copy-start | bytes 1572868
  110.0 41.9 %copy-start.5 = (f32[256,512]{1,0:T(8,128)S(1)}, f32[256,512]{1,0:T(8,128)}, u32[]{:S(2)}) copy-start(f32[256,512]{1,0:T(8,128)} %param.12) | copy-start | bytes 1572868
  110.0 41.9 %copy-start.6 = (bf16[2,256,512]{2,1,0:T(8,128)(2,1)S(1)}, bf16[2,256,512]{2,1,0:T(8,128)(2,1)}, u32[]{:S(2)}) copy-start(bf16[2,256,512]{2,1,0:T(8,128)(2,1)} %param.15) | copy-start | bytes 1572868
  110.0 41.9 %copy-start.8 = (f32[256,512]{1,0:T(8,128)S(1)}, f32[256,512]{1,0:T(8,128)}, u32[]{:S(2)}) copy-start(f32[256,512]{1,0:T(8,128)} %param.14) | copy-start | bytes 1572868
  146.3 5.6 %collective-permute-start.10 = (f32[256,512]{1,0:T(8,128)S(1)}, f32[256,512]{1,0:T(8,128)S(1)}, u32[]{:S(2)}, u32[]{:S(2)}) collective-permute-start(f32[256,512]{1,0:T(8,128)S(1)} %convolution_multiply_fusion), channel_id=1, source_target_pairs={{0,16},{16,0},{1,17},{17,1},{2,18},{18,2},{3,19},{19,3},{4,20},{20... | collective-permute-start | bytes 1572872 | tf_op jit(solution)/shard_map/ppermute | solution.py:188

commit v6 on v4

--- a/solution.py
+++ b/solution.py
@@ -71,7 +71,7 @@
     core = lax.axis_index("c")
 
     terms = gate_up_terms(
-        tokens, gate_weights.reshape(both, width), up_weights.reshape(both, width), size_x
+        tokens, gate_weights.reshape(both, width), up_weights.reshape(both, width), 2
     )
     terms = trade(terms.reshape(size_x, -1, 2 * both), "x")
     terms = jnp.sum(terms.astype(f32), axis=0).astype(bf16)
@@ -105,19 +105,20 @@
     partial = partial.astype(bf16).reshape(chips, rows_share, size_x * width)
     hidden, partial = lax.optimization_barrier((hidden, partial))
     here = lax.axis_index("x")
+    near = {k: lax.ppermute(hidden, "x", turn(size_x, k)) for k in (1, size_x - 1)}
+    partial, near = lax.optimization_barrier((trade(partial, ("y", "zl")), near))
+    out_share = (jnp.sum(partial.astype(f32), axis=0) * scale_out).astype(bf16)
+    out_share = out_share.reshape(rows_share, size_x, width)
+    out_share, hidden = lax.optimization_barrier((out_share, hidden))
     rows = jnp.zeros((size_c, size_x, rows_x, unit_count), bf16)
     for k in range(size_x):
-        block = hidden if k == 0 else lax.ppermute(hidden, "x", turn(size_x, k))
+        block = near.get(k, hidden)
+        if k and k not in near:
+            block = lax.ppermute(hidden, "x", turn(size_x, k))
         rows = lax.dynamic_update_slice(rows, block[:, None], (0, (here - k) % size_x, 0, 0))
     rows = rows.reshape(size_c, token_count, unit_count)
     rows_own = lax.dynamic_index_in_dim(rows, core, 0, False)
     rows_other = lax.dynamic_index_in_dim(rows, 1 - core, 0, False)
-
-    partial, rows_own, rows_other = lax.optimization_barrier(
-        (trade(partial, ("y", "zl")), rows_own, rows_other)
-    )
-    out_share = (jnp.sum(partial.astype(f32), axis=0) * scale_out).astype(bf16)
-    out_share = out_share.reshape(rows_share, size_x, width)
     sends = jnp.stack(
         [lax.dynamic_index_in_dim(out_share, (here - place) % size_x, 1, False) for place in range(size_x)]
     )

time: 156 us -> 157 us (level)
  blocking collectives: 32.5 us -> 0 us
  waiting for transfers between devices: 23.4 us -> 45.7 us
  starting transfers between devices: 82.6 us -> 93.6 us
    all_to_all x1 -> x0, blocking collectives: 32.5 us -> none  [trade(): return lax.all_to_all(parts, axis, 0, 0, tiled=True)]
    all_to_all x4 -> x5, waiting for transfers between devices: 11.4 us -> 28.1 us  [trade(): return lax.all_to_all(parts, axis, 0, 0, tiled=True)]
    all_to_all x4 -> x5, starting transfers between devices: 50.6 us -> 59.1 us  [trade(): return lax.all_to_all(parts, axis, 0, 0, tiled=True)]
    ppermute x3, waiting for transfers between devices: 7.15 us -> 12.8 us  [the longest x1 8.69 us: shards(): block = lax.ppermute(hidden, 'x', turn(size_x, k))]
    ppermute x3, starting transfers between devices: 8.42 us -> 10.9 us  [the longest x2 6.49 us: shards(): lax.ppermute(hidden, 'x', turn(size_x, k))]
  transfers between devices with their start and end apart: 12 -> 13, of which waited for: 9 -> 10; matrix products, arithmetic and copies ran while one was open for 3% -> 3% of each run, Pallas kernels for 0% -> 0%
where the time goes in v6:
time: 157 us; the launch traced here: 156 us
  starting transfers between devices  93.6 us (60%)
  waiting for transfers between devices  45.7 us (29%)
  matrix products  5.44 us (3%)
  local copies, waits for them, and re-layouts  5.23 us (3%)
  Pallas kernels  3.49 us (2%)
  other arithmetic  1.76 us (1%)
    all_to_all x5, starting transfers between devices, trade(): return lax.all_to_all(parts, axis, 0, 0, tiled=True)  59.1 us
    all_to_all x5, waiting for transfers between devices, trade(): return lax.all_to_all(parts, axis, 0, 0, tiled=True)  28.1 us
    ppermute x1, starting transfers between devices, shards(): lax.ppermute(lax.dynamic_index_in_dim(samples, 1 - core, 0, False), 'c',...  11.2 us
    ppermute x1, waiting for transfers between devices, shards(): block = lax.ppermute(hidden, 'x', turn(size_x, k))  8.69 us
    ppermute x3, starting transfers between devices, shards(): lax.ppermute(weights, 'x', turn(size_x, k))  8.41 us
    ppermute x2, starting transfers between devices, shards(): lax.ppermute(hidden, 'x', turn(size_x, k))  6.49 us
    ppermute x1, starting transfers between devices, shards(): block = lax.ppermute(hidden, 'x', turn(size_x, k))  4.41 us
    ppermute x2, waiting for transfers between devices, shards(): lax.ppermute(hidden, 'x', turn(size_x, k))  4.07 us
  transfers between devices with their start and end apart: 13, of which 10 were waited for; matrix products, arithmetic and copies ran while one was open for 3% of the time, Pallas kernels for 0%

profile of v6, /device:TPU:1, one launch (start us, length us, event | category | flops | bytes accessed | tf_op | source)
XLA Modules:
  0.0 156.2 jit_solution(11011146615155864515)
XLA Ops:
  0.6 3.5 %shard_map.103 = bf16[768,1024]{1,0:T(8,128)(2,1)} custom-call(bf16[768,512]{1,0:T(8,128)(2,1)} %tokens_ref.1, bf16[512,512]{1,0:T(8,128)(2,1)} %bitcast.79, bf16[512,512]{1,0:T(8,128)(2,1)} %bitcast.80), custom_call_target="tpu_custom_call" | custom-call | tf_op jit(solution)/shard_map/pallas_call | solution.py:46
  4.1 5.0 %all-to-all-start = ((bf16[4,192,1024]{2,1,0:T(8,128)(2,1)}), bf16[4,192,1024]{2,1,0:T(8,128)(2,1)S(1)}, u32[]{:S(2)}, u32[]{:S(2)}) async-start(bf16[4,192,1024]{2,1,0:T(8,128)(2,1)} %bitcast.70), calls=%async_computation | async-start | bytes 3145728 | tf_op jit(solution)/shard_map/all_to_all | solution.py:27
  9.5 11.2 %collective-permute-start = (bf16[256,512]{1,0:T(8,128)(2,1)S(1)}, bf16[256,512]{1,0:T(8,128)(2,1)S(1)}, u32[]{:S(2)}, u32[]{:S(2)}) collective-permute-start(bf16[256,512]{1,0:T(8,128)(2,1)S(1)} %get-tuple-element.25), channel_id=1, source_target_pairs={{0,16},{16,0},{1,17},{17,1},{2,18},{18,2},{3,19},{19,3},{4,20},{20... | collective-permute-start | bytes 786440 | tf_op jit(solution)/shard_map/ppermute | solution.py:82
  20.7 1.1 collective-permute-done
  21.9 1.1 reduce_sum.30
  23.0 21.2 %all-to-all-start.1 = ((bf16[4,48,1024]{2,1,0:T(8,128)(2,1)}), bf16[4,48,1024]{2,1,0:T(8,128)(2,1)S(1)}, u32[]{:S(2)}, u32[]{:S(2)}) async-start(bf16[4,48,1024]{2,1,0:T(8,128)(2,1)} %bitcast.5), calls=%async_computation.1 | async-start | bytes 786432 | tf_op jit(solution)/shard_map/all_to_all | solution.py:27
  44.3 2.2 %collective-permute-start.1 = (bf16[512,512]{1,0:T(8,128)(2,1)S(1)}, bf16[512,512]{1,0:T(8,128)(2,1)}, u32[]{:S(2)}, u32[]{:S(2)}) collective-permute-start(bf16[512,512]{1,0:T(8,128)(2,1)S(1)} %pad_maximum_fusion), channel_id=1, source_target_pairs={{0,1},{1,2},{2,3},{3,0},{4,5},{5,6},{6,7},{7,4},{8,9},{9,10},{10,1... | collective-permute-start | bytes 1572872 | tf_op jit(solution)/shard_map/ppermute | solution.py:85
  46.5 3.7 %collective-permute-start.2 = (bf16[512,512]{1,0:T(8,128)(2,1)S(1)}, bf16[512,512]{1,0:T(8,128)(2,1)}, u32[]{:S(2)}, u32[]{:S(2)}) collective-permute-start(bf16[512,512]{1,0:T(8,128)(2,1)S(1)} %pad_maximum_fusion), channel_id=1, source_target_pairs={{0,2},{1,3},{2,0},{3,1},{4,6},{5,7},{6,4},{7,5},{8,10},{9,11},{10,... | collective-permute-start | bytes 1572872 | tf_op jit(solution)/shard_map/ppermute | solution.py:85
  50.2 2.5 %collective-permute-start.3 = (bf16[512,512]{1,0:T(8,128)(2,1)S(1)}, bf16[512,512]{1,0:T(8,128)(2,1)}, u32[]{:S(2)}, u32[]{:S(2)}) collective-permute-start(bf16[512,512]{1,0:T(8,128)(2,1)S(1)} %pad_maximum_fusion), channel_id=1, source_target_pairs={{0,3},{1,0},{2,1},{3,2},{4,7},{5,4},{6,5},{7,6},{8,11},{9,8},{10,9... | collective-permute-start | bytes 1572872 | tf_op jit(solution)/shard_map/ppermute | solution.py:85
  52.7 2.9 %all-to-all-done.1 = bf16[4,48,1024]{2,1,0:T(8,128)(2,1)S(1)} async-done(((bf16[4,48,1024]{2,1,0:T(8,128)(2,1)}), bf16[4,48,1024]{2,1,0:T(8,128)(2,1)S(1)}, u32[]{:S(2)}, u32[]{:S(2)}) %all-to-all-start.1) | async-done | bytes 393248 | tf_op jit(solution)/shard_map/all_to_all | solution.py:27
  56.4 12.9 %all-to-all-start.2 = ((bf16[8,48,256]{2,1,0:T(8,128)(2,1)}), bf16[8,48,256]{2,1,0:T(8,128)(2,1)S(1)}, u32[]{:S(2)}, u32[]{:S(2)}) async-start(bf16[8,48,256]{2,1,0:T(8,128)(2,1)} %bitcast.8), calls=%async_computation.2 | async-start | bytes 393216 | tf_op jit(solution)/shard_map/all_to_all | solution.py:27
  69.4 1.1 constant_dynamic-update-slice_fusion.2
  70.5 1.1 constant_dynamic-update-slice_fusion.1
  71.7 2.3 %collective-permute-done.3 = bf16[512,512]{1,0:T(8,128)(2,1)} collective-permute-done((bf16[512,512]{1,0:T(8,128)(2,1)S(1)}, bf16[512,512]{1,0:T(8,128)(2,1)}, u32[]{:S(2)}, u32[]{:S(2)}) %collective-permute-start.3) | collective-permute-done | bytes 524320 | tf_op jit(solution)/shard_map/ppermute | solution.py:85
  73.9 1.1 constant_dynamic-update-slice_fusion
  75.0 4.9 %all-to-all-done.2 = bf16[8,48,256]{2,1,0:T(8,128)(2,1)S(1)} async-done(((bf16[8,48,256]{2,1,0:T(8,128)(2,1)}), bf16[8,48,256]{2,1,0:T(8,128)(2,1)S(1)}, u32[]{:S(2)}, u32[]{:S(2)}) %all-to-all-start.2) | async-done | bytes 196640 | tf_op jit(solution)/shard_map/all_to_all | solution.py:27
  80.3 1.3 fusion.1
  81.5 11.9 %all-to-all-start.3 = ((bf16[24,8,2048]{2,1,0:T(8,128)(2,1)}), bf16[24,8,2048]{2,1,0:T(8,128)(2,1)S(1)}, u32[]{:S(2)}, u32[]{:S(2)}) async-start(bf16[24,8,2048]{2,1,0:T(8,128)(2,1)} %fusion.1), calls=%async_computation.3 | async-start | bytes 1572864 | tf_op jit(solution)/shard_map/all_to_all | solution.py:27
  93.5 2.2 %collective-permute-start.4 = (bf16[2,192,256]{2,1,0:T(8,128)(2,1)S(1)}, bf16[2,192,256]{2,1,0:T(8,128)(2,1)S(1)}, u32[]{:S(2)}, u32[]{:S(2)}) collective-permute-start(bf16[2,192,256]{2,1,0:T(8,128)(2,1)S(1)} %bitcast.73), channel_id=1, source_target_pairs={{0,1},{1,2},{2,3},{3,0},{4,5},{5,6},{6,7},{7,4},{8,9},{9,10},{10,1... | collective-permute-start | bytes 589832 | tf_op jit(solution)/shard_map/ppermute | solution.py:108
  95.7 4.3 %collective-permute-start.5 = (bf16[2,192,256]{2,1,0:T(8,128)(2,1)S(1)}, bf16[2,192,256]{2,1,0:T(8,128)(2,1)S(1)}, u32[]{:S(2)}, u32[]{:S(2)}) collective-permute-start(bf16[2,192,256]{2,1,0:T(8,128)(2,1)S(1)} %bitcast.74), channel_id=1, source_target_pairs={{0,3},{1,0},{2,1},{3,2},{4,7},{5,4},{6,5},{7,6},{8,11},{9,8},{10,9... | collective-permute-start | bytes 589832 | tf_op jit(solution)/shard_map/ppermute | solution.py:108
  100.1 3.1 %collective-permute-done.4 = bf16[2,192,256]{2,1,0:T(8,128)(2,1)S(1)} collective-permute-done((bf16[2,192,256]{2,1,0:T(8,128)(2,1)S(1)}, bf16[2,192,256]{2,1,0:T(8,128)(2,1)S(1)}, u32[]{:S(2)}, u32[]{:S(2)}) %collective-permute-start.4) | collective-permute-done | bytes 196640 | tf_op jit(solution)/shard_map/ppermute | solution.py:108
  103.2 0.9 collective-permute-done.5
  104.1 10.3 %all-to-all-done.3 = bf16[24,8,2048]{2,1,0:T(8,128)(2,1)S(1)} async-done(((bf16[24,8,2048]{2,1,0:T(8,128)(2,1)}), bf16[24,8,2048]{2,1,0:T(8,128)(2,1)S(1)}, u32[]{:S(2)}, u32[]{:S(2)}) %all-to-all-start.3) | async-done | bytes 786464 | tf_op jit(solution)/shard_map/all_to_all | solution.py:27
  114.6 0.9 broadcast_in_dim.35
  115.6 8.0 %all-to-all-start.4 = ((bf16[96,8,512]{2,1,0:T(8,128)(2,1)}), bf16[96,8,512]{2,1,0:T(8,128)(2,1)S(1)}, u32[]{:S(2)}, u32[]{:S(2)}) async-start(bf16[96,8,512]{2,1,0:T(8,128)(2,1)} %bitcast.27), calls=%async_computation.4 | async-start | bytes 1572864 | tf_op jit(solution)/shard_map/all_to_all | solution.py:27
  123.6 4.4 %collective-permute-start.6 = (bf16[2,192,256]{2,1,0:T(8,128)(2,1)S(1)}, bf16[2,192,256]{2,1,0:T(8,128)(2,1)S(1)}, u32[]{:S(2)}, u32[]{:S(2)}) collective-permute-start(bf16[2,192,256]{2,1,0:T(8,128)(2,1)S(1)} %bitcast.75), channel_id=1, source_target_pairs={{0,2},{1,3},{2,0},{3,1},{4,6},{5,7},{6,4},{7,5},{8,10},{9,11},{10,... | collective-permute-start | bytes 589832 | tf_op jit(solution)/shard_map/ppermute | solution.py:117
  128.1 8.7 %collective-permute-done.6 = bf16[2,192,256]{2,1,0:T(8,128)(2,1)S(1)} collective-permute-done((bf16[2,192,256]{2,1,0:T(8,128)(2,1)S(1)}, bf16[2,192,256]{2,1,0:T(8,128)(2,1)S(1)}, u32[]{:S(2)}, u32[]{:S(2)}) %collective-permute-start.6) | collective-permute-done | bytes 196640 | tf_op jit(solution)/shard_map/ppermute | solution.py:117
  136.9 10.0 %all-to-all-done.4 = bf16[96,8,512]{2,1,0:T(8,128)(2,1)S(1)} async-done(((bf16[96,8,512]{2,1,0:T(8,128)(2,1)}), bf16[96,8,512]{2,1,0:T(8,128)(2,1)S(1)}, u32[]{:S(2)}, u32[]{:S(2)}) %all-to-all-start.4) | async-done | bytes 786464 | tf_op jit(solution)/shard_map/all_to_all | solution.py:27
  146.9 1.7 %convolution_multiply_fusion = f32[256,512]{1,0:T(8,128)S(1)} fusion(bf16[2,768,256]{2,1,0:T(8,128)(2,1)S(1)} %bitcast.77, s32[]{:T(128)S(6)} %select_n.60, bf16[768,512]{1,0:T(8,128)(2,1)} %param.9, bf16[96,8,512]{2,1,0:T(8,128)(2,1)S(1)} %all-to-all-done.4), kind=kOutput, calls=%fused_computation.7 | convolution fusion | flops 203423744 | bytes 2490372 | tf_op jit(solution)/shard_map/dot_general | solution.py:130
  148.6 4.0 %collective-permute-start.7 = (f32[256,512]{1,0:T(8,128)S(1)}, f32[256,512]{1,0:T(8,128)S(1)}, u32[]{:S(2)}, u32[]{:S(2)}) collective-permute-start(f32[256,512]{1,0:T(8,128)S(1)} %convolution_multiply_fusion), channel_id=1, source_target_pairs={{0,16},{16,0},{1,17},{17,1},{2,18},{18,2},{3,19},{19,3},{4,20},{20... | collective-permute-start | bytes 1572872 | tf_op jit(solution)/shard_map/ppermute | solution.py:132
  152.6 1.5 collective-permute-done.7
  154.1 2.1 %divide_subtract_fusion = (f32[256,512]{1,0:T(8,128)}, f32[256,512]{1,0:T(8,128)}, f32[256,512]{1,0:T(8,128)}) fusion(f32[256,512]{1,0:T(8,128)S(1)} %copy-done.2, f32[256,512]{1,0:T(8,128)S(1)} %collective-permute-done.7, f32[256,512]{1,0:T(8,128)S(1)} %copy-done.6, f32[256,512]{1,0:T(8,128)S(1)} %copy-done, bf16[2,256,512]{2,1,0:T(8,128)(2,1)S(1)} %copy-done.4, ...), kind=kOutput, calls=%fused_computation.23 | convolution fusion | flops 206962688 | bytes 6161920 | tf_op jit(solution)/shard_map/dot_general | solution.py:130
  (38 shorter events, 2.0 us)
Async XLA Ops:
  4.1 5.0 %copy-start = (f32[256,512]{1,0:T(8,128)S(1)}, f32[256,512]{1,0:T(8,128)}, u32[]{:S(2)}) copy-start(f32[256,512]{1,0:T(8,128)} %param.13) | copy-start | bytes 1572868
  4.1 5.2 %copy-start.1 = (f32[256,512]{1,0:T(8,128)S(1)}, f32[256,512]{1,0:T(8,128)}, u32[]{:S(2)}) copy-start(f32[256,512]{1,0:T(8,128)} %param.12) | copy-start | bytes 1572868
  4.1 5.2 %copy-start.3 = (bf16[2,256,512]{2,1,0:T(8,128)(2,1)S(1)}, bf16[2,256,512]{2,1,0:T(8,128)(2,1)}, u32[]{:S(2)}) copy-start(bf16[2,256,512]{2,1,0:T(8,128)(2,1)} %param.15) | copy-start | bytes 1572868
  4.1 17.8 %all-to-all-start = ((bf16[4,192,1024]{2,1,0:T(8,128)(2,1)}), bf16[4,192,1024]{2,1,0:T(8,128)(2,1)S(1)}, u32[]{:S(2)}, u32[]{:S(2)}) async-start(bf16[4,192,1024]{2,1,0:T(8,128)(2,1)} %bitcast.70), calls=%async_computation | async-start | bytes 3145728 | tf_op jit(solution)/shard_map/all_to_all | solution.py:27
  9.5 12.3 %collective-permute-start = (bf16[256,512]{1,0:T(8,128)(2,1)S(1)}, bf16[256,512]{1,0:T(8,128)(2,1)S(1)}, u32[]{:S(2)}, u32[]{:S(2)}) collective-permute-start(bf16[256,512]{1,0:T(8,128)(2,1)S(1)} %get-tuple-element.25), channel_id=1, source_target_pairs={{0,16},{16,0},{1,17},{17,1},{2,18},{18,2},{3,19},{19,3},{4,20},{20... | collective-permute-start | bytes 786440 | tf_op jit(solution)/shard_map/ppermute | solution.py:82
  23.0 32.5 %all-to-all-start.1 = ((bf16[4,48,1024]{2,1,0:T(8,128)(2,1)}), bf16[4,48,1024]{2,1,0:T(8,128)(2,1)S(1)}, u32[]{:S(2)}, u32[]{:S(2)}) async-start(bf16[4,48,1024]{2,1,0:T(8,128)(2,1)} %bitcast.5), calls=%async_computation.1 | async-start | bytes 786432 | tf_op jit(solution)/shard_map/all_to_all | solution.py:27
  44.3 25.1 %collective-permute-start.1 = (bf16[512,512]{1,0:T(8,128)(2,1)S(1)}, bf16[512,512]{1,0:T(8,128)(2,1)}, u32[]{:S(2)}, u32[]{:S(2)}) collective-permute-start(bf16[512,512]{1,0:T(8,128)(2,1)S(1)} %pad_maximum_fusion), channel_id=1, source_target_pairs={{0,1},{1,2},{2,3},{3,0},{4,5},{5,6},{6,7},{7,4},{8,9},{9,10},{10,1... | collective-permute-start | bytes 1572872 | tf_op jit(solution)/shard_map/ppermute | solution.py:85
  46.5 24.1 %collective-permute-start.2 = (bf16[512,512]{1,0:T(8,128)(2,1)S(1)}, bf16[512,512]{1,0:T(8,128)(2,1)}, u32[]{:S(2)}, u32[]{:S(2)}) collective-permute-start(bf16[512,512]{1,0:T(8,128)(2,1)S(1)} %pad_maximum_fusion), channel_id=1, source_target_pairs={{0,2},{1,3},{2,0},{3,1},{4,6},{5,7},{6,4},{7,5},{8,10},{9,11},{10,... | collective-permute-start | bytes 1572872 | tf_op jit(solution)/shard_map/ppermute | solution.py:85
  50.2 23.8 %collective-permute-start.3 = (bf16[512,512]{1,0:T(8,128)(2,1)S(1)}, bf16[512,512]{1,0:T(8,128)(2,1)}, u32[]{:S(2)}, u32[]{:S(2)}) collective-permute-start(bf16[512,512]{1,0:T(8,128)(2,1)S(1)} %pad_maximum_fusion), channel_id=1, source_target_pairs={{0,3},{1,0},{2,1},{3,2},{4,7},{5,4},{6,5},{7,6},{8,11},{9,8},{10,9... | collective-permute-start | bytes 1572872 | tf_op jit(solution)/shard_map/ppermute | solution.py:85
  56.4 23.5 %all-to-all-start.2 = ((bf16[8,48,256]{2,1,0:T(8,128)(2,1)}), bf16[8,48,256]{2,1,0:T(8,128)(2,1)S(1)}, u32[]{:S(2)}, u32[]{:S(2)}) async-start(bf16[8,48,256]{2,1,0:T(8,128)(2,1)} %bitcast.8), calls=%async_computation.2 | async-start | bytes 393216 | tf_op jit(solution)/shard_map/all_to_all | solution.py:27
  81.5 32.9 %all-to-all-start.3 = ((bf16[24,8,2048]{2,1,0:T(8,128)(2,1)}), bf16[24,8,2048]{2,1,0:T(8,128)(2,1)S(1)}, u32[]{:S(2)}, u32[]{:S(2)}) async-start(bf16[24,8,2048]{2,1,0:T(8,128)(2,1)} %fusion.1), calls=%async_computation.3 | async-start | bytes 1572864 | tf_op jit(solution)/shard_map/all_to_all | solution.py:27
  93.5 9.7 %collective-permute-start.4 = (bf16[2,192,256]{2,1,0:T(8,128)(2,1)S(1)}, bf16[2,192,256]{2,1,0:T(8,128)(2,1)S(1)}, u32[]{:S(2)}, u32[]{:S(2)}) collective-permute-start(bf16[2,192,256]{2,1,0:T(8,128)(2,1)S(1)} %bitcast.73), channel_id=1, source_target_pairs={{0,1},{1,2},{2,3},{3,0},{4,5},{5,6},{6,7},{7,4},{8,9},{9,10},{10,1... | collective-permute-start | bytes 589832 | tf_op jit(solution)/shard_map/ppermute | solution.py:108
  95.7 8.5 %collective-permute-start.5 = (bf16[2,192,256]{2,1,0:T(8,128)(2,1)S(1)}, bf16[2,192,256]{2,1,0:T(8,128)(2,1)S(1)}, u32[]{:S(2)}, u32[]{:S(2)}) collective-permute-start(bf16[2,192,256]{2,1,0:T(8,128)(2,1)S(1)} %bitcast.74), channel_id=1, source_target_pairs={{0,3},{1,0},{2,1},{3,2},{4,7},{5,4},{6,5},{7,6},{8,11},{9,8},{10,9... | collective-permute-start | bytes 589832 | tf_op jit(solution)/shard_map/ppermute | solution.py:108
  115.6 31.3 %all-to-all-start.4 = ((bf16[96,8,512]{2,1,0:T(8,128)(2,1)}), bf16[96,8,512]{2,1,0:T(8,128)(2,1)S(1)}, u32[]{:S(2)}, u32[]{:S(2)}) async-start(bf16[96,8,512]{2,1,0:T(8,128)(2,1)} %bitcast.27), calls=%async_computation.4 | async-start | bytes 1572864 | tf_op jit(solution)/shard_map/all_to_all | solution.py:27
  123.6 13.2 %collective-permute-start.6 = (bf16[2,192,256]{2,1,0:T(8,128)(2,1)S(1)}, bf16[2,192,256]{2,1,0:T(8,128)(2,1)S(1)}, u32[]{:S(2)}, u32[]{:S(2)}) collective-permute-start(bf16[2,192,256]{2,1,0:T(8,128)(2,1)S(1)} %bitcast.75), channel_id=1, source_target_pairs={{0,2},{1,3},{2,0},{3,1},{4,6},{5,7},{6,4},{7,5},{8,10},{9,11},{10,... | collective-permute-start | bytes 589832 | tf_op jit(solution)/shard_map/ppermute | solution.py:117
  136.8 17.2 %copy-start.2 = (f32[256,512]{1,0:T(8,128)S(1)}, f32[256,512]{1,0:T(8,128)}, u32[]{:S(2)}) copy-start(f32[256,512]{1,0:T(8,128)} %param.12) | copy-start | bytes 1572868
  136.8 17.2 %copy-start.4 = (bf16[2,256,512]{2,1,0:T(8,128)(2,1)S(1)}, bf16[2,256,512]{2,1,0:T(8,128)(2,1)}, u32[]{:S(2)}) copy-start(bf16[2,256,512]{2,1,0:T(8,128)(2,1)} %param.15) | copy-start | bytes 1572868
  146.9 7.2 %copy-start.5 = (bf16[768,512]{1,0:T(8,128)(2,1)S(1)}, bf16[768,512]{1,0:T(8,128)(2,1)}, u32[]{:S(2)}) copy-start(bf16[768,512]{1,0:T(8,128)(2,1)} %param.9) | copy-start | bytes 2359300
  146.9 7.2 %copy-start.6 = (f32[256,512]{1,0:T(8,128)S(1)}, f32[256,512]{1,0:T(8,128)}, u32[]{:S(2)}) copy-start(f32[256,512]{1,0:T(8,128)} %param.14) | copy-start | bytes 1572868
  148.6 5.5 %collective-permute-start.7 = (f32[256,512]{1,0:T(8,128)S(1)}, f32[256,512]{1,0:T(8,128)S(1)}, u32[]{:S(2)}, u32[]{:S(2)}) collective-permute-start(f32[256,512]{1,0:T(8,128)S(1)} %convolution_multiply_fusion), channel_id=1, source_target_pairs={{0,16},{16,0},{1,17},{17,1},{2,18},{18,2},{3,19},{19,3},{4,20},{20... | collective-permute-start | bytes 1572872 | tf_op jit(solution)/shard_map/ppermute | solution.py:132

commit v7 on v4

--- a/solution.py
+++ b/solution.py
@@ -71,7 +71,7 @@
     core = lax.axis_index("c")
 
     terms = gate_up_terms(
-        tokens, gate_weights.reshape(both, width), up_weights.reshape(both, width), size_x
+        tokens, gate_weights.reshape(both, width), up_weights.reshape(both, width), 2
     )
     terms = trade(terms.reshape(size_x, -1, 2 * both), "x")
     terms = jnp.sum(terms.astype(f32), axis=0).astype(bf16)
@@ -128,19 +128,20 @@
     def grad(hidden_part):
         return jnp.dot(hidden_part.T, d_out, preferred_element_type=f32) * scale_out
 
-    grad_other = lax.ppermute(grad(rows_other), "c", SWAP)
+    grad_sent = grad(rows_other)
     grad_own = grad(rows_own)
     noise_own = lax.dynamic_index_in_dim(noise, core, 0, False).astype(f32)
-    noise_other = lax.dynamic_index_in_dim(noise, 1 - core, 0, False).astype(f32)
-    grad_mean = 0.5 * (grad_own + grad_other)
-    curv_mean = 0.5 * (grad_own * noise_own + grad_other * noise_other) * inv_sigma
-    new_momentum = beta_one * momentum + (1.0 - beta_one) * grad_mean
+    noise_other = lax.dynamic_index_in_dim(noise, 1 - core, 0, False).astype(f32) * (0.5 * inv_sigma)
+    momentum_own = beta_one * momentum + (1.0 - beta_one) * 0.5 * grad_own
+    curv_own = grad_own * noise_own * (0.5 * inv_sigma)
+    spread_gain = 0.5 * (1.0 - beta_two) ** 2 / (hessian + weight_decay)
+    grad_other, momentum_own, curv_own, noise_other, spread_gain = lax.optimization_barrier(
+        (lax.ppermute(grad_sent, "c", SWAP), momentum_own, curv_own, noise_other, spread_gain)
+    )
+    new_momentum = momentum_own + (1.0 - beta_one) * 0.5 * grad_other
+    curv_mean = curv_own + grad_other * noise_other
     spread = hessian - curv_mean
-    new_hessian = (
-        beta_two * hessian
-        + (1.0 - beta_two) * curv_mean
-        + 0.5 * (1.0 - beta_two) ** 2 * spread * spread / (hessian + weight_decay)
-    )
+    new_hessian = beta_two * hessian + (1.0 - beta_two) * curv_mean + spread_gain * spread * spread
     new_means = means - step_rate * (new_momentum + weight_decay * means) / (
         new_hessian + weight_decay
     )

time: 156 us -> 154 us (0.987)
  other arithmetic: 1.76 us -> 4.04 us
    unnamed x17 -> x15, local copies, waits for them, and re-layouts: 2.3 us -> 3.33 us
  transfers between devices with their start and end apart: 12 -> 12, of which waited for: 9 -> 8; matrix products, arithmetic and copies ran while one was open for 3% -> 5% of each run, Pallas kernels for 0% -> 0%
where the time goes in v7:
time: 154 us; the launch traced here: 153 us
  starting transfers between devices  82.3 us (53%)
  blocking collectives  31.1 us (20%)
  waiting for transfers between devices  23.1 us (15%)
  local copies, waits for them, and re-layouts  5.43 us (4%)
  other arithmetic  4.04 us (3%)
  Pallas kernels  3.48 us (2%)
  matrix products  2.8 us (2%)
    all_to_all x4, starting transfers between devices, trade(): return lax.all_to_all(parts, axis, 0, 0, tiled=True)  50.3 us
    all_to_all x1, blocking collectives, trade(): return lax.all_to_all(parts, axis, 0, 0, tiled=True)  31.1 us
    all_to_all x4, waiting for transfers between devices, trade(): return lax.all_to_all(parts, axis, 0, 0, tiled=True)  12 us
    ppermute x1, starting transfers between devices, shards(): lax.ppermute(lax.dynamic_index_in_dim(samples, 1 - core, 0, False), 'c',...  11.2 us
    ppermute x3, starting transfers between devices, shards(): block = hidden if k == 0 else lax.ppermute(hidden, 'x', turn(size_x, k))  8.41 us
    ppermute x3, starting transfers between devices, shards(): lax.ppermute(weights, 'x', turn(size_x, k))  8.41 us
    ppermute x3, waiting for transfers between devices, shards(): block = hidden if k == 0 else lax.ppermute(hidden, 'x', turn(size_x, k))  7.64 us
    ppermute x1, starting transfers between devices, shards(): lax.ppermute(grad_sent, 'c', SWAP)  3.98 us
  transfers between devices with their start and end apart: 12, of which 8 were waited for; matrix products, arithmetic and copies ran while one was open for 5% of the time, Pallas kernels for 0%

profile of v7, /device:TPU:1, one launch (start us, length us, event | category | flops | bytes accessed | tf_op | source)
XLA Modules:
  0.0 153.3 jit_solution(8430537449460421946)
XLA Ops:
  0.6 3.5 %shard_map.103 = bf16[768,1024]{1,0:T(8,128)(2,1)} custom-call(bf16[768,512]{1,0:T(8,128)(2,1)} %tokens_ref.1, bf16[512,512]{1,0:T(8,128)(2,1)} %bitcast.75, bf16[512,512]{1,0:T(8,128)(2,1)} %bitcast.76), custom_call_target="tpu_custom_call" | custom-call | tf_op jit(solution)/shard_map/pallas_call | solution.py:46
  4.1 5.0 %all-to-all-start = ((bf16[4,192,1024]{2,1,0:T(8,128)(2,1)}), bf16[4,192,1024]{2,1,0:T(8,128)(2,1)S(1)}, u32[]{:S(2)}, u32[]{:S(2)}) async-start(bf16[4,192,1024]{2,1,0:T(8,128)(2,1)} %bitcast.66), calls=%async_computation | async-start | bytes 3145728 | tf_op jit(solution)/shard_map/all_to_all | solution.py:27
  9.5 11.2 %collective-permute-start = (bf16[256,512]{1,0:T(8,128)(2,1)S(1)}, bf16[256,512]{1,0:T(8,128)(2,1)S(1)}, u32[]{:S(2)}, u32[]{:S(2)}) collective-permute-start(bf16[256,512]{1,0:T(8,128)(2,1)S(1)} %get-tuple-element.37), channel_id=1, source_target_pairs={{0,16},{16,0},{1,17},{17,1},{2,18},{18,2},{3,19},{19,3},{4,20},{20... | collective-permute-start | bytes 786440 | tf_op jit(solution)/shard_map/ppermute | solution.py:82
  20.7 1.1 collective-permute-done
  21.8 0.8 pad_maximum_fusion
  22.7 1.1 reduce_sum.30
  23.8 20.4 %all-to-all-start.1 = ((bf16[4,48,1024]{2,1,0:T(8,128)(2,1)}), bf16[4,48,1024]{2,1,0:T(8,128)(2,1)S(1)}, u32[]{:S(2)}, u32[]{:S(2)}) async-start(bf16[4,48,1024]{2,1,0:T(8,128)(2,1)} %bitcast.5), calls=%async_computation.1 | async-start | bytes 786432 | tf_op jit(solution)/shard_map/all_to_all | solution.py:27
  44.3 2.2 %collective-permute-start.1 = (bf16[512,512]{1,0:T(8,128)(2,1)}, bf16[512,512]{1,0:T(8,128)(2,1)}, u32[]{:S(2)}, u32[]{:S(2)}) collective-permute-start(bf16[512,512]{1,0:T(8,128)(2,1)} %pad_maximum_fusion), channel_id=1, source_target_pairs={{0,1},{1,2},{2,3},{3,0},{4,5},{5,6},{6,7},{7,4},{8,9},{9,10},{10,1... | collective-permute-start | bytes 1572872 | tf_op jit(solution)/shard_map/ppermute | solution.py:85
  46.4 3.7 %collective-permute-start.2 = (bf16[512,512]{1,0:T(8,128)(2,1)}, bf16[512,512]{1,0:T(8,128)(2,1)}, u32[]{:S(2)}, u32[]{:S(2)}) collective-permute-start(bf16[512,512]{1,0:T(8,128)(2,1)} %pad_maximum_fusion), channel_id=1, source_target_pairs={{0,2},{1,3},{2,0},{3,1},{4,6},{5,7},{6,4},{7,5},{8,10},{9,11},{10,... | collective-permute-start | bytes 1572872 | tf_op jit(solution)/shard_map/ppermute | solution.py:85
  50.2 2.5 %collective-permute-start.3 = (bf16[512,512]{1,0:T(8,128)(2,1)}, bf16[512,512]{1,0:T(8,128)(2,1)}, u32[]{:S(2)}, u32[]{:S(2)}) collective-permute-start(bf16[512,512]{1,0:T(8,128)(2,1)} %pad_maximum_fusion), channel_id=1, source_target_pairs={{0,3},{1,0},{2,1},{3,2},{4,7},{5,4},{6,5},{7,6},{8,11},{9,8},{10,9... | collective-permute-start | bytes 1572872 | tf_op jit(solution)/shard_map/ppermute | solution.py:85
  52.7 2.9 %all-to-all-done.1 = bf16[4,48,1024]{2,1,0:T(8,128)(2,1)S(1)} async-done(((bf16[4,48,1024]{2,1,0:T(8,128)(2,1)}), bf16[4,48,1024]{2,1,0:T(8,128)(2,1)S(1)}, u32[]{:S(2)}, u32[]{:S(2)}) %all-to-all-start.1) | async-done | bytes 393248 | tf_op jit(solution)/shard_map/all_to_all | solution.py:27
  55.7 0.7 broadcast_in_dim.14
  56.4 12.9 %all-to-all-start.2 = ((bf16[8,48,256]{2,1,0:T(8,128)(2,1)}), bf16[8,48,256]{2,1,0:T(8,128)(2,1)S(1)}, u32[]{:S(2)}, u32[]{:S(2)}) async-start(bf16[8,48,256]{2,1,0:T(8,128)(2,1)} %bitcast.8), calls=%async_computation.2 | async-start | bytes 393216 | tf_op jit(solution)/shard_map/all_to_all | solution.py:27
  69.3 1.1 constant_dynamic-update-slice_fusion.3
  70.5 1.1 constant_dynamic-update-slice_fusion.2
  71.6 1.1 constant_dynamic-update-slice_fusion.1
  72.7 1.5 %collective-permute-done.3 = bf16[512,512]{1,0:T(8,128)(2,1)} collective-permute-done((bf16[512,512]{1,0:T(8,128)(2,1)}, bf16[512,512]{1,0:T(8,128)(2,1)}, u32[]{:S(2)}, u32[]{:S(2)}) %collective-permute-start.3) | collective-permute-done | bytes 524320 | tf_op jit(solution)/shard_map/ppermute | solution.py:85
  74.2 1.1 constant_dynamic-update-slice_fusion
  75.3 4.5 %all-to-all-done.2 = bf16[8,48,256]{2,1,0:T(8,128)(2,1)S(1)} async-done(((bf16[8,48,256]{2,1,0:T(8,128)(2,1)}), bf16[8,48,256]{2,1,0:T(8,128)(2,1)S(1)}, u32[]{:S(2)}, u32[]{:S(2)}) %all-to-all-start.2) | async-done | bytes 196640 | tf_op jit(solution)/shard_map/all_to_all | solution.py:27
  80.3 1.3 fusion.1
  81.5 11.9 %all-to-all-start.3 = ((bf16[24,8,2048]{2,1,0:T(8,128)(2,1)}), bf16[24,8,2048]{2,1,0:T(8,128)(2,1)S(1)}, u32[]{:S(2)}, u32[]{:S(2)}) async-start(bf16[24,8,2048]{2,1,0:T(8,128)(2,1)} %fusion.1), calls=%async_computation.3 | async-start | bytes 1572864 | tf_op jit(solution)/shard_map/all_to_all | solution.py:27
  93.5 2.2 %collective-permute-start.4 = (bf16[2,192,256]{2,1,0:T(8,128)(2,1)S(1)}, bf16[2,192,256]{2,1,0:T(8,128)(2,1)S(1)}, u32[]{:S(2)}, u32[]{:S(2)}) collective-permute-start(bf16[2,192,256]{2,1,0:T(8,128)(2,1)S(1)} %bitcast.71), channel_id=1, source_target_pairs={{0,1},{1,2},{2,3},{3,0},{4,5},{5,6},{6,7},{7,4},{8,9},{9,10},{10,1... | collective-permute-start | bytes 589832 | tf_op jit(solution)/shard_map/ppermute | solution.py:110
  95.7 3.7 %collective-permute-start.5 = (bf16[2,192,256]{2,1,0:T(8,128)(2,1)S(1)}, bf16[2,192,256]{2,1,0:T(8,128)(2,1)S(1)}, u32[]{:S(2)}, u32[]{:S(2)}) collective-permute-start(bf16[2,192,256]{2,1,0:T(8,128)(2,1)S(1)} %bitcast.72), channel_id=1, source_target_pairs={{0,2},{1,3},{2,0},{3,1},{4,6},{5,7},{6,4},{7,5},{8,10},{9,11},{10,... | collective-permute-start | bytes 589832 | tf_op jit(solution)/shard_map/ppermute | solution.py:110
  99.4 2.5 %collective-permute-start.6 = (bf16[2,192,256]{2,1,0:T(8,128)(2,1)S(1)}, bf16[2,192,256]{2,1,0:T(8,128)(2,1)S(1)}, u32[]{:S(2)}, u32[]{:S(2)}) collective-permute-start(bf16[2,192,256]{2,1,0:T(8,128)(2,1)S(1)} %bitcast.73), channel_id=1, source_target_pairs={{0,3},{1,0},{2,1},{3,2},{4,7},{5,4},{6,5},{7,6},{8,11},{9,8},{10,9... | collective-permute-start | bytes 589832 | tf_op jit(solution)/shard_map/ppermute | solution.py:110
  102.1 5.4 %collective-permute-done.4 = bf16[2,192,256]{2,1,0:T(8,128)(2,1)S(1)} collective-permute-done((bf16[2,192,256]{2,1,0:T(8,128)(2,1)S(1)}, bf16[2,192,256]{2,1,0:T(8,128)(2,1)S(1)}, u32[]{:S(2)}, u32[]{:S(2)}) %collective-permute-start.4) | collective-permute-done | bytes 196640 | tf_op jit(solution)/shard_map/ppermute | solution.py:110
  107.5 2.2 %collective-permute-done.6 = bf16[2,192,256]{2,1,0:T(8,128)(2,1)S(1)} collective-permute-done((bf16[2,192,256]{2,1,0:T(8,128)(2,1)S(1)}, bf16[2,192,256]{2,1,0:T(8,128)(2,1)S(1)}, u32[]{:S(2)}, u32[]{:S(2)}) %collective-permute-start.6) | collective-permute-done | bytes 196640 | tf_op jit(solution)/shard_map/ppermute | solution.py:110
  109.8 4.6 %all-to-all-done.3 = bf16[24,8,2048]{2,1,0:T(8,128)(2,1)S(1)} async-done(((bf16[24,8,2048]{2,1,0:T(8,128)(2,1)}), bf16[24,8,2048]{2,1,0:T(8,128)(2,1)S(1)}, u32[]{:S(2)}, u32[]{:S(2)}) %all-to-all-start.3) | async-done | bytes 786464 | tf_op jit(solution)/shard_map/all_to_all | solution.py:27
  114.7 31.1 %all_to_all.25 = bf16[96,8,512]{2,1,0:T(8,128)(2,1)S(1)} all-to-all(bf16[96,8,512]{2,1,0:T(8,128)(2,1)S(1)} %bitcast.67), channel_id=1, replica_groups=mesh['y'=8,'zl'=3,'c'=2,'zh'=4,'x'=4] {'x','y','zl'}, dimensions={0} | all-to-all | bytes 1572864 | tf_op jit(solution)/shard_map/all_to_all | solution.py:27
  146.3 4.0 %collective-permute-start.7 = (f32[256,512]{1,0:T(8,128)S(1)}, f32[256,512]{1,0:T(8,128)S(1)}, u32[]{:S(2)}, u32[]{:S(2)}) collective-permute-start(f32[256,512]{1,0:T(8,128)S(1)} %convolution_multiply_fusion), channel_id=1, source_target_pairs={{0,16},{16,0},{1,17},{17,1},{2,18},{18,2},{3,19},{19,3},{4,20},{20... | collective-permute-start | bytes 1572872 | tf_op jit(solution)/shard_map/ppermute | solution.py:139
  150.3 0.7 convert_multiply_fusion
  151.0 0.8 collective-permute-done.7
  151.8 1.5 divide_subtract_fusion
  (37 shorter events, 1.8 us)
Async XLA Ops:
  4.1 5.0 %copy-start = (f32[256,512]{1,0:T(8,128)S(1)}, f32[256,512]{1,0:T(8,128)}, u32[]{:S(2)}) copy-start(f32[256,512]{1,0:T(8,128)} %param.13) | copy-start | bytes 1572868
  4.1 5.2 %copy-start.1 = (f32[256,512]{1,0:T(8,128)S(1)}, f32[256,512]{1,0:T(8,128)}, u32[]{:S(2)}) copy-start(f32[256,512]{1,0:T(8,128)} %param.12) | copy-start | bytes 1572868
  4.1 5.2 %copy-start.2 = (bf16[2,256,512]{2,1,0:T(8,128)(2,1)S(1)}, bf16[2,256,512]{2,1,0:T(8,128)(2,1)}, u32[]{:S(2)}) copy-start(bf16[2,256,512]{2,1,0:T(8,128)(2,1)} %param.15) | copy-start | bytes 1572868
  4.1 18.6 %all-to-all-start = ((bf16[4,192,1024]{2,1,0:T(8,128)(2,1)}), bf16[4,192,1024]{2,1,0:T(8,128)(2,1)S(1)}, u32[]{:S(2)}, u32[]{:S(2)}) async-start(bf16[4,192,1024]{2,1,0:T(8,128)(2,1)} %bitcast.66), calls=%async_computation | async-start | bytes 3145728 | tf_op jit(solution)/shard_map/all_to_all | solution.py:27
  9.5 12.3 %collective-permute-start = (bf16[256,512]{1,0:T(8,128)(2,1)S(1)}, bf16[256,512]{1,0:T(8,128)(2,1)S(1)}, u32[]{:S(2)}, u32[]{:S(2)}) collective-permute-start(bf16[256,512]{1,0:T(8,128)(2,1)S(1)} %get-tuple-element.37), channel_id=1, source_target_pairs={{0,16},{16,0},{1,17},{17,1},{2,18},{18,2},{3,19},{19,3},{4,20},{20... | collective-permute-start | bytes 786440 | tf_op jit(solution)/shard_map/ppermute | solution.py:82
  23.8 31.7 %all-to-all-start.1 = ((bf16[4,48,1024]{2,1,0:T(8,128)(2,1)}), bf16[4,48,1024]{2,1,0:T(8,128)(2,1)S(1)}, u32[]{:S(2)}, u32[]{:S(2)}) async-start(bf16[4,48,1024]{2,1,0:T(8,128)(2,1)} %bitcast.5), calls=%async_computation.1 | async-start | bytes 786432 | tf_op jit(solution)/shard_map/all_to_all | solution.py:27
  44.3 26.2 %collective-permute-start.1 = (bf16[512,512]{1,0:T(8,128)(2,1)}, bf16[512,512]{1,0:T(8,128)(2,1)}, u32[]{:S(2)}, u32[]{:S(2)}) collective-permute-start(bf16[512,512]{1,0:T(8,128)(2,1)} %pad_maximum_fusion), channel_id=1, source_target_pairs={{0,1},{1,2},{2,3},{3,0},{4,5},{5,6},{6,7},{7,4},{8,9},{9,10},{10,1... | collective-permute-start | bytes 1572872 | tf_op jit(solution)/shard_map/ppermute | solution.py:85
  46.4 25.1 %collective-permute-start.2 = (bf16[512,512]{1,0:T(8,128)(2,1)}, bf16[512,512]{1,0:T(8,128)(2,1)}, u32[]{:S(2)}, u32[]{:S(2)}) collective-permute-start(bf16[512,512]{1,0:T(8,128)(2,1)} %pad_maximum_fusion), channel_id=1, source_target_pairs={{0,2},{1,3},{2,0},{3,1},{4,6},{5,7},{6,4},{7,5},{8,10},{9,11},{10,... | collective-permute-start | bytes 1572872 | tf_op jit(solution)/shard_map/ppermute | solution.py:85
  50.2 24.1 %collective-permute-start.3 = (bf16[512,512]{1,0:T(8,128)(2,1)}, bf16[512,512]{1,0:T(8,128)(2,1)}, u32[]{:S(2)}, u32[]{:S(2)}) collective-permute-start(bf16[512,512]{1,0:T(8,128)(2,1)} %pad_maximum_fusion), channel_id=1, source_target_pairs={{0,3},{1,0},{2,1},{3,2},{4,7},{5,4},{6,5},{7,6},{8,11},{9,8},{10,9... | collective-permute-start | bytes 1572872 | tf_op jit(solution)/shard_map/ppermute | solution.py:85
  56.4 23.5 %all-to-all-start.2 = ((bf16[8,48,256]{2,1,0:T(8,128)(2,1)}), bf16[8,48,256]{2,1,0:T(8,128)(2,1)S(1)}, u32[]{:S(2)}, u32[]{:S(2)}) async-start(bf16[8,48,256]{2,1,0:T(8,128)(2,1)} %bitcast.8), calls=%async_computation.2 | async-start | bytes 393216 | tf_op jit(solution)/shard_map/all_to_all | solution.py:27
  81.5 32.9 %all-to-all-start.3 = ((bf16[24,8,2048]{2,1,0:T(8,128)(2,1)}), bf16[24,8,2048]{2,1,0:T(8,128)(2,1)S(1)}, u32[]{:S(2)}, u32[]{:S(2)}) async-start(bf16[24,8,2048]{2,1,0:T(8,128)(2,1)} %fusion.1), calls=%async_computation.3 | async-start | bytes 1572864 | tf_op jit(solution)/shard_map/all_to_all | solution.py:27
  93.5 13.9 %collective-permute-start.4 = (bf16[2,192,256]{2,1,0:T(8,128)(2,1)S(1)}, bf16[2,192,256]{2,1,0:T(8,128)(2,1)S(1)}, u32[]{:S(2)}, u32[]{:S(2)}) collective-permute-start(bf16[2,192,256]{2,1,0:T(8,128)(2,1)S(1)} %bitcast.71), channel_id=1, source_target_pairs={{0,1},{1,2},{2,3},{3,0},{4,5},{5,6},{6,7},{7,4},{8,9},{9,10},{10,1... | collective-permute-start | bytes 589832 | tf_op jit(solution)/shard_map/ppermute | solution.py:110
  95.7 11.8 %collective-permute-start.5 = (bf16[2,192,256]{2,1,0:T(8,128)(2,1)S(1)}, bf16[2,192,256]{2,1,0:T(8,128)(2,1)S(1)}, u32[]{:S(2)}, u32[]{:S(2)}) collective-permute-start(bf16[2,192,256]{2,1,0:T(8,128)(2,1)S(1)} %bitcast.72), channel_id=1, source_target_pairs={{0,2},{1,3},{2,0},{3,1},{4,6},{5,7},{6,4},{7,5},{8,10},{9,11},{10,... | collective-permute-start | bytes 589832 | tf_op jit(solution)/shard_map/ppermute | solution.py:110
  99.4 10.3 %collective-permute-start.6 = (bf16[2,192,256]{2,1,0:T(8,128)(2,1)S(1)}, bf16[2,192,256]{2,1,0:T(8,128)(2,1)S(1)}, u32[]{:S(2)}, u32[]{:S(2)}) collective-permute-start(bf16[2,192,256]{2,1,0:T(8,128)(2,1)S(1)} %bitcast.73), channel_id=1, source_target_pairs={{0,3},{1,0},{2,1},{3,2},{4,7},{5,4},{6,5},{7,6},{8,11},{9,8},{10,9... | collective-permute-start | bytes 589832 | tf_op jit(solution)/shard_map/ppermute | solution.py:110
  114.4 31.4 %copy-start.4 = (bf16[768,512]{1,0:T(8,128)(2,1)S(1)}, bf16[768,512]{1,0:T(8,128)(2,1)}, u32[]{:S(2)}) copy-start(bf16[768,512]{1,0:T(8,128)(2,1)} %param.9) | copy-start | bytes 2359300
  145.8 4.5 %copy-start.3 = (bf16[2,256,512]{2,1,0:T(8,128)(2,1)S(1)}, bf16[2,256,512]{2,1,0:T(8,128)(2,1)}, u32[]{:S(2)}) copy-start(bf16[2,256,512]{2,1,0:T(8,128)(2,1)} %param.15) | copy-start | bytes 1572868
  145.8 4.5 %copy-start.5 = (f32[256,512]{1,0:T(8,128)S(1)}, f32[256,512]{1,0:T(8,128)}, u32[]{:S(2)}) copy-start(f32[256,512]{1,0:T(8,128)} %param.14) | copy-start | bytes 1572868
  146.3 5.5 %collective-permute-start.7 = (f32[256,512]{1,0:T(8,128)S(1)}, f32[256,512]{1,0:T(8,128)S(1)}, u32[]{:S(2)}, u32[]{:S(2)}) collective-permute-start(f32[256,512]{1,0:T(8,128)S(1)} %convolution_multiply_fusion), channel_id=1, source_target_pairs={{0,16},{16,0},{1,17},{17,1},{2,18},{18,2},{3,19},{19,3},{4,20},{20... | collective-permute-start | bytes 1572872 | tf_op jit(solution)/shard_map/ppermute | solution.py:139

commit v8 on v7

--- a/solution.py
+++ b/solution.py
@@ -29,6 +29,10 @@
 
 def turn(size, steps):
     return [(i, (i + steps) % size) for i in range(size)]
+
+
+def farthest_first(size):
+    return sorted(range(1, size), key=lambda k: -min(k, size - k))
 
 
 def terms_kernel(tokens_ref, gate_ref, up_ref, terms_ref):
@@ -82,7 +86,10 @@
     weights_other = lax.ppermute(lax.dynamic_index_in_dim(samples, 1 - core, 0, False), "c", SWAP)
     weights = jnp.concatenate([weights_own, weights_other], axis=0)
     terms, weights = lax.optimization_barrier((terms, weights))
-    wide = jnp.concatenate([weights] + [lax.ppermute(weights, "x", turn(size_x, k)) for k in range(1, size_x)], axis=1)
+    slots = [0] + farthest_first(size_x)
+    wide = jnp.concatenate(
+        [lax.ppermute(weights, "x", turn(size_x, k)) if k else weights for k in slots], axis=1
+    )
 
     terms = trade(terms.reshape(size_zh, -1, 2 * both), "zh")
     sums = jnp.sum(terms.astype(f32), axis=0) * scale_in
@@ -118,8 +125,12 @@
     )
     out_share = (jnp.sum(partial.astype(f32), axis=0) * scale_out).astype(bf16)
     out_share = out_share.reshape(rows_share, size_x, width)
+    slot_of = jnp.asarray([slots.index(k) for k in range(size_x)], jnp.int32)
     sends = jnp.stack(
-        [lax.dynamic_index_in_dim(out_share, (here - place) % size_x, 1, False) for place in range(size_x)]
+        [
+            lax.dynamic_index_in_dim(out_share, slot_of[(here - place) % size_x], 1, False)
+            for place in range(size_x)
+        ]
     )
     sends = jnp.broadcast_to(sends[:, None], (size_x, chips, rows_share, width))
     out = trade(sends.reshape(-1, rows_share, width), ("x", "y", "zl")).reshape(token_count, width)
@@ -136,8 +147,9 @@
     curv_own = grad_own * noise_own * (0.5 * inv_sigma)
     spread_gain = 0.5 * (1.0 - beta_two) ** 2 / (hessian + weight_decay)
     grad_other, momentum_own, curv_own, noise_other, spread_gain = lax.optimization_barrier(
-        (lax.ppermute(grad_sent, "c", SWAP), momentum_own, curv_own, noise_other, spread_gain)
+        (lax.ppermute(grad_sent.astype(bf16), "c", SWAP), momentum_own, curv_own, noise_other, spread_gain)
     )
+    grad_other = grad_other.astype(f32)
     new_momentum = momentum_own + (1.0 - beta_one) * 0.5 * grad_other
     curv_mean = curv_own + grad_other * noise_other
     spread = hessian - curv_mean

time: 154 us -> 162 us (1.052)
  between operations: 1.02 us -> 8.89 us
  waiting for transfers between devices: 23.1 us -> 17.8 us
  blocking collectives: 31.1 us -> 35.5 us
    all_to_all x4, waiting for transfers between devices: 12 us -> 7.11 us  [trade(): return lax.all_to_all(parts, axis, 0, 0, tiled=True)]
    all_to_all x1, blocking collectives: 31.1 us -> 35.5 us  [trade(): return lax.all_to_all(parts, axis, 0, 0, tiled=True)]
  transfers between devices with their start and end apart: 12 -> 12, of which waited for: 8 -> 7; matrix products, arithmetic and copies ran while one was open for 5% -> 6% of each run, Pallas kernels for 0% -> 0%
where the time goes in v8:
time: 162 us; the launch traced here: 161 us
  starting transfers between devices  81.7 us (50%)
  blocking collectives  35.5 us (22%)
  waiting for transfers between devices  17.8 us (11%)
  between operations  8.89 us (5%)
  local copies, waits for them, and re-layouts  6.11 us (4%)
  other arithmetic  5.02 us (3%)
  Pallas kernels  3.49 us (2%)
  matrix products  2.79 us (2%)
    all_to_all x4, starting transfers between devices, trade(): return lax.all_to_all(parts, axis, 0, 0, tiled=True)  49.4 us
    all_to_all x1, blocking collectives, trade(): return lax.all_to_all(parts, axis, 0, 0, tiled=True)  35.5 us
    ppermute x1, starting transfers between devices, shards(): lax.ppermute(lax.dynamic_index_in_dim(samples, 1 - core, 0, False), 'c',...  11.2 us
    ppermute x3, starting transfers between devices, shards(): lax.ppermute(weights, 'x', turn(size_x, k))  8.76 us
    ppermute x3, starting transfers between devices, shards(): block = hidden if k == 0 else lax.ppermute(hidden, 'x', turn(size_x, k))  8.41 us
    ppermute x3, waiting for transfers between devices, shards(): block = hidden if k == 0 else lax.ppermute(hidden, 'x', turn(size_x, k))  7.64 us
    all_to_all x4, waiting for transfers between devices, trade(): return lax.all_to_all(parts, axis, 0, 0, tiled=True)  7.11 us
    ppermute x1, starting transfers between devices, shards(): lax.ppermute(grad_sent.astype(bf16), 'c', SWAP)  3.99 us
  transfers between devices with their start and end apart: 12, of which 7 were waited for; matrix products, arithmetic and copies ran while one was open for 6% of the time, Pallas kernels for 0%

profile of v8, /device:TPU:1, one launch (start us, length us, event | category | flops | bytes accessed | tf_op | source)
XLA Modules:
  0.0 161.3 jit_solution(7245753391111118053)
XLA Ops:
  0.6 3.5 %shard_map.112 = bf16[768,1024]{1,0:T(8,128)(2,1)} custom-call(bf16[768,512]{1,0:T(8,128)(2,1)} %tokens_ref.1, bf16[512,512]{1,0:T(8,128)(2,1)} %bitcast.79, bf16[512,512]{1,0:T(8,128)(2,1)} %bitcast.80), custom_call_target="tpu_custom_call" | custom-call | tf_op jit(solution)/shard_map/pallas_call | solution.py:50
  4.1 5.0 %all-to-all-start = ((bf16[4,192,1024]{2,1,0:T(8,128)(2,1)}), bf16[4,192,1024]{2,1,0:T(8,128)(2,1)S(1)}, u32[]{:S(2)}, u32[]{:S(2)}) async-start(bf16[4,192,1024]{2,1,0:T(8,128)(2,1)} %bitcast.70), calls=%async_computation | async-start | bytes 3145728 | tf_op jit(solution)/shard_map/all_to_all | solution.py:27
  9.3 1.2 add_convert_fusion
  10.5 11.2 %collective-permute-start = (bf16[256,512]{1,0:T(8,128)(2,1)S(1)}, bf16[256,512]{1,0:T(8,128)(2,1)S(1)}, u32[]{:S(2)}, u32[]{:S(2)}) collective-permute-start(bf16[256,512]{1,0:T(8,128)(2,1)S(1)} %get-tuple-element.37), channel_id=1, source_target_pairs={{0,16},{16,0},{1,17},{17,1},{2,18},{18,2},{3,19},{19,3},{4,20},{20... | collective-permute-start | bytes 786440 | tf_op jit(solution)/shard_map/ppermute | solution.py:86
  21.7 1.1 collective-permute-done
  22.9 0.8 pad_maximum_fusion
  23.7 1.1 reduce_sum.30
  24.8 19.4 %all-to-all-start.1 = ((bf16[4,48,1024]{2,1,0:T(8,128)(2,1)}), bf16[4,48,1024]{2,1,0:T(8,128)(2,1)S(1)}, u32[]{:S(2)}, u32[]{:S(2)}) async-start(bf16[4,48,1024]{2,1,0:T(8,128)(2,1)} %bitcast.5), calls=%async_computation.1 | async-start | bytes 786432 | tf_op jit(solution)/shard_map/all_to_all | solution.py:27
  44.3 2.3 %collective-permute-start.1 = (bf16[512,512]{1,0:T(8,128)(2,1)}, bf16[512,512]{1,0:T(8,128)(2,1)}, u32[]{:S(2)}, u32[]{:S(2)}) collective-permute-start(bf16[512,512]{1,0:T(8,128)(2,1)} %pad_maximum_fusion), channel_id=1, source_target_pairs={{0,2},{1,3},{2,0},{3,1},{4,6},{5,7},{6,4},{7,5},{8,10},{9,11},{10,... | collective-permute-start | bytes 1572872 | tf_op jit(solution)/shard_map/ppermute | solution.py:91
  46.5 3.0 %collective-permute-start.2 = (bf16[512,512]{1,0:T(8,128)(2,1)}, bf16[512,512]{1,0:T(8,128)(2,1)}, u32[]{:S(2)}, u32[]{:S(2)}) collective-permute-start(bf16[512,512]{1,0:T(8,128)(2,1)} %pad_maximum_fusion), channel_id=1, source_target_pairs={{0,1},{1,2},{2,3},{3,0},{4,5},{5,6},{6,7},{7,4},{8,9},{9,10},{10,1... | collective-permute-start | bytes 1572872 | tf_op jit(solution)/shard_map/ppermute | solution.py:91
  49.5 3.5 %collective-permute-start.3 = (bf16[512,512]{1,0:T(8,128)(2,1)}, bf16[512,512]{1,0:T(8,128)(2,1)}, u32[]{:S(2)}, u32[]{:S(2)}) collective-permute-start(bf16[512,512]{1,0:T(8,128)(2,1)} %pad_maximum_fusion), channel_id=1, source_target_pairs={{0,3},{1,0},{2,1},{3,2},{4,7},{5,4},{6,5},{7,6},{8,11},{9,8},{10,9... | collective-permute-start | bytes 1572872 | tf_op jit(solution)/shard_map/ppermute | solution.py:91
  53.0 2.5 %all-to-all-done.1 = bf16[4,48,1024]{2,1,0:T(8,128)(2,1)S(1)} async-done(((bf16[4,48,1024]{2,1,0:T(8,128)(2,1)}), bf16[4,48,1024]{2,1,0:T(8,128)(2,1)S(1)}, u32[]{:S(2)}, u32[]{:S(2)}) %all-to-all-start.1) | async-done | bytes 393248 | tf_op jit(solution)/shard_map/all_to_all | solution.py:27
  55.7 0.7 broadcast_in_dim.14
  56.4 12.9 %all-to-all-start.2 = ((bf16[8,48,256]{2,1,0:T(8,128)(2,1)}), bf16[8,48,256]{2,1,0:T(8,128)(2,1)S(1)}, u32[]{:S(2)}, u32[]{:S(2)}) async-start(bf16[8,48,256]{2,1,0:T(8,128)(2,1)} %bitcast.8), calls=%async_computation.2 | async-start | bytes 393216 | tf_op jit(solution)/shard_map/all_to_all | solution.py:27
  69.3 1.1 constant_dynamic-update-slice_fusion.3
  70.4 1.1 constant_dynamic-update-slice_fusion.2
  71.6 1.5 collective-permute-done.2
  73.0 1.1 constant_dynamic-update-slice_fusion.1
  74.2 1.1 constant_dynamic-update-slice_fusion
  75.3 4.6 %all-to-all-done.2 = bf16[8,48,256]{2,1,0:T(8,128)(2,1)S(1)} async-done(((bf16[8,48,256]{2,1,0:T(8,128)(2,1)}), bf16[8,48,256]{2,1,0:T(8,128)(2,1)S(1)}, u32[]{:S(2)}, u32[]{:S(2)}) %all-to-all-start.2) | async-done | bytes 196640 | tf_op jit(solution)/shard_map/all_to_all | solution.py:27
  80.2 1.3 fusion.1
  81.5 12.1 %all-to-all-start.3 = ((bf16[24,8,2048]{2,1,0:T(8,128)(2,1)}), bf16[24,8,2048]{2,1,0:T(8,128)(2,1)S(1)}, u32[]{:S(2)}, u32[]{:S(2)}) async-start(bf16[24,8,2048]{2,1,0:T(8,128)(2,1)} %fusion.1), calls=%async_computation.3 | async-start | bytes 1572864 | tf_op jit(solution)/shard_map/all_to_all | solution.py:27
  93.7 0.7 fusion.26
  102.2 2.2 %collective-permute-start.4 = (bf16[2,192,256]{2,1,0:T(8,128)(2,1)S(1)}, bf16[2,192,256]{2,1,0:T(8,128)(2,1)S(1)}, u32[]{:S(2)}, u32[]{:S(2)}) collective-permute-start(bf16[2,192,256]{2,1,0:T(8,128)(2,1)S(1)} %bitcast.75), channel_id=1, source_target_pairs={{0,1},{1,2},{2,3},{3,0},{4,5},{5,6},{6,7},{7,4},{8,9},{9,10},{10,1... | collective-permute-start | bytes 589832 | tf_op jit(solution)/shard_map/ppermute | solution.py:117
  104.4 3.7 %collective-permute-start.5 = (bf16[2,192,256]{2,1,0:T(8,128)(2,1)S(1)}, bf16[2,192,256]{2,1,0:T(8,128)(2,1)S(1)}, u32[]{:S(2)}, u32[]{:S(2)}) collective-permute-start(bf16[2,192,256]{2,1,0:T(8,128)(2,1)S(1)} %bitcast.76), channel_id=1, source_target_pairs={{0,2},{1,3},{2,0},{3,1},{4,6},{5,7},{6,4},{7,5},{8,10},{9,11},{10,... | collective-permute-start | bytes 589832 | tf_op jit(solution)/shard_map/ppermute | solution.py:117
  108.1 2.5 %collective-permute-start.6 = (bf16[2,192,256]{2,1,0:T(8,128)(2,1)S(1)}, bf16[2,192,256]{2,1,0:T(8,128)(2,1)S(1)}, u32[]{:S(2)}, u32[]{:S(2)}) collective-permute-start(bf16[2,192,256]{2,1,0:T(8,128)(2,1)S(1)} %bitcast.77), channel_id=1, source_target_pairs={{0,3},{1,0},{2,1},{3,2},{4,7},{5,4},{6,5},{7,6},{8,11},{9,8},{10,9... | collective-permute-start | bytes 589832 | tf_op jit(solution)/shard_map/ppermute | solution.py:117
  110.7 5.4 %collective-permute-done.4 = bf16[2,192,256]{2,1,0:T(8,128)(2,1)S(1)} collective-permute-done((bf16[2,192,256]{2,1,0:T(8,128)(2,1)S(1)}, bf16[2,192,256]{2,1,0:T(8,128)(2,1)S(1)}, u32[]{:S(2)}, u32[]{:S(2)}) %collective-permute-start.4) | collective-permute-done | bytes 196640 | tf_op jit(solution)/shard_map/ppermute | solution.py:117
  116.2 2.2 %collective-permute-done.6 = bf16[2,192,256]{2,1,0:T(8,128)(2,1)S(1)} collective-permute-done((bf16[2,192,256]{2,1,0:T(8,128)(2,1)S(1)}, bf16[2,192,256]{2,1,0:T(8,128)(2,1)S(1)}, u32[]{:S(2)}, u32[]{:S(2)}) %collective-permute-start.6) | collective-permute-done | bytes 196640 | tf_op jit(solution)/shard_map/ppermute | solution.py:117
  118.8 35.5 %all_to_all.25 = bf16[96,8,512]{2,1,0:T(8,128)(2,1)S(1)} all-to-all(bf16[96,8,512]{2,1,0:T(8,128)(2,1)S(1)} %bitcast.71), channel_id=1, replica_groups=mesh['y'=8,'zl'=3,'c'=2,'zh'=4,'x'=4] {'x','y','zl'}, dimensions={0} | all-to-all | bytes 1572864 | tf_op jit(solution)/shard_map/all_to_all | solution.py:27
  154.8 4.0 %collective-permute-start.7 = (bf16[256,512]{1,0:T(8,128)(2,1)S(1)}, bf16[256,512]{1,0:T(8,128)(2,1)S(1)}, u32[]{:S(2)}, u32[]{:S(2)}) collective-permute-start(bf16[256,512]{1,0:T(8,128)(2,1)S(1)} %fusion.4), channel_id=1, source_target_pairs={{0,16},{16,0},{1,17},{17,1},{2,18},{18,2},{3,19},{19,3},{4,20},{20... | collective-permute-start | bytes 786440 | tf_op jit(solution)/shard_map/ppermute | solution.py:150
  158.8 0.7 convert_multiply_fusion.2
  159.9 1.4 divide_subtract_fusion
  (38 shorter events, 2.0 us)
Async XLA Ops:
  4.1 5.0 %copy-start = (f32[256,512]{1,0:T(8,128)S(1)}, f32[256,512]{1,0:T(8,128)}, u32[]{:S(2)}) copy-start(f32[256,512]{1,0:T(8,128)} %param.14) | copy-start | bytes 1572868
  4.1 5.1 %copy-start.1 = (f32[256,512]{1,0:T(8,128)S(1)}, f32[256,512]{1,0:T(8,128)}, u32[]{:S(2)}) copy-start(f32[256,512]{1,0:T(8,128)} %param.13) | copy-start | bytes 1572868
  4.1 19.6 %all-to-all-start = ((bf16[4,192,1024]{2,1,0:T(8,128)(2,1)}), bf16[4,192,1024]{2,1,0:T(8,128)(2,1)S(1)}, u32[]{:S(2)}, u32[]{:S(2)}) async-start(bf16[4,192,1024]{2,1,0:T(8,128)(2,1)} %bitcast.70), calls=%async_computation | async-start | bytes 3145728 | tf_op jit(solution)/shard_map/all_to_all | solution.py:27
  10.5 12.3 %collective-permute-start = (bf16[256,512]{1,0:T(8,128)(2,1)S(1)}, bf16[256,512]{1,0:T(8,128)(2,1)S(1)}, u32[]{:S(2)}, u32[]{:S(2)}) collective-permute-start(bf16[256,512]{1,0:T(8,128)(2,1)S(1)} %get-tuple-element.37), channel_id=1, source_target_pairs={{0,16},{16,0},{1,17},{17,1},{2,18},{18,2},{3,19},{19,3},{4,20},{20... | collective-permute-start | bytes 786440 | tf_op jit(solution)/shard_map/ppermute | solution.py:86
  24.8 30.7 %all-to-all-start.1 = ((bf16[4,48,1024]{2,1,0:T(8,128)(2,1)}), bf16[4,48,1024]{2,1,0:T(8,128)(2,1)S(1)}, u32[]{:S(2)}, u32[]{:S(2)}) async-start(bf16[4,48,1024]{2,1,0:T(8,128)(2,1)} %bitcast.5), calls=%async_computation.1 | async-start | bytes 786432 | tf_op jit(solution)/shard_map/all_to_all | solution.py:27
  44.3 26.2 %collective-permute-start.1 = (bf16[512,512]{1,0:T(8,128)(2,1)}, bf16[512,512]{1,0:T(8,128)(2,1)}, u32[]{:S(2)}, u32[]{:S(2)}) collective-permute-start(bf16[512,512]{1,0:T(8,128)(2,1)} %pad_maximum_fusion), channel_id=1, source_target_pairs={{0,2},{1,3},{2,0},{3,1},{4,6},{5,7},{6,4},{7,5},{8,10},{9,11},{10,... | collective-permute-start | bytes 1572872 | tf_op jit(solution)/shard_map/ppermute | solution.py:91
  46.5 26.5 %collective-permute-start.2 = (bf16[512,512]{1,0:T(8,128)(2,1)}, bf16[512,512]{1,0:T(8,128)(2,1)}, u32[]{:S(2)}, u32[]{:S(2)}) collective-permute-start(bf16[512,512]{1,0:T(8,128)(2,1)} %pad_maximum_fusion), channel_id=1, source_target_pairs={{0,1},{1,2},{2,3},{3,0},{4,5},{5,6},{6,7},{7,4},{8,9},{9,10},{10,1... | collective-permute-start | bytes 1572872 | tf_op jit(solution)/shard_map/ppermute | solution.py:91
  49.5 24.6 %collective-permute-start.3 = (bf16[512,512]{1,0:T(8,128)(2,1)}, bf16[512,512]{1,0:T(8,128)(2,1)}, u32[]{:S(2)}, u32[]{:S(2)}) collective-permute-start(bf16[512,512]{1,0:T(8,128)(2,1)} %pad_maximum_fusion), channel_id=1, source_target_pairs={{0,3},{1,0},{2,1},{3,2},{4,7},{5,4},{6,5},{7,6},{8,11},{9,8},{10,9... | collective-permute-start | bytes 1572872 | tf_op jit(solution)/shard_map/ppermute | solution.py:91
  56.4 23.5 %all-to-all-start.2 = ((bf16[8,48,256]{2,1,0:T(8,128)(2,1)}), bf16[8,48,256]{2,1,0:T(8,128)(2,1)S(1)}, u32[]{:S(2)}, u32[]{:S(2)}) async-start(bf16[8,48,256]{2,1,0:T(8,128)(2,1)} %bitcast.8), calls=%async_computation.2 | async-start | bytes 393216 | tf_op jit(solution)/shard_map/all_to_all | solution.py:27
  81.5 12.1 %copy-start.3 = (s32[4]{0:T(128)S(1)}, s32[4]{0:T(128)}, u32[]{:S(2)}) copy-start(s32[4]{0:T(128)} %constant.122.clone) | copy-start | bytes 52
  81.5 37.0 %all-to-all-start.3 = ((bf16[24,8,2048]{2,1,0:T(8,128)(2,1)}), bf16[24,8,2048]{2,1,0:T(8,128)(2,1)S(1)}, u32[]{:S(2)}, u32[]{:S(2)}) async-start(bf16[24,8,2048]{2,1,0:T(8,128)(2,1)} %fusion.1), calls=%async_computation.3 | async-start | bytes 1572864 | tf_op jit(solution)/shard_map/all_to_all | solution.py:27
  102.2 13.9 %collective-permute-start.4 = (bf16[2,192,256]{2,1,0:T(8,128)(2,1)S(1)}, bf16[2,192,256]{2,1,0:T(8,128)(2,1)S(1)}, u32[]{:S(2)}, u32[]{:S(2)}) collective-permute-start(bf16[2,192,256]{2,1,0:T(8,128)(2,1)S(1)} %bitcast.75), channel_id=1, source_target_pairs={{0,1},{1,2},{2,3},{3,0},{4,5},{5,6},{6,7},{7,4},{8,9},{9,10},{10,1... | collective-permute-start | bytes 589832 | tf_op jit(solution)/shard_map/ppermute | solution.py:117
  104.4 11.8 %collective-permute-start.5 = (bf16[2,192,256]{2,1,0:T(8,128)(2,1)S(1)}, bf16[2,192,256]{2,1,0:T(8,128)(2,1)S(1)}, u32[]{:S(2)}, u32[]{:S(2)}) collective-permute-start(bf16[2,192,256]{2,1,0:T(8,128)(2,1)S(1)} %bitcast.76), channel_id=1, source_target_pairs={{0,2},{1,3},{2,0},{3,1},{4,6},{5,7},{6,4},{7,5},{8,10},{9,11},{10,... | collective-permute-start | bytes 589832 | tf_op jit(solution)/shard_map/ppermute | solution.py:117
  108.1 10.3 %collective-permute-start.6 = (bf16[2,192,256]{2,1,0:T(8,128)(2,1)S(1)}, bf16[2,192,256]{2,1,0:T(8,128)(2,1)S(1)}, u32[]{:S(2)}, u32[]{:S(2)}) collective-permute-start(bf16[2,192,256]{2,1,0:T(8,128)(2,1)S(1)} %bitcast.77), channel_id=1, source_target_pairs={{0,3},{1,0},{2,1},{3,2},{4,7},{5,4},{6,5},{7,6},{8,11},{9,8},{10,9... | collective-permute-start | bytes 589832 | tf_op jit(solution)/shard_map/ppermute | solution.py:117
  118.5 35.8 %copy-start.4 = (bf16[768,512]{1,0:T(8,128)(2,1)S(1)}, bf16[768,512]{1,0:T(8,128)(2,1)}, u32[]{:S(2)}) copy-start(bf16[768,512]{1,0:T(8,128)(2,1)} %param.10) | copy-start | bytes 2359300
  154.3 4.5 %copy-start.2 = (bf16[2,256,512]{2,1,0:T(8,128)(2,1)S(1)}, bf16[2,256,512]{2,1,0:T(8,128)(2,1)}, u32[]{:S(2)}) copy-start(bf16[2,256,512]{2,1,0:T(8,128)(2,1)} %param.16) | copy-start | bytes 1572868
  154.3 4.5 %copy-start.5 = (f32[256,512]{1,0:T(8,128)S(1)}, f32[256,512]{1,0:T(8,128)}, u32[]{:S(2)}) copy-start(f32[256,512]{1,0:T(8,128)} %param.15) | copy-start | bytes 1572868
  154.8 5.1 %collective-permute-start.7 = (bf16[256,512]{1,0:T(8,128)(2,1)S(1)}, bf16[256,512]{1,0:T(8,128)(2,1)S(1)}, u32[]{:S(2)}, u32[]{:S(2)}) collective-permute-start(bf16[256,512]{1,0:T(8,128)(2,1)S(1)} %fusion.4), channel_id=1, source_target_pairs={{0,16},{16,0},{1,17},{17,1},{2,18},{18,2},{3,19},{19,3},{4,20},{20... | collective-permute-start | bytes 786440 | tf_op jit(solution)/shard_map/ppermute | solution.py:150

commit v9 on v7

--- a/solution.py
+++ b/solution.py
@@ -94,28 +94,27 @@
     hidden = trade(parts.reshape(-1, share, unit_count), ("c", "zh"))
     rows_x = size_zh * share
     hidden = hidden.reshape(size_c, rows_x, unit_count)
-    hidden_own = lax.dynamic_index_in_dim(hidden, core, 0, False)
-    hidden_other = lax.dynamic_index_in_dim(hidden, 1 - core, 0, False)
+    hidden = jnp.concatenate(
+        [
+            lax.dynamic_index_in_dim(hidden, core, 0, False),
+            lax.dynamic_index_in_dim(hidden, 1 - core, 0, False),
+        ],
+        axis=1,
+    )
 
-    partial = jnp.dot(hidden_own, wide[:unit_count], preferred_element_type=f32) + jnp.dot(
-        hidden_other, wide[unit_count:], preferred_element_type=f32
-    )
+    wide = lax.optimization_barrier(wide)
+    partial = jnp.dot(hidden, wide, preferred_element_type=f32)
     chips = size_y * size_zl
     rows_share = rows_x // chips
     partial = partial.astype(bf16).reshape(chips, rows_share, size_x * width)
     hidden, partial = lax.optimization_barrier((hidden, partial))
     here = lax.axis_index("x")
-    rows = jnp.zeros((size_c, size_x, rows_x, unit_count), bf16)
+    rows = jnp.zeros((size_x, rows_x, both), bf16)
     for k in range(size_x):
         block = hidden if k == 0 else lax.ppermute(hidden, "x", turn(size_x, k))
-        rows = lax.dynamic_update_slice(rows, block[:, None], (0, (here - k) % size_x, 0, 0))
-    rows = rows.reshape(size_c, token_count, unit_count)
-    rows_own = lax.dynamic_index_in_dim(rows, core, 0, False)
-    rows_other = lax.dynamic_index_in_dim(rows, 1 - core, 0, False)
-
-    partial, rows_own, rows_other = lax.optimization_barrier(
-        (trade(partial, ("y", "zl")), rows_own, rows_other)
-    )
+        rows = lax.dynamic_update_slice(rows, block[None], ((here - k) % size_x, 0, 0))
+    rows = rows.reshape(token_count, both)
+    partial, rows = lax.optimization_barrier((trade(partial, ("y", "zl")), rows))
     out_share = (jnp.sum(partial.astype(f32), axis=0) * scale_out).astype(bf16)
     out_share = out_share.reshape(rows_share, size_x, width)
     sends = jnp.stack(
@@ -128,8 +127,8 @@
     def grad(hidden_part):
         return jnp.dot(hidden_part.T, d_out, preferred_element_type=f32) * scale_out
 
-    grad_sent = grad(rows_other)
-    grad_own = grad(rows_own)
+    grad_sent = grad(rows[:, unit_count:]).astype(bf16)
+    grad_own = grad(rows[:, :unit_count])
     noise_own = lax.dynamic_index_in_dim(noise, core, 0, False).astype(f32)
     noise_other = lax.dynamic_index_in_dim(noise, 1 - core, 0, False).astype(f32) * (0.5 * inv_sigma)
     momentum_own = beta_one * momentum + (1.0 - beta_one) * 0.5 * grad_own
@@ -138,6 +137,7 @@
     grad_other, momentum_own, curv_own, noise_other, spread_gain = lax.optimization_barrier(
         (lax.ppermute(grad_sent, "c", SWAP), momentum_own, curv_own, noise_other, spread_gain)
     )
+    grad_other = grad_other.astype(f32)
     new_momentum = momentum_own + (1.0 - beta_one) * 0.5 * grad_other
     curv_mean = curv_own + grad_other * noise_other
     spread = hessian - curv_mean

time: 154 us -> 155 us (level)
  local copies, waits for them, and re-layouts: 5.43 us -> 0.99 us
  waiting for transfers between devices: 23.1 us -> 26.1 us
    ppermute x3, waiting for transfers between devices: 1.54 us -> 6.3 us  [shards(): lax.ppermute(weights, 'x', turn(size_x, k))]
    unnamed x15 -> x14, local copies, waits for them, and re-layouts: 3.33 us -> 0.04 us
    concatenate x0 -> x2, other arithmetic: none -> 1.76 us  [the longest x1 1.75 us: shards(): jnp.concatenate([weights] + [lax.ppermute(weights, 'x', turn(size_x, k))...]
  transfers between devices with their start and end apart: 12 -> 12, of which waited for: 8 -> 8; matrix products, arithmetic and copies ran while one was open for 5% -> 2% of each run, Pallas kernels for 0% -> 0%
where the time goes in v9:
time: 155 us; the launch traced here: 154 us
  starting transfers between devices  82.4 us (53%)
  blocking collectives  31.3 us (20%)
  waiting for transfers between devices  26.1 us (17%)
  other arithmetic  4.94 us (3%)
  matrix products  3.76 us (2%)
  Pallas kernels  3.49 us (2%)
    all_to_all x4, starting transfers between devices, trade(): return lax.all_to_all(parts, axis, 0, 0, tiled=True)  51 us
    all_to_all x1, blocking collectives, trade(): return lax.all_to_all(parts, axis, 0, 0, tiled=True)  31.3 us
    ppermute x1, starting transfers between devices, shards(): lax.ppermute(lax.dynamic_index_in_dim(samples, 1 - core, 0, False), 'c',...  11.2 us
    all_to_all x4, waiting for transfers between devices, trade(): return lax.all_to_all(parts, axis, 0, 0, tiled=True)  10.6 us
    ppermute x3, starting transfers between devices, shards(): block = hidden if k == 0 else lax.ppermute(hidden, 'x', turn(size_x, k))  8.42 us
    ppermute x3, starting transfers between devices, shards(): lax.ppermute(weights, 'x', turn(size_x, k))  7.8 us
    ppermute x3, waiting for transfers between devices, shards(): block = hidden if k == 0 else lax.ppermute(hidden, 'x', turn(size_x, k))  7.63 us
    ppermute x3, waiting for transfers between devices, shards(): lax.ppermute(weights, 'x', turn(size_x, k))  6.3 us
  transfers between devices with their start and end apart: 12, of which 8 were waited for; matrix products, arithmetic and copies ran while one was open for 2% of the time, Pallas kernels for 0%

profile of v9, /device:TPU:1, one launch (start us, length us, event | category | flops | bytes accessed | tf_op | source)
XLA Modules:
  0.0 154.0 jit_solution(1333115344055791264)
XLA Ops:
  0.6 3.5 %shard_map.103 = bf16[768,1024]{1,0:T(8,128)(2,1)} custom-call(bf16[768,512]{1,0:T(8,128)(2,1)} %tokens_ref.1, bf16[512,512]{1,0:T(8,128)(2,1)} %bitcast.58, bf16[512,512]{1,0:T(8,128)(2,1)} %bitcast.59), custom_call_target="tpu_custom_call" | custom-call | tf_op jit(solution)/shard_map/pallas_call | solution.py:46
  4.1 5.0 %all-to-all-start = ((bf16[4,192,1024]{2,1,0:T(8,128)(2,1)}), bf16[4,192,1024]{2,1,0:T(8,128)(2,1)S(1)}, u32[]{:S(2)}, u32[]{:S(2)}) async-start(bf16[4,192,1024]{2,1,0:T(8,128)(2,1)} %bitcast.53), calls=%async_computation | async-start | bytes 3145728 | tf_op jit(solution)/shard_map/all_to_all | solution.py:27
  9.1 0.2 multiply_sqrt_fusion
  9.3 0.2 add_convert_fusion
  9.5 11.2 %collective-permute-start = (bf16[256,512]{1,0:T(8,128)(2,1)S(1)}, bf16[256,512]{1,0:T(8,128)(2,1)S(1)}, u32[]{:S(2)}, u32[]{:S(2)}) collective-permute-start(bf16[256,512]{1,0:T(8,128)(2,1)S(1)} %get-tuple-element.33), channel_id=1, source_target_pairs={{0,16},{16,0},{1,17},{17,1},{2,18},{18,2},{3,19},{19,3},{4,20},{20... | collective-permute-start | bytes 786440 | tf_op jit(solution)/shard_map/ppermute | solution.py:82
  20.7 1.1 collective-permute-done
  21.9 1.1 reduce_sum.30
  23.1 21.2 %all-to-all-start.1 = ((bf16[4,48,1024]{2,1,0:T(8,128)(2,1)}), bf16[4,48,1024]{2,1,0:T(8,128)(2,1)S(1)}, u32[]{:S(2)}, u32[]{:S(2)}) async-start(bf16[4,48,1024]{2,1,0:T(8,128)(2,1)} %bitcast.5), calls=%async_computation.1 | async-start | bytes 786432 | tf_op jit(solution)/shard_map/all_to_all | solution.py:27
  44.3 2.8 %collective-permute-start.3 = (bf16[512,512]{1,0:T(8,128)(2,1)S(1)}, bf16[512,512]{1,0:T(8,128)(2,1)}, u32[]{:S(2)}, u32[]{:S(2)}) collective-permute-start(bf16[512,512]{1,0:T(8,128)(2,1)S(1)} %pad_maximum_fusion.1), channel_id=1, source_target_pairs={{0,3},{1,0},{2,1},{3,2},{4,7},{5,4},{6,5},{7,6},{8,11},{9,8},{10,9... | collective-permute-start | bytes 1572872 | tf_op jit(solution)/shard_map/ppermute | solution.py:85
  47.1 3.1 %collective-permute-start.2 = (bf16[512,512]{1,0:T(8,128)(2,1)S(1)}, bf16[512,512]{1,0:T(8,128)(2,1)}, u32[]{:S(2)}, u32[]{:S(2)}) collective-permute-start(bf16[512,512]{1,0:T(8,128)(2,1)S(1)} %pad_maximum_fusion.1), channel_id=1, source_target_pairs={{0,2},{1,3},{2,0},{3,1},{4,6},{5,7},{6,4},{7,5},{8,10},{9,11},{10,... | collective-permute-start | bytes 1572872 | tf_op jit(solution)/shard_map/ppermute | solution.py:85
  50.2 1.9 %collective-permute-start.1 = (bf16[512,512]{1,0:T(8,128)(2,1)S(1)}, bf16[512,512]{1,0:T(8,128)(2,1)}, u32[]{:S(2)}, u32[]{:S(2)}) collective-permute-start(bf16[512,512]{1,0:T(8,128)(2,1)S(1)} %pad_maximum_fusion.1), channel_id=1, source_target_pairs={{0,1},{1,2},{2,3},{3,0},{4,5},{5,6},{6,7},{7,4},{8,9},{9,10},{10,1... | collective-permute-start | bytes 1572872 | tf_op jit(solution)/shard_map/ppermute | solution.py:85
  52.1 3.5 %all-to-all-done.1 = bf16[4,48,1024]{2,1,0:T(8,128)(2,1)S(1)} async-done(((bf16[4,48,1024]{2,1,0:T(8,128)(2,1)}), bf16[4,48,1024]{2,1,0:T(8,128)(2,1)S(1)}, u32[]{:S(2)}, u32[]{:S(2)}) %all-to-all-start.1) | async-done | bytes 393248 | tf_op jit(solution)/shard_map/all_to_all | solution.py:27
  55.7 0.7 broadcast_in_dim.14
  56.4 12.9 %all-to-all-start.2 = ((bf16[8,48,256]{2,1,0:T(8,128)(2,1)}), bf16[8,48,256]{2,1,0:T(8,128)(2,1)S(1)}, u32[]{:S(2)}, u32[]{:S(2)}) async-start(bf16[8,48,256]{2,1,0:T(8,128)(2,1)} %bitcast.8), calls=%async_computation.2 | async-start | bytes 393216 | tf_op jit(solution)/shard_map/all_to_all | solution.py:27
  69.4 6.3 %collective-permute-done.1 = bf16[512,512]{1,0:T(8,128)(2,1)} collective-permute-done((bf16[512,512]{1,0:T(8,128)(2,1)S(1)}, bf16[512,512]{1,0:T(8,128)(2,1)}, u32[]{:S(2)}, u32[]{:S(2)}) %collective-permute-start.1) | collective-permute-done | bytes 524320 | tf_op jit(solution)/shard_map/ppermute | solution.py:85
  75.7 1.7 %pad_maximum_fusion = bf16[512,2048]{1,0:T(8,128)(2,1)S(1)} fusion(bf16[512,512]{1,0:T(8,128)(2,1)} %collective-permute-done.3, bf16[512,512]{1,0:T(8,128)(2,1)} %collective-permute-done.2, bf16[512,512]{1,0:T(8,128)(2,1)} %collective-permute-done.1, bf16[512,512]{1,0:T(8,128)(2,1)} %copy-done.2), kind=kLoop, calls=%fused_computation.2 | loop fusion | flops 8388608 | bytes 4194304 | tf_op jit(solution)/shard_map/concatenate | solution.py:85
  77.4 2.5 %all-to-all-done.2 = bf16[8,48,256]{2,1,0:T(8,128)(2,1)S(1)} async-done(((bf16[8,48,256]{2,1,0:T(8,128)(2,1)}), bf16[8,48,256]{2,1,0:T(8,128)(2,1)S(1)}, u32[]{:S(2)}, u32[]{:S(2)}) %all-to-all-start.2) | async-done | bytes 196640 | tf_op jit(solution)/shard_map/all_to_all | solution.py:27
  79.9 1.5 fusion
  81.4 11.9 %all-to-all-start.3 = ((bf16[24,8,2048]{2,1,0:T(8,128)(2,1)}), bf16[24,8,2048]{2,1,0:T(8,128)(2,1)S(1)}, u32[]{:S(2)}, u32[]{:S(2)}) async-start(bf16[24,8,2048]{2,1,0:T(8,128)(2,1)} %fusion), calls=%async_computation.3 | async-start | bytes 1572864 | tf_op jit(solution)/shard_map/all_to_all | solution.py:27
  93.4 2.2 %collective-permute-start.4 = (bf16[192,512]{1,0:T(8,128)(2,1)S(1)}, bf16[192,512]{1,0:T(8,128)(2,1)S(1)}, u32[]{:S(2)}, u32[]{:S(2)}) collective-permute-start(bf16[192,512]{1,0:T(8,128)(2,1)S(1)} %pad_maximum_fusion.2), channel_id=1, source_target_pairs={{0,1},{1,2},{2,3},{3,0},{4,5},{5,6},{6,7},{7,4},{8,9},{9,10},{10,1... | collective-permute-start | bytes 589832 | tf_op jit(solution)/shard_map/ppermute | solution.py:114
  95.6 3.7 %collective-permute-start.5 = (bf16[192,512]{1,0:T(8,128)(2,1)S(1)}, bf16[192,512]{1,0:T(8,128)(2,1)S(1)}, u32[]{:S(2)}, u32[]{:S(2)}) collective-permute-start(bf16[192,512]{1,0:T(8,128)(2,1)S(1)} %pad_maximum_fusion.2), channel_id=1, source_target_pairs={{0,2},{1,3},{2,0},{3,1},{4,6},{5,7},{6,4},{7,5},{8,10},{9,11},{10,... | collective-permute-start | bytes 589832 | tf_op jit(solution)/shard_map/ppermute | solution.py:114
  99.3 2.5 %collective-permute-start.6 = (bf16[192,512]{1,0:T(8,128)(2,1)S(1)}, bf16[192,512]{1,0:T(8,128)(2,1)S(1)}, u32[]{:S(2)}, u32[]{:S(2)}) collective-permute-start(bf16[192,512]{1,0:T(8,128)(2,1)S(1)} %pad_maximum_fusion.2), channel_id=1, source_target_pairs={{0,3},{1,0},{2,1},{3,2},{4,7},{5,4},{6,5},{7,6},{8,11},{9,8},{10,9... | collective-permute-start | bytes 589832 | tf_op jit(solution)/shard_map/ppermute | solution.py:114
  101.9 5.4 %collective-permute-done.4 = bf16[192,512]{1,0:T(8,128)(2,1)S(1)} collective-permute-done((bf16[192,512]{1,0:T(8,128)(2,1)S(1)}, bf16[192,512]{1,0:T(8,128)(2,1)S(1)}, u32[]{:S(2)}, u32[]{:S(2)}) %collective-permute-start.4) | collective-permute-done | bytes 196640 | tf_op jit(solution)/shard_map/ppermute | solution.py:114
  107.4 2.2 %collective-permute-done.6 = bf16[192,512]{1,0:T(8,128)(2,1)S(1)} collective-permute-done((bf16[192,512]{1,0:T(8,128)(2,1)S(1)}, bf16[192,512]{1,0:T(8,128)(2,1)S(1)}, u32[]{:S(2)}, u32[]{:S(2)}) %collective-permute-start.6) | collective-permute-done | bytes 196640 | tf_op jit(solution)/shard_map/ppermute | solution.py:114
  109.6 4.7 %all-to-all-done.3 = bf16[24,8,2048]{2,1,0:T(8,128)(2,1)S(1)} async-done(((bf16[24,8,2048]{2,1,0:T(8,128)(2,1)}), bf16[24,8,2048]{2,1,0:T(8,128)(2,1)S(1)}, u32[]{:S(2)}, u32[]{:S(2)}) %all-to-all-start.3) | async-done | bytes 786464 | tf_op jit(solution)/shard_map/all_to_all | solution.py:27
  114.3 0.1 convert_reduce_fusion
  114.6 31.3 %all_to_all.25 = bf16[96,8,512]{2,1,0:T(8,128)(2,1)S(1)} all-to-all(bf16[96,8,512]{2,1,0:T(8,128)(2,1)S(1)} %bitcast.54), channel_id=1, replica_groups=mesh['y'=8,'zl'=3,'c'=2,'zh'=4,'x'=4] {'x','y','zl'}, dimensions={0} | all-to-all | bytes 1572864 | tf_op jit(solution)/shard_map/all_to_all | solution.py:27
  145.8 1.6 %fusion.3 = bf16[256,512]{1,0:T(8,128)(2,1)S(1)} fusion(bf16[768,512]{1,0:T(8,128)(2,1)S(1)} %bitcast.56, bf16[768,512]{1,0:T(8,128)(2,1)} %param.9, bf16[96,8,512]{2,1,0:T(8,128)(2,1)S(1)} %all_to_all.25), kind=kOutput, calls=%fused_computation.8 | convolution fusion | flops 203554816 | bytes 2228224 | tf_op jit(solution)/shard_map/dot_general | solution.py:128
  147.4 4.0 %collective-permute-start.7 = (bf16[256,512]{1,0:T(8,128)(2,1)S(1)}, bf16[256,512]{1,0:T(8,128)(2,1)S(1)}, u32[]{:S(2)}, u32[]{:S(2)}) collective-permute-start(bf16[256,512]{1,0:T(8,128)(2,1)S(1)} %fusion.3), channel_id=1, source_target_pairs={{0,16},{16,0},{1,17},{17,1},{2,18},{18,2},{3,19},{19,3},{4,20},{20... | collective-permute-start | bytes 786440 | tf_op jit(solution)/shard_map/ppermute | solution.py:138
  151.4 0.7 convert_multiply_fusion.2
  152.2 0.4 collective-permute-done.7
  152.6 1.4 divide_subtract_fusion
  (36 shorter events, 0.5 us)
Async XLA Ops:
  4.1 5.0 %copy-start = (f32[256,512]{1,0:T(8,128)S(1)}, f32[256,512]{1,0:T(8,128)}, u32[]{:S(2)}) copy-start(f32[256,512]{1,0:T(8,128)} %param.13) | copy-start | bytes 1572868
  4.1 5.2 %copy-start.1 = (f32[256,512]{1,0:T(8,128)S(1)}, f32[256,512]{1,0:T(8,128)}, u32[]{:S(2)}) copy-start(f32[256,512]{1,0:T(8,128)} %param.12) | copy-start | bytes 1572868
  4.1 5.2 %copy-start.3 = (bf16[2,256,512]{2,1,0:T(8,128)(2,1)S(1)}, bf16[2,256,512]{2,1,0:T(8,128)(2,1)}, u32[]{:S(2)}) copy-start(bf16[2,256,512]{2,1,0:T(8,128)(2,1)} %param.15) | copy-start | bytes 1572868
  4.1 17.8 %all-to-all-start = ((bf16[4,192,1024]{2,1,0:T(8,128)(2,1)}), bf16[4,192,1024]{2,1,0:T(8,128)(2,1)S(1)}, u32[]{:S(2)}, u32[]{:S(2)}) async-start(bf16[4,192,1024]{2,1,0:T(8,128)(2,1)} %bitcast.53), calls=%async_computation | async-start | bytes 3145728 | tf_op jit(solution)/shard_map/all_to_all | solution.py:27
  9.5 12.3 %collective-permute-start = (bf16[256,512]{1,0:T(8,128)(2,1)S(1)}, bf16[256,512]{1,0:T(8,128)(2,1)S(1)}, u32[]{:S(2)}, u32[]{:S(2)}) collective-permute-start(bf16[256,512]{1,0:T(8,128)(2,1)S(1)} %get-tuple-element.33), channel_id=1, source_target_pairs={{0,16},{16,0},{1,17},{17,1},{2,18},{18,2},{3,19},{19,3},{4,20},{20... | collective-permute-start | bytes 786440 | tf_op jit(solution)/shard_map/ppermute | solution.py:82
  21.9 34.5 %copy-start.2 = (bf16[512,512]{1,0:T(8,128)(2,1)}, bf16[512,512]{1,0:T(8,128)(2,1)S(1)}, u32[]{:S(2)}) copy-start(bf16[512,512]{1,0:T(8,128)(2,1)S(1)} %pad_maximum_fusion.1) | copy-start | bytes 1572868
  23.1 32.5 %all-to-all-start.1 = ((bf16[4,48,1024]{2,1,0:T(8,128)(2,1)}), bf16[4,48,1024]{2,1,0:T(8,128)(2,1)S(1)}, u32[]{:S(2)}, u32[]{:S(2)}) async-start(bf16[4,48,1024]{2,1,0:T(8,128)(2,1)} %bitcast.5), calls=%async_computation.1 | async-start | bytes 786432 | tf_op jit(solution)/shard_map/all_to_all | solution.py:27
  44.3 25.1 %collective-permute-start.3 = (bf16[512,512]{1,0:T(8,128)(2,1)S(1)}, bf16[512,512]{1,0:T(8,128)(2,1)}, u32[]{:S(2)}, u32[]{:S(2)}) collective-permute-start(bf16[512,512]{1,0:T(8,128)(2,1)S(1)} %pad_maximum_fusion.1), channel_id=1, source_target_pairs={{0,3},{1,0},{2,1},{3,2},{4,7},{5,4},{6,5},{7,6},{8,11},{9,8},{10,9... | collective-permute-start | bytes 1572872 | tf_op jit(solution)/shard_map/ppermute | solution.py:85
  47.1 22.3 %collective-permute-start.2 = (bf16[512,512]{1,0:T(8,128)(2,1)S(1)}, bf16[512,512]{1,0:T(8,128)(2,1)}, u32[]{:S(2)}, u32[]{:S(2)}) collective-permute-start(bf16[512,512]{1,0:T(8,128)(2,1)S(1)} %pad_maximum_fusion.1), channel_id=1, source_target_pairs={{0,2},{1,3},{2,0},{3,1},{4,6},{5,7},{6,4},{7,5},{8,10},{9,11},{10,... | collective-permute-start | bytes 1572872 | tf_op jit(solution)/shard_map/ppermute | solution.py:85
  50.2 25.5 %collective-permute-start.1 = (bf16[512,512]{1,0:T(8,128)(2,1)S(1)}, bf16[512,512]{1,0:T(8,128)(2,1)}, u32[]{:S(2)}, u32[]{:S(2)}) collective-permute-start(bf16[512,512]{1,0:T(8,128)(2,1)S(1)} %pad_maximum_fusion.1), channel_id=1, source_target_pairs={{0,1},{1,2},{2,3},{3,0},{4,5},{5,6},{6,7},{7,4},{8,9},{9,10},{10,1... | collective-permute-start | bytes 1572872 | tf_op jit(solution)/shard_map/ppermute | solution.py:85
  56.4 23.5 %all-to-all-start.2 = ((bf16[8,48,256]{2,1,0:T(8,128)(2,1)}), bf16[8,48,256]{2,1,0:T(8,128)(2,1)S(1)}, u32[]{:S(2)}, u32[]{:S(2)}) async-start(bf16[8,48,256]{2,1,0:T(8,128)(2,1)} %bitcast.8), calls=%async_computation.2 | async-start | bytes 393216 | tf_op jit(solution)/shard_map/all_to_all | solution.py:27
  81.4 32.9 %all-to-all-start.3 = ((bf16[24,8,2048]{2,1,0:T(8,128)(2,1)}), bf16[24,8,2048]{2,1,0:T(8,128)(2,1)S(1)}, u32[]{:S(2)}, u32[]{:S(2)}) async-start(bf16[24,8,2048]{2,1,0:T(8,128)(2,1)} %fusion), calls=%async_computation.3 | async-start | bytes 1572864 | tf_op jit(solution)/shard_map/all_to_all | solution.py:27
  93.4 13.9 %collective-permute-start.4 = (bf16[192,512]{1,0:T(8,128)(2,1)S(1)}, bf16[192,512]{1,0:T(8,128)(2,1)S(1)}, u32[]{:S(2)}, u32[]{:S(2)}) collective-permute-start(bf16[192,512]{1,0:T(8,128)(2,1)S(1)} %pad_maximum_fusion.2), channel_id=1, source_target_pairs={{0,1},{1,2},{2,3},{3,0},{4,5},{5,6},{6,7},{7,4},{8,9},{9,10},{10,1... | collective-permute-start | bytes 589832 | tf_op jit(solution)/shard_map/ppermute | solution.py:114
  95.6 11.7 %collective-permute-start.5 = (bf16[192,512]{1,0:T(8,128)(2,1)S(1)}, bf16[192,512]{1,0:T(8,128)(2,1)S(1)}, u32[]{:S(2)}, u32[]{:S(2)}) collective-permute-start(bf16[192,512]{1,0:T(8,128)(2,1)S(1)} %pad_maximum_fusion.2), channel_id=1, source_target_pairs={{0,2},{1,3},{2,0},{3,1},{4,6},{5,7},{6,4},{7,5},{8,10},{9,11},{10,... | collective-permute-start | bytes 589832 | tf_op jit(solution)/shard_map/ppermute | solution.py:114
  99.3 10.3 %collective-permute-start.6 = (bf16[192,512]{1,0:T(8,128)(2,1)S(1)}, bf16[192,512]{1,0:T(8,128)(2,1)S(1)}, u32[]{:S(2)}, u32[]{:S(2)}) collective-permute-start(bf16[192,512]{1,0:T(8,128)(2,1)S(1)} %pad_maximum_fusion.2), channel_id=1, source_target_pairs={{0,3},{1,0},{2,1},{3,2},{4,7},{5,4},{6,5},{7,6},{8,11},{9,8},{10,9... | collective-permute-start | bytes 589832 | tf_op jit(solution)/shard_map/ppermute | solution.py:114
  114.5 36.9 %copy-start.4 = (bf16[2,256,512]{2,1,0:T(8,128)(2,1)S(1)}, bf16[2,256,512]{2,1,0:T(8,128)(2,1)}, u32[]{:S(2)}) copy-start(bf16[2,256,512]{2,1,0:T(8,128)(2,1)} %param.15) | copy-start | bytes 1572868
  114.6 36.9 %copy-start.5 = (bf16[768,512]{1,0:T(8,128)(2,1)S(1)}, bf16[768,512]{1,0:T(8,128)(2,1)}, u32[]{:S(2)}) copy-start(bf16[768,512]{1,0:T(8,128)(2,1)} %param.9) | copy-start | bytes 2359300
  114.6 36.9 %copy-start.6 = (f32[256,512]{1,0:T(8,128)S(1)}, f32[256,512]{1,0:T(8,128)}, u32[]{:S(2)}) copy-start(f32[256,512]{1,0:T(8,128)} %param.14) | copy-start | bytes 1572868
  147.4 5.1 %collective-permute-start.7 = (bf16[256,512]{1,0:T(8,128)(2,1)S(1)}, bf16[256,512]{1,0:T(8,128)(2,1)S(1)}, u32[]{:S(2)}, u32[]{:S(2)}) collective-permute-start(bf16[256,512]{1,0:T(8,128)(2,1)S(1)} %fusion.3), channel_id=1, source_target_pairs={{0,16},{16,0},{1,17},{17,1},{2,18},{18,2},{3,19},{19,3},{4,20},{20... | collective-permute-start | bytes 786440 | tf_op jit(solution)/shard_map/ppermute | solution.py:138

commit v10 on v7

--- a/solution.py
+++ b/solution.py
@@ -136,8 +136,9 @@
     curv_own = grad_own * noise_own * (0.5 * inv_sigma)
     spread_gain = 0.5 * (1.0 - beta_two) ** 2 / (hessian + weight_decay)
     grad_other, momentum_own, curv_own, noise_other, spread_gain = lax.optimization_barrier(
-        (lax.ppermute(grad_sent, "c", SWAP), momentum_own, curv_own, noise_other, spread_gain)
+        (lax.ppermute(grad_sent.astype(bf16), "c", SWAP), momentum_own, curv_own, noise_other, spread_gain)
     )
+    grad_other = grad_other.astype(f32)
     new_momentum = momentum_own + (1.0 - beta_one) * 0.5 * grad_other
     curv_mean = curv_own + grad_other * noise_other
     spread = hessian - curv_mean

time: 154 us -> 154 us (level)
  no operation moved by 1% of the time
where the time goes in v10:
time: 154 us; the launch traced here: 153 us
  starting transfers between devices  82.3 us (53%)
  blocking collectives  31.1 us (20%)
  waiting for transfers between devices  22.7 us (15%)
  local copies, waits for them, and re-layouts  5.43 us (4%)
  other arithmetic  3.97 us (3%)
  Pallas kernels  3.48 us (2%)
  matrix products  2.8 us (2%)
    all_to_all x4, starting transfers between devices, trade(): return lax.all_to_all(parts, axis, 0, 0, tiled=True)  50.3 us
    all_to_all x1, blocking collectives, trade(): return lax.all_to_all(parts, axis, 0, 0, tiled=True)  31.1 us
    all_to_all x4, waiting for transfers between devices, trade(): return lax.all_to_all(parts, axis, 0, 0, tiled=True)  12 us
    ppermute x1, starting transfers between devices, shards(): lax.ppermute(lax.dynamic_index_in_dim(samples, 1 - core, 0, False), 'c',...  11.2 us
    ppermute x3, starting transfers between devices, shards(): block = hidden if k == 0 else lax.ppermute(hidden, 'x', turn(size_x, k))  8.41 us
    ppermute x3, starting transfers between devices, shards(): lax.ppermute(weights, 'x', turn(size_x, k))  8.41 us
    ppermute x3, waiting for transfers between devices, shards(): block = hidden if k == 0 else lax.ppermute(hidden, 'x', turn(size_x, k))  7.64 us
    ppermute x1, starting transfers between devices, shards(): lax.ppermute(grad_sent.astype(bf16), 'c', SWAP)  3.98 us
  transfers between devices with their start and end apart: 12, of which 8 were waited for; matrix products, arithmetic and copies ran while one was open for 5% of the time, Pallas kernels for 0%

profile of v10, /device:TPU:1, one launch (start us, length us, event | category | flops | bytes accessed | tf_op | source)
XLA Modules:
  0.0 152.8 jit_solution(14467821354108129996)
XLA Ops:
  0.6 3.5 %shard_map.103 = bf16[768,1024]{1,0:T(8,128)(2,1)} custom-call(bf16[768,512]{1,0:T(8,128)(2,1)} %tokens_ref.1, bf16[512,512]{1,0:T(8,128)(2,1)} %bitcast.75, bf16[512,512]{1,0:T(8,128)(2,1)} %bitcast.76), custom_call_target="tpu_custom_call" | custom-call | tf_op jit(solution)/shard_map/pallas_call | solution.py:46
  4.1 5.0 %all-to-all-start = ((bf16[4,192,1024]{2,1,0:T(8,128)(2,1)}), bf16[4,192,1024]{2,1,0:T(8,128)(2,1)S(1)}, u32[]{:S(2)}, u32[]{:S(2)}) async-start(bf16[4,192,1024]{2,1,0:T(8,128)(2,1)} %bitcast.66), calls=%async_computation | async-start | bytes 3145728 | tf_op jit(solution)/shard_map/all_to_all | solution.py:27
  9.5 11.2 %collective-permute-start = (bf16[256,512]{1,0:T(8,128)(2,1)S(1)}, bf16[256,512]{1,0:T(8,128)(2,1)S(1)}, u32[]{:S(2)}, u32[]{:S(2)}) collective-permute-start(bf16[256,512]{1,0:T(8,128)(2,1)S(1)} %get-tuple-element.37), channel_id=1, source_target_pairs={{0,16},{16,0},{1,17},{17,1},{2,18},{18,2},{3,19},{19,3},{4,20},{20... | collective-permute-start | bytes 786440 | tf_op jit(solution)/shard_map/ppermute | solution.py:82
  20.7 1.1 collective-permute-done
  21.8 0.8 pad_maximum_fusion
  22.7 1.1 reduce_sum.30
  23.8 20.4 %all-to-all-start.1 = ((bf16[4,48,1024]{2,1,0:T(8,128)(2,1)}), bf16[4,48,1024]{2,1,0:T(8,128)(2,1)S(1)}, u32[]{:S(2)}, u32[]{:S(2)}) async-start(bf16[4,48,1024]{2,1,0:T(8,128)(2,1)} %bitcast.5), calls=%async_computation.1 | async-start | bytes 786432 | tf_op jit(solution)/shard_map/all_to_all | solution.py:27
  44.3 2.2 %collective-permute-start.1 = (bf16[512,512]{1,0:T(8,128)(2,1)}, bf16[512,512]{1,0:T(8,128)(2,1)}, u32[]{:S(2)}, u32[]{:S(2)}) collective-permute-start(bf16[512,512]{1,0:T(8,128)(2,1)} %pad_maximum_fusion), channel_id=1, source_target_pairs={{0,1},{1,2},{2,3},{3,0},{4,5},{5,6},{6,7},{7,4},{8,9},{9,10},{10,1... | collective-permute-start | bytes 1572872 | tf_op jit(solution)/shard_map/ppermute | solution.py:85
  46.4 3.7 %collective-permute-start.2 = (bf16[512,512]{1,0:T(8,128)(2,1)}, bf16[512,512]{1,0:T(8,128)(2,1)}, u32[]{:S(2)}, u32[]{:S(2)}) collective-permute-start(bf16[512,512]{1,0:T(8,128)(2,1)} %pad_maximum_fusion), channel_id=1, source_target_pairs={{0,2},{1,3},{2,0},{3,1},{4,6},{5,7},{6,4},{7,5},{8,10},{9,11},{10,... | collective-permute-start | bytes 1572872 | tf_op jit(solution)/shard_map/ppermute | solution.py:85
  50.2 2.5 %collective-permute-start.3 = (bf16[512,512]{1,0:T(8,128)(2,1)}, bf16[512,512]{1,0:T(8,128)(2,1)}, u32[]{:S(2)}, u32[]{:S(2)}) collective-permute-start(bf16[512,512]{1,0:T(8,128)(2,1)} %pad_maximum_fusion), channel_id=1, source_target_pairs={{0,3},{1,0},{2,1},{3,2},{4,7},{5,4},{6,5},{7,6},{8,11},{9,8},{10,9... | collective-permute-start | bytes 1572872 | tf_op jit(solution)/shard_map/ppermute | solution.py:85
  52.7 2.9 %all-to-all-done.1 = bf16[4,48,1024]{2,1,0:T(8,128)(2,1)S(1)} async-done(((bf16[4,48,1024]{2,1,0:T(8,128)(2,1)}), bf16[4,48,1024]{2,1,0:T(8,128)(2,1)S(1)}, u32[]{:S(2)}, u32[]{:S(2)}) %all-to-all-start.1) | async-done | bytes 393248 | tf_op jit(solution)/shard_map/all_to_all | solution.py:27
  55.7 0.7 broadcast_in_dim.14
  56.4 12.9 %all-to-all-start.2 = ((bf16[8,48,256]{2,1,0:T(8,128)(2,1)}), bf16[8,48,256]{2,1,0:T(8,128)(2,1)S(1)}, u32[]{:S(2)}, u32[]{:S(2)}) async-start(bf16[8,48,256]{2,1,0:T(8,128)(2,1)} %bitcast.8), calls=%async_computation.2 | async-start | bytes 393216 | tf_op jit(solution)/shard_map/all_to_all | solution.py:27
  69.3 1.1 constant_dynamic-update-slice_fusion.3
  70.5 1.1 constant_dynamic-update-slice_fusion.2
  71.6 1.1 constant_dynamic-update-slice_fusion.1
  72.7 1.5 %collective-permute-done.3 = bf16[512,512]{1,0:T(8,128)(2,1)} collective-permute-done((bf16[512,512]{1,0:T(8,128)(2,1)}, bf16[512,512]{1,0:T(8,128)(2,1)}, u32[]{:S(2)}, u32[]{:S(2)}) %collective-permute-start.3) | collective-permute-done | bytes 524320 | tf_op jit(solution)/shard_map/ppermute | solution.py:85
  74.2 1.1 constant_dynamic-update-slice_fusion
  75.3 4.5 %all-to-all-done.2 = bf16[8,48,256]{2,1,0:T(8,128)(2,1)S(1)} async-done(((bf16[8,48,256]{2,1,0:T(8,128)(2,1)}), bf16[8,48,256]{2,1,0:T(8,128)(2,1)S(1)}, u32[]{:S(2)}, u32[]{:S(2)}) %all-to-all-start.2) | async-done | bytes 196640 | tf_op jit(solution)/shard_map/all_to_all | solution.py:27
  80.3 1.3 fusion.1
  81.5 11.9 %all-to-all-start.3 = ((bf16[24,8,2048]{2,1,0:T(8,128)(2,1)}), bf16[24,8,2048]{2,1,0:T(8,128)(2,1)S(1)}, u32[]{:S(2)}, u32[]{:S(2)}) async-start(bf16[24,8,2048]{2,1,0:T(8,128)(2,1)} %fusion.1), calls=%async_computation.3 | async-start | bytes 1572864 | tf_op jit(solution)/shard_map/all_to_all | solution.py:27
  93.5 2.2 %collective-permute-start.4 = (bf16[2,192,256]{2,1,0:T(8,128)(2,1)S(1)}, bf16[2,192,256]{2,1,0:T(8,128)(2,1)S(1)}, u32[]{:S(2)}, u32[]{:S(2)}) collective-permute-start(bf16[2,192,256]{2,1,0:T(8,128)(2,1)S(1)} %bitcast.71), channel_id=1, source_target_pairs={{0,1},{1,2},{2,3},{3,0},{4,5},{5,6},{6,7},{7,4},{8,9},{9,10},{10,1... | collective-permute-start | bytes 589832 | tf_op jit(solution)/shard_map/ppermute | solution.py:110
  95.7 3.7 %collective-permute-start.5 = (bf16[2,192,256]{2,1,0:T(8,128)(2,1)S(1)}, bf16[2,192,256]{2,1,0:T(8,128)(2,1)S(1)}, u32[]{:S(2)}, u32[]{:S(2)}) collective-permute-start(bf16[2,192,256]{2,1,0:T(8,128)(2,1)S(1)} %bitcast.72), channel_id=1, source_target_pairs={{0,2},{1,3},{2,0},{3,1},{4,6},{5,7},{6,4},{7,5},{8,10},{9,11},{10,... | collective-permute-start | bytes 589832 | tf_op jit(solution)/shard_map/ppermute | solution.py:110
  99.4 2.5 %collective-permute-start.6 = (bf16[2,192,256]{2,1,0:T(8,128)(2,1)S(1)}, bf16[2,192,256]{2,1,0:T(8,128)(2,1)S(1)}, u32[]{:S(2)}, u32[]{:S(2)}) collective-permute-start(bf16[2,192,256]{2,1,0:T(8,128)(2,1)S(1)} %bitcast.73), channel_id=1, source_target_pairs={{0,3},{1,0},{2,1},{3,2},{4,7},{5,4},{6,5},{7,6},{8,11},{9,8},{10,9... | collective-permute-start | bytes 589832 | tf_op jit(solution)/shard_map/ppermute | solution.py:110
  102.1 5.4 %collective-permute-done.4 = bf16[2,192,256]{2,1,0:T(8,128)(2,1)S(1)} collective-permute-done((bf16[2,192,256]{2,1,0:T(8,128)(2,1)S(1)}, bf16[2,192,256]{2,1,0:T(8,128)(2,1)S(1)}, u32[]{:S(2)}, u32[]{:S(2)}) %collective-permute-start.4) | collective-permute-done | bytes 196640 | tf_op jit(solution)/shard_map/ppermute | solution.py:110
  107.5 2.2 %collective-permute-done.6 = bf16[2,192,256]{2,1,0:T(8,128)(2,1)S(1)} collective-permute-done((bf16[2,192,256]{2,1,0:T(8,128)(2,1)S(1)}, bf16[2,192,256]{2,1,0:T(8,128)(2,1)S(1)}, u32[]{:S(2)}, u32[]{:S(2)}) %collective-permute-start.6) | collective-permute-done | bytes 196640 | tf_op jit(solution)/shard_map/ppermute | solution.py:110
  109.8 4.6 %all-to-all-done.3 = bf16[24,8,2048]{2,1,0:T(8,128)(2,1)S(1)} async-done(((bf16[24,8,2048]{2,1,0:T(8,128)(2,1)}), bf16[24,8,2048]{2,1,0:T(8,128)(2,1)S(1)}, u32[]{:S(2)}, u32[]{:S(2)}) %all-to-all-start.3) | async-done | bytes 786464 | tf_op jit(solution)/shard_map/all_to_all | solution.py:27
  114.7 31.1 %all_to_all.25 = bf16[96,8,512]{2,1,0:T(8,128)(2,1)S(1)} all-to-all(bf16[96,8,512]{2,1,0:T(8,128)(2,1)S(1)} %bitcast.67), channel_id=1, replica_groups=mesh['y'=8,'zl'=3,'c'=2,'zh'=4,'x'=4] {'x','y','zl'}, dimensions={0} | all-to-all | bytes 1572864 | tf_op jit(solution)/shard_map/all_to_all | solution.py:27
  145.8 0.5 fusion.4
  146.3 4.0 %collective-permute-start.7 = (bf16[256,512]{1,0:T(8,128)(2,1)S(1)}, bf16[256,512]{1,0:T(8,128)(2,1)S(1)}, u32[]{:S(2)}, u32[]{:S(2)}) collective-permute-start(bf16[256,512]{1,0:T(8,128)(2,1)S(1)} %fusion.4), channel_id=1, source_target_pairs={{0,16},{16,0},{1,17},{17,1},{2,18},{18,2},{3,19},{19,3},{4,20},{20... | collective-permute-start | bytes 786440 | tf_op jit(solution)/shard_map/ppermute | solution.py:139
  150.3 0.7 convert_multiply_fusion.2
  151.4 1.4 divide_subtract_fusion
  (37 shorter events, 1.7 us)
Async XLA Ops:
  4.1 5.0 %copy-start = (f32[256,512]{1,0:T(8,128)S(1)}, f32[256,512]{1,0:T(8,128)}, u32[]{:S(2)}) copy-start(f32[256,512]{1,0:T(8,128)} %param.13) | copy-start | bytes 1572868
  4.1 5.2 %copy-start.1 = (f32[256,512]{1,0:T(8,128)S(1)}, f32[256,512]{1,0:T(8,128)}, u32[]{:S(2)}) copy-start(f32[256,512]{1,0:T(8,128)} %param.12) | copy-start | bytes 1572868
  4.1 5.2 %copy-start.2 = (bf16[2,256,512]{2,1,0:T(8,128)(2,1)S(1)}, bf16[2,256,512]{2,1,0:T(8,128)(2,1)}, u32[]{:S(2)}) copy-start(bf16[2,256,512]{2,1,0:T(8,128)(2,1)} %param.15) | copy-start | bytes 1572868
  4.1 18.6 %all-to-all-start = ((bf16[4,192,1024]{2,1,0:T(8,128)(2,1)}), bf16[4,192,1024]{2,1,0:T(8,128)(2,1)S(1)}, u32[]{:S(2)}, u32[]{:S(2)}) async-start(bf16[4,192,1024]{2,1,0:T(8,128)(2,1)} %bitcast.66), calls=%async_computation | async-start | bytes 3145728 | tf_op jit(solution)/shard_map/all_to_all | solution.py:27
  9.5 12.3 %collective-permute-start = (bf16[256,512]{1,0:T(8,128)(2,1)S(1)}, bf16[256,512]{1,0:T(8,128)(2,1)S(1)}, u32[]{:S(2)}, u32[]{:S(2)}) collective-permute-start(bf16[256,512]{1,0:T(8,128)(2,1)S(1)} %get-tuple-element.37), channel_id=1, source_target_pairs={{0,16},{16,0},{1,17},{17,1},{2,18},{18,2},{3,19},{19,3},{4,20},{20... | collective-permute-start | bytes 786440 | tf_op jit(solution)/shard_map/ppermute | solution.py:82
  23.8 31.7 %all-to-all-start.1 = ((bf16[4,48,1024]{2,1,0:T(8,128)(2,1)}), bf16[4,48,1024]{2,1,0:T(8,128)(2,1)S(1)}, u32[]{:S(2)}, u32[]{:S(2)}) async-start(bf16[4,48,1024]{2,1,0:T(8,128)(2,1)} %bitcast.5), calls=%async_computation.1 | async-start | bytes 786432 | tf_op jit(solution)/shard_map/all_to_all | solution.py:27
  44.3 26.2 %collective-permute-start.1 = (bf16[512,512]{1,0:T(8,128)(2,1)}, bf16[512,512]{1,0:T(8,128)(2,1)}, u32[]{:S(2)}, u32[]{:S(2)}) collective-permute-start(bf16[512,512]{1,0:T(8,128)(2,1)} %pad_maximum_fusion), channel_id=1, source_target_pairs={{0,1},{1,2},{2,3},{3,0},{4,5},{5,6},{6,7},{7,4},{8,9},{9,10},{10,1... | collective-permute-start | bytes 1572872 | tf_op jit(solution)/shard_map/ppermute | solution.py:85
  46.4 25.1 %collective-permute-start.2 = (bf16[512,512]{1,0:T(8,128)(2,1)}, bf16[512,512]{1,0:T(8,128)(2,1)}, u32[]{:S(2)}, u32[]{:S(2)}) collective-permute-start(bf16[512,512]{1,0:T(8,128)(2,1)} %pad_maximum_fusion), channel_id=1, source_target_pairs={{0,2},{1,3},{2,0},{3,1},{4,6},{5,7},{6,4},{7,5},{8,10},{9,11},{10,... | collective-permute-start | bytes 1572872 | tf_op jit(solution)/shard_map/ppermute | solution.py:85
  50.2 24.1 %collective-permute-start.3 = (bf16[512,512]{1,0:T(8,128)(2,1)}, bf16[512,512]{1,0:T(8,128)(2,1)}, u32[]{:S(2)}, u32[]{:S(2)}) collective-permute-start(bf16[512,512]{1,0:T(8,128)(2,1)} %pad_maximum_fusion), channel_id=1, source_target_pairs={{0,3},{1,0},{2,1},{3,2},{4,7},{5,4},{6,5},{7,6},{8,11},{9,8},{10,9... | collective-permute-start | bytes 1572872 | tf_op jit(solution)/shard_map/ppermute | solution.py:85
  56.4 23.5 %all-to-all-start.2 = ((bf16[8,48,256]{2,1,0:T(8,128)(2,1)}), bf16[8,48,256]{2,1,0:T(8,128)(2,1)S(1)}, u32[]{:S(2)}, u32[]{:S(2)}) async-start(bf16[8,48,256]{2,1,0:T(8,128)(2,1)} %bitcast.8), calls=%async_computation.2 | async-start | bytes 393216 | tf_op jit(solution)/shard_map/all_to_all | solution.py:27
  81.5 32.9 %all-to-all-start.3 = ((bf16[24,8,2048]{2,1,0:T(8,128)(2,1)}), bf16[24,8,2048]{2,1,0:T(8,128)(2,1)S(1)}, u32[]{:S(2)}, u32[]{:S(2)}) async-start(bf16[24,8,2048]{2,1,0:T(8,128)(2,1)} %fusion.1), calls=%async_computation.3 | async-start | bytes 1572864 | tf_op jit(solution)/shard_map/all_to_all | solution.py:27
  93.5 13.9 %collective-permute-start.4 = (bf16[2,192,256]{2,1,0:T(8,128)(2,1)S(1)}, bf16[2,192,256]{2,1,0:T(8,128)(2,1)S(1)}, u32[]{:S(2)}, u32[]{:S(2)}) collective-permute-start(bf16[2,192,256]{2,1,0:T(8,128)(2,1)S(1)} %bitcast.71), channel_id=1, source_target_pairs={{0,1},{1,2},{2,3},{3,0},{4,5},{5,6},{6,7},{7,4},{8,9},{9,10},{10,1... | collective-permute-start | bytes 589832 | tf_op jit(solution)/shard_map/ppermute | solution.py:110
  95.7 11.8 %collective-permute-start.5 = (bf16[2,192,256]{2,1,0:T(8,128)(2,1)S(1)}, bf16[2,192,256]{2,1,0:T(8,128)(2,1)S(1)}, u32[]{:S(2)}, u32[]{:S(2)}) collective-permute-start(bf16[2,192,256]{2,1,0:T(8,128)(2,1)S(1)} %bitcast.72), channel_id=1, source_target_pairs={{0,2},{1,3},{2,0},{3,1},{4,6},{5,7},{6,4},{7,5},{8,10},{9,11},{10,... | collective-permute-start | bytes 589832 | tf_op jit(solution)/shard_map/ppermute | solution.py:110
  99.4 10.3 %collective-permute-start.6 = (bf16[2,192,256]{2,1,0:T(8,128)(2,1)S(1)}, bf16[2,192,256]{2,1,0:T(8,128)(2,1)S(1)}, u32[]{:S(2)}, u32[]{:S(2)}) collective-permute-start(bf16[2,192,256]{2,1,0:T(8,128)(2,1)S(1)} %bitcast.73), channel_id=1, source_target_pairs={{0,3},{1,0},{2,1},{3,2},{4,7},{5,4},{6,5},{7,6},{8,11},{9,8},{10,9... | collective-permute-start | bytes 589832 | tf_op jit(solution)/shard_map/ppermute | solution.py:110
  114.4 31.4 %copy-start.4 = (bf16[768,512]{1,0:T(8,128)(2,1)S(1)}, bf16[768,512]{1,0:T(8,128)(2,1)}, u32[]{:S(2)}) copy-start(bf16[768,512]{1,0:T(8,128)(2,1)} %param.9) | copy-start | bytes 2359300
  145.8 4.5 %copy-start.3 = (bf16[2,256,512]{2,1,0:T(8,128)(2,1)S(1)}, bf16[2,256,512]{2,1,0:T(8,128)(2,1)}, u32[]{:S(2)}) copy-start(bf16[2,256,512]{2,1,0:T(8,128)(2,1)} %param.15) | copy-start | bytes 1572868
  145.8 4.5 %copy-start.5 = (f32[256,512]{1,0:T(8,128)S(1)}, f32[256,512]{1,0:T(8,128)}, u32[]{:S(2)}) copy-start(f32[256,512]{1,0:T(8,128)} %param.14) | copy-start | bytes 1572868
  146.3 5.1 %collective-permute-start.7 = (bf16[256,512]{1,0:T(8,128)(2,1)S(1)}, bf16[256,512]{1,0:T(8,128)(2,1)S(1)}, u32[]{:S(2)}, u32[]{:S(2)}) collective-permute-start(bf16[256,512]{1,0:T(8,128)(2,1)S(1)} %fusion.4), channel_id=1, source_target_pairs={{0,16},{16,0},{1,17},{17,1},{2,18},{18,2},{3,19},{19,3},{4,20},{20... | collective-permute-start | bytes 786440 | tf_op jit(solution)/shard_map/ppermute | solution.py:139
